TPU v7x, 32 devices: a whole 2x2x4 slice. The times are simulated.
32 devices in a mesh: rows: 8 (over z, y), panels: 4 (over x, core).
Axes of the slice: x: 2, y: 2, z: 4, core: 2. Of those that a mesh axis runs over, the one named last changes fastest.
Arguments:
- panel_left: float32 [8, 32, 64, 2048], P('rows', 'panels'), may hold values from -6 to 6
- panel_right: float32 [8, 32, 64, 2048], P('rows', 'panels'), may hold values from -0.09375 to 0.09375
- pivot_left: float32 [32, 64, 2048], P('panels', None, 'rows'), may hold values from -6 to 6
- pivot_right: float32 [32, 64, 2048], P('panels', None, 'rows'), may hold values from -0.09375 to 0.09375
- pattern: int32 [8, 32], P('rows', 'panels'), may hold values 0 or 1
- tile_left: float32 [8, 64, 2048], P('rows', None, 'panels'), may hold values from -6 to 6
- tile_right: float32 [8, 64, 2048], P('rows', None, 'panels'), may hold values from -0.75 to 0.75
- sketch: float32 [64, 2048], replicated, may hold values from -0.125 to 0.125
Outputs:
- new_left: float32 [8, 64, 2048], P('rows', None, 'panels')
- new_right: float32 [8, 64, 2048], P('rows', None, 'panels')
All inputs are finite; a program needn't handle non-finite values. No bound on the sum of `pattern` on one device may be relied on, other than what follows from the above.
Results may differ from a plain program's by a relative error of at most 0.0003.
Values sent between devices are 32-bit elements; how exact they have to be, the bound alone decides.
No kernel may reach another device: no remote copies, remote signals or barrier semaphores. Data moves between devices by JAX's collectives and lax.ppermute only.
A program may use at most 128 MiB of HBM per device.

v0:
```python
import functools

import jax
import jax.numpy as jnp
from jax import lax
from jax.experimental import pallas as pl
from jax.experimental.pallas import tpu as pltpu
from jax.sharding import PartitionSpec as P

highest = lax.Precision.HIGHEST
f32 = jnp.float32
VMEM = pl.BlockSpec(memory_space=pltpu.VMEM)
SMEM = pl.BlockSpec(memory_space=pltpu.SMEM)
LIMIT = pltpu.CompilerParams(vmem_limit_bytes=40 * 1024 * 1024)


def dot(a, b, dims):
    return lax.dot_general(a, b, (dims, ((), ())), precision=highest, preferred_element_type=f32)


def nn(a, b):
    return dot(a, b, ((1,), (0,)))


def nt(a, b):
    return dot(a, b, ((1,), (1,)))


def tn(a, b):
    return dot(a, b, ((0,), (0,)))


def identity(n):
    return (lax.broadcasted_iota(jnp.int32, (n, n), 0) == lax.broadcasted_iota(jnp.int32, (n, n), 1)).astype(f32)


def inverse_factors(matrices):
    n = matrices[0].shape[0]
    step = 8 if len(matrices) < 3 else 4
    eye = identity(n)
    states = []
    for matrix in matrices:
        both = jnp.concatenate([matrix, eye], axis=1)
        states.append([both[8 * m : 8 * m + 8] for m in range(n // 8)])
    sub = lax.broadcasted_iota(jnp.int32, (8, 2 * n), 0)
    for k in range(0, n, step):
        m, s = k // 8, k % 8
        for state in states:
            row = [state[m][s + a : s + a + 1] for a in range(step)]
            pivot = [
                [jnp.broadcast_to(row[a][:, k + b : k + b + 1], (1, 2 * n)) if b >= a else None for b in range(step)]
                for a in range(step)
            ]
            rest = [t for t in range(m, n // 8) if not (t == m and s + step == 8)]
            column = [{t: jnp.broadcast_to(state[t][:, k + b : k + b + 1], (8, 2 * n)) for t in rest} for b in range(step)]
            if m in rest:
                for b in range(step):
                    column[b][m] = jnp.where(sub >= s + step, column[b][m], 0.0)
            done = state[m]
            scaled = []
            for a in range(step):
                inverse = 1.0 / pivot[a][a]
                for b in range(a + 1, step):
                    factor = pivot[a][b] * inverse
                    row[b] = row[b] - factor * row[a]
                    for c in range(b, step):
                        pivot[b][c] = pivot[b][c] - factor * pivot[a][c]
                    for t in rest:
                        column[b][t] = column[b][t] - column[a][t] * factor
                scaled.append(row[a] * inverse)
                done = jnp.where(sub == s + a, row[a] * lax.rsqrt(pivot[a][a]), done)
            state[m] = done
            for t in rest:
                total = state[t]
                for a in range(step):
                    total = total - column[a][t] * scaled[a]
                state[t] = total
    return [jnp.concatenate([block[:, n:] for block in state], axis=0) for state in states]


def ridge_inverses(grams):
    n = grams[0].shape[0]
    eye = identity(n)
    ridges = [0.001 * jnp.sum(jnp.sum(g * eye, axis=1, keepdims=True), axis=0, keepdims=True) / n + 1e-06 for g in grams]
    factors = inverse_factors([g + e * eye for g, e in zip(grams, ridges)])
    return ridges, factors


def shrink(grams):
    eye = identity(grams[0].shape[0])
    ridges, factors = ridge_inverses(grams)
    inverses = [tn(c, c) for c in factors]
    return inverses, [eye - e * s for e, s in zip(ridges, inverses)]


def inner_kernel(count, *refs):
    panels, pieces, add, out = refs[1 : 1 + count], refs[1 + count : 1 + 2 * count], refs[1 + 2 * count : -1], refs[-1]
    total = add[0][0] if add else None
    for panel, piece in zip(panels, pieces):
        term = nt(piece[0], panel[0, 0])
        total = term if total is None else total + term
    out[0] = total


def inner_products(panel_right, pieces, sources, add=None):
    count = len(pieces)
    _, j, rank, _ = panel_right.shape
    width = pieces[0].shape[2]
    square = pl.BlockSpec((1, rank, rank), lambda i, s: (i, 0, 0))
    in_specs = [pl.BlockSpec((1, 1, rank, width), functools.partial(lambda i, s, k: (0, i, 0, s[k]), k=k)) for k in range(count)]
    in_specs += [pl.BlockSpec((1, rank, width), lambda i, s: (i, 0, 0))] * count
    in_specs += [square] if add is not None else []
    return pl.pallas_call(
        functools.partial(inner_kernel, count),
        grid_spec=pltpu.PrefetchScalarGridSpec(num_scalar_prefetch=1, grid=(j,), in_specs=in_specs, out_specs=square),
        out_shape=jax.ShapeDtypeStruct((j, rank, rank), f32),
        compiler_params=LIMIT,
    )(jnp.stack(sources).astype(jnp.int32), *([panel_right] * count), *pieces, *([] if add is None else [add]))


def tree_kernel(weights, sketched, inner, panel, basis, path, top, sent, inverse_out, own_out):
    count, rank, width = panel.shape
    nodes = count // 2
    for n in range(nodes):
        coefs = [nn(sketched[j], inner[j]) * weights[0, j].astype(f32) for j in (2 * n, 2 * n + 1)]
        basis[n] = nn(jnp.concatenate(coefs, axis=1), panel[2 * n : 2 * n + 2].reshape(2 * rank, width))
    basis_all = basis[...].reshape(nodes * rank, width)
    gram = nt(basis_all, basis_all)
    chains = [None] * nodes
    level = [(n, n + 1, None) for n in range(nodes)]

    def times(coefs, matrix):
        return matrix if coefs is None else nn(coefs, matrix)

    def times_t(matrix, coefs):
        return matrix if coefs is None else nt(matrix, coefs)

    while True:
        spans = [slice(a * rank, b * rank) for a, b, _ in level]
        crossed = [times(h, gram[s]) for (_, _, h), s in zip(level, spans)]
        inverses, shrunk = shrink([times_t(x[:, s], h) for x, s, (_, _, h) in zip(crossed, spans, level)])
        if len(level) == 1:
            break
        parents = []
        for m in range(0, len(level), 2):
            (a, _, ha), (_, b, hb) = level[m], level[m + 1]
            coefs = jnp.concatenate([times_t_first(shrunk[m], ha), times_t_first(shrunk[m + 1], hb)], axis=1)
            rows = nn(coefs, gram[a * rank : b * rank])
            for child in (m, m + 1):
                first, last, h = level[child]
                step = nn(times_t(rows[:, spans[child]], h), inverses[child])
                for n in range(first, last):
                    chains[n] = step if chains[n] is None else nn(step, chains[n])
            parents.append((a, b, coefs))
        level = parents
    coefs = level[0][2]
    for j in range(count):
        crossing = nt(basis[j // 2], panel[j])
        path[:, j * rank : (j + 1) * rank] = nt(nn(chains[j // 2], crossing), inner[j]) * weights[0, j].astype(f32)
    top[...] = nn(coefs, basis_all)
    sent[...] = nn(nn(shrunk[0], coefs), basis_all)
    inverse_out[...] = inverses[0]
    own_out[...] = nn(shrunk[0], times_t(crossed[0][:, spans[0]], coefs))


def times_t_first(matrix, coefs):
    return matrix if coefs is None else nn(matrix, coefs)


def local_tree(weights, sketched, inner, panel):
    count, rank, width = panel.shape
    wide = jax.ShapeDtypeStruct((rank, width), f32)
    square = jax.ShapeDtypeStruct((rank, rank), f32)
    return pl.pallas_call(
        tree_kernel,
        in_specs=[SMEM, VMEM, VMEM, VMEM],
        out_specs=[VMEM] * 6,
        out_shape=[
            jax.ShapeDtypeStruct((count // 2, rank, width), f32),
            jax.ShapeDtypeStruct((rank, count * rank), f32),
            wide,
            wide,
            square,
            square,
        ],
        compiler_params=LIMIT,
    )(weights, sketched, inner, panel)


def chip_kernel(partner, top, inverse, own, step):
    step[...] = nn(own[...] + nt(partner[...], top[...]), inverse[...])


def root_kernel(chunk, own, core, far, far_core, tile, sketched, new_left, coefs_out):
    rank, width = tile.shape
    near = own[...] + core[...]
    other = far[...] + far_core[...]
    stack = jnp.concatenate([tile[...], near, other], axis=0)
    gram = nt(stack, stack)
    parts = [slice(k * rank, (k + 1) * rank) for k in range(3)]
    inverses, shrunk = shrink([gram[s, s] for s in parts[1:]])
    both = jnp.concatenate(shrunk, axis=1)
    rows = nn(both, gram[rank:])
    inverse, last = shrink([nt(rows[:, rank:], both)])
    coefs = jnp.concatenate([sketched[...], -nn(last[0], both)], axis=1)
    final = nn(coefs, gram)
    _, factors = ridge_inverses([nt(final, coefs)])
    factor = factors[0]
    scale = float(width) ** 0.5
    columns = new_left.shape[1]
    first = pl.multiple_of(chunk[0] * columns, columns)
    here = [tile[:, pl.ds(first, columns)]]
    here += [own[:, pl.ds(first, columns)] + core[:, pl.ds(first, columns)]]
    here += [far[:, pl.ds(first, columns)] + far_core[:, pl.ds(first, columns)]]
    new_left[...] = nn(nn(factor, coefs) * scale, jnp.concatenate(here, axis=0))
    down = nn(nt(final[:, rank:], both), inverse[0])
    steps = [-nn(nn(down, rows[:, s]), i) for s, i in zip(parts[1:], inverses)]
    coefs_out[...] = nn(factor, jnp.concatenate([final[:, parts[0]]] + steps, axis=1)) / scale


def finish_kernel(coefs, tile, own, core, far, far_core, new_right):
    stack = jnp.concatenate([tile[...], own[...] + core[...], far[...] + far_core[...]], axis=0)
    new_right[...] = nn(coefs[...], stack)


def call(kernel, out_shape, *operands, scalars=0):
    return pl.pallas_call(
        kernel,
        in_specs=[SMEM] * scalars + [VMEM] * (len(operands) - scalars),
        out_specs=jax.tree.map(lambda _: VMEM, out_shape),
        out_shape=out_shape,
        compiler_params=LIMIT,
    )(*operands)


def swap(value, axis, mask, members=None):
    members = range(lax.axis_size(axis)) if members is None else members
    return lax.ppermute(value, axis, [(i, i ^ mask) for i in members])


def gather_line(block, index):
    rows = lax.axis_size("rows")
    middle = range(2, rows - 2)
    ends = [i for i in range(rows) if i not in middle]
    low = index < rows // 2
    top = rows - 1

    def move(value, pairs):
        return lax.ppermute(value, "rows", pairs)

    up = move(block, [(i, i - 2) for i in range(2, rows)])
    down = move(block, [(i, i + 2) for i in range(rows - 2)])
    side = swap(block, "rows", 1)
    near = jnp.where(low, up, down)
    far_side = swap(side, "rows", top - 1, ends)
    up_two = move(up, [(i, i - 2) for i in range(2, rows - 2)])
    down_two = move(down, [(i, i + 2) for i in range(2, rows - 2)])
    two = jnp.where(low, up_two, down_two)
    near_side = swap(near, "rows", 1)
    other_side = swap(jnp.where(low, down, up), "rows", 1, middle)
    three = move(two, [(2, 0), (3, 1), (top - 3, top - 1), (top - 2, top)])
    two_side = swap(two, "rows", 1)
    above = jnp.minimum(index + 2, top - 1 + index % 2)
    below = jnp.maximum(index - 2, index % 2)
    nearest = jnp.where(low, index + 2, index - 2)
    early = [(block, index), (side, index ^ 1), (up, above), (down, below), (near_side, nearest ^ 1)]
    late = [
        (other_side, jnp.where(low, below, above) ^ 1),
        (two, index ^ 4),
        (far_side, top - index),
        (three, index ^ (top - 1)),
        (two_side, index ^ 5),
    ]
    return early, late


def local(panel_left, panel_right, pivot_left, pivot_right, pattern, tile_left, tile_right, sketch):
    rows = lax.axis_size("rows")
    row = lax.axis_index("rows")
    place = lax.axis_index("panels")
    count, rank, local_columns = pivot_left.shape
    columns = tile_left.shape[2]
    width = panel_left.shape[3]
    wide = jax.ShapeDtypeStruct((rank, width), f32)
    square = jax.ShapeDtypeStruct((rank, rank), f32)
    chunk = jax.ShapeDtypeStruct((rank, columns), f32)
    tile_left, tile_right = tile_left[0], tile_right[0]

    sketch_here = lax.dynamic_slice_in_dim(sketch, row * local_columns, local_columns, 1)
    sketched = jnp.einsum("rb,jkb->jrk", sketch_here, pivot_left, precision=highest)
    if rows == 8:
        for mask in (1, 2, 4):
            sketched = sketched + swap(sketched, "rows", mask)
    else:
        sketched = lax.psum(sketched, "rows")
    sketch_tile = lax.dynamic_slice_in_dim(sketch, place * columns, columns, 1)
    tile_sketched = nt(sketch_tile, tile_right)
    for mask in (1, 2):
        tile_sketched = tile_sketched + swap(tile_sketched, "panels", mask)
    whole_tile = lax.all_gather(tile_left, "panels", axis=1, tiled=True)

    if rows == 8 and local_columns % 128 == 0:
        early, late = gather_line(pivot_right, row)
        inner = inner_products(panel_right, [v for v, _ in early], [s for _, s in early])
        inner = inner_products(panel_right, [v for v, _ in late], [s for _, s in late], inner)
    else:
        full = lax.all_gather(pivot_right, "rows", axis=2, tiled=True)
        inner = inner_products(panel_right, [full], [jnp.int32(0)])

    _, path, top, sent, inverse, own = local_tree(pattern, sketched, inner, panel_left[0])
    far = swap(sent, "panels", 2)
    core = swap(sent, "panels", 1)
    far_core = swap(far, "panels", 1)
    step = call(chip_kernel, square, core, top, inverse, own)

    full_left = lax.all_gather(pivot_left, "rows", axis=2, tiled=True)
    right = nn(path, full_left.reshape(count * rank, width))
    right = nn(step, right)
    rights = []
    for mask in range(4):
        part = lax.dynamic_slice_in_dim(right, (place ^ mask) * columns, columns, 1)
        rights.append(swap(part, "panels", mask) if mask else part)

    new_left, coefs = call(
        root_kernel,
        [chunk, jax.ShapeDtypeStruct((rank, 3 * rank), f32)],
        place.reshape(1).astype(jnp.int32),
        sent,
        core,
        far,
        far_core,
        whole_tile,
        tile_sketched,
        scalars=1,
    )
    new_right = call(finish_kernel, chunk, coefs, tile_right, *rights)
    return (new_left[None], new_right[None])


def solution(mesh):
    return jax.shard_map(
        local,
        mesh=mesh,
        in_specs=(
            P("rows", "panels", None, None),
            P("rows", "panels", None, None),
            P("panels", None, "rows"),
            P("panels", None, "rows"),
            P("rows", "panels"),
            P("rows", None, "panels"),
            P("rows", None, "panels"),
            P(),
        ),
        out_specs=(P("rows", None, "panels"), P("rows", None, "panels")),
        check_vma=False,
    )
```

profile of v0, /device:TPU:1, one launch (start us, length us, event | category | flops | bytes accessed | tf_op | source)
XLA Modules:
  0.0 217.6 jit_solution(7914059761794361962)
XLA Ops:
  7.2 0.0 copy-start
  7.2 0.0 copy-start.4
  7.2 0.0 all-gather.3.cloned.1.call-start
  7.2 0.7 all-gather.3.cloned.1.call-update
  7.9 1.3 collective-permute-start.4
  9.2 4.7 %collective-permute-start.3 = (f32[8,64,256]{2,1,0:T(8,128)}, f32[8,64,256]{2,1,0:T(8,128)S(1)}, u32[]{:S(2)}, u32[]{:S(2)}) collective-permute-start(f32[8,64,256]{2,1,0:T(8,128)} %refs_6_.1), channel_id=1, source_target_pairs={{0,8},{4,12},{8,16},{12,20},{16,24},{20,28},{1,9},{5,13},{9,17},{1... | collective-permute-start | bytes 1572872 | tf_op jit(solution)/shard_map/ppermute | solution.py:249
  13.9 1.9 convolution_bitcast_fusion
  15.9 1.5 collective-permute-start
  17.3 0.1 collective-permute-start.8
  17.4 6.6 %collective-permute-done.4.refs_8_ = f32[8,64,256]{2,1,0:T(8,128)S(1)} collective-permute-done((f32[8,64,256]{2,1,0:T(8,128)}, f32[8,64,256]{2,1,0:T(8,128)S(1)}, u32[]{:S(2)}, u32[]{:S(2)}) %collective-permute-start.4) | collective-permute-done | bytes 524320 | tf_op jit(solution)/shard_map/ppermute | solution.py:249
  24.0 1.3 collective-permute-start.6
  25.3 2.7 %collective-permute-done.3.refs_9_ = f32[8,64,256]{2,1,0:T(8,128)S(1)} collective-permute-done((f32[8,64,256]{2,1,0:T(8,128)}, f32[8,64,256]{2,1,0:T(8,128)S(1)}, u32[]{:S(2)}, u32[]{:S(2)}) %collective-permute-start.3) | collective-permute-done | bytes 524320 | tf_op jit(solution)/shard_map/ppermute | solution.py:249
  28.0 1.4 collective-permute-start.7
  29.4 0.0 collective-permute-done
  29.5 7.1 %collective-permute-start.1 = (f32[8,64,64]{2,1,0:T(8,128)S(1)}, f32[8,64,64]{2,1,0:T(8,128)S(1)}, u32[]{:S(2)}, u32[]{:S(2)}) collective-permute-start(f32[8,64,64]{2,1,0:T(8,128)S(1)} %add.45), channel_id=1, source_target_pairs={{0,8},{4,12},{8,0},{12,4},{16,24},{20,28},{24,16},{28,20},{1,9},{5... | collective-permute-start | bytes 393224 | tf_op jit(solution)/shard_map/ppermute | solution.py:238
  36.5 14.8 %collective-permute-done.1 = f32[8,64,64]{2,1,0:T(8,128)S(1)} collective-permute-done((f32[8,64,64]{2,1,0:T(8,128)S(1)}, f32[8,64,64]{2,1,0:T(8,128)S(1)}, u32[]{:S(2)}, u32[]{:S(2)}) %collective-permute-start.1) | collective-permute-done | bytes 131104 | tf_op jit(solution)/shard_map/ppermute | solution.py:238
  51.4 13.4 %collective-permute-start.2 = (f32[8,64,64]{2,1,0:T(8,128)S(1)}, f32[8,64,64]{2,1,0:T(8,128)}, u32[]{:S(2)}, u32[]{:S(2)}) collective-permute-start(f32[8,64,64]{2,1,0:T(8,128)S(1)} %add.46), channel_id=1, source_target_pairs={{0,16},{4,20},{8,24},{12,28},{16,0},{20,4},{24,8},{28,12},{1,17},{... | collective-permute-start | bytes 393224 | tf_op jit(solution)/shard_map/ppermute | solution.py:238
  64.8 1.1 broadcast_select_fusion
  65.9 1.5 collective-permute-start.5
  67.4 0.0 collective-permute-done.8.refs_7_
  67.4 0.4 collective-permute-start.12
  67.8 4.5 %collective-permute-start.9 = (f32[8,64,256]{2,1,0:T(8,128)S(1)}, f32[8,64,256]{2,1,0:T(8,128)}, u32[]{:S(2)}, u32[]{:S(2)}) collective-permute-start(f32[8,64,256]{2,1,0:T(8,128)S(1)} %collective-permute-done.8.refs_7_), channel_id=1, source_target_pairs={{0,24},{4,28},{24,0},{28,4},{1,25},{5,29},{25,1},{29,5},{2,26},{6,... | collective-permute-start | bytes 1572872 | tf_op jit(solution)/shard_map/ppermute | solution.py:238
  72.4 1.1 broadcast_select_fusion.1.refs_7_
  73.5 1.3 collective-permute-start.10
  74.8 29.8 %collective-permute-done.2 = f32[8,64,64]{2,1,0:T(8,128)} collective-permute-done((f32[8,64,64]{2,1,0:T(8,128)S(1)}, f32[8,64,64]{2,1,0:T(8,128)}, u32[]{:S(2)}, u32[]{:S(2)}) %collective-permute-start.2) | collective-permute-done | bytes 131104 | tf_op jit(solution)/shard_map/ppermute | solution.py:238
  104.6 0.9 collective-permute-start.11
  105.5 0.1 stack.41.refs_0_
  105.6 0.1 stack.47.refs_0_
  105.7 1.0 add.47.sketched
  106.7 0.0 collective-permute-done.12.refs_10_
  106.7 0.0 copy-start.1
  106.7 2.2 %copy-done.1 = f32[1,8,64,2048]{3,2,1,0:T(8,128)S(1)} copy-done((f32[1,8,64,2048]{3,2,1,0:T(8,128)S(1)}, f32[1,8,64,2048]{3,2,1,0:T(8,128)}, u32[]{:S(2)}) %copy-start.1) | copy-done | bytes 4194328
  108.9 6.7 %shard_map.95.refs_11_ = f32[8,64,64]{2,1,0:T(8,128)S(1)} custom-call(s32[5]{0:T(128)S(1)} %stack.47.refs_0_, f32[1,8,64,2048]{3,2,1,0:T(8,128)S(1)} %copy-done.1, f32[1,8,64,2048]{3,2,1,0:T(8,128)S(1)} %copy-done.1, f32[1,8,64,2048]{3,2,1,0:T(8,128)S(1)} %copy-done.1, f32[1,8,64,2048]{3,2,1,0:T(8,128)S(1)} %copy-done.1, f32[1,8,64,2048]{3,2,1,0:T(8,128)S(1)} %copy-done.1, ...), custom_call_target="tpu_custom_call" | custom-call | tf_op jit(solution)/shard_map/pallas_call | solution.py:113
  115.6 0.0 copy-start.3
  115.6 0.0 copy-start.6
  115.6 0.0 collective-permute-done.9.refs_8_
  115.6 12.1 %collective-permute-done.10.refs_9_ = f32[8,64,256]{2,1,0:T(8,128)} collective-permute-done((f32[8,64,256]{2,1,0:T(8,128)S(1)}, f32[8,64,256]{2,1,0:T(8,128)}, u32[]{:S(2)}, u32[]{:S(2)}) %collective-permute-start.10) | collective-permute-done | bytes 524320 | tf_op jit(solution)/shard_map/ppermute | solution.py:249
  127.8 7.0 %shard_map.96.inner = f32[8,64,64]{2,1,0:T(8,128)S(1)} custom-call(s32[5]{0:T(128)S(1)} %stack.41.refs_0_, f32[1,8,64,2048]{3,2,1,0:T(8,128)S(1)} %copy-done.2, f32[1,8,64,2048]{3,2,1,0:T(8,128)S(1)} %copy-done.2, f32[1,8,64,2048]{3,2,1,0:T(8,128)S(1)} %copy-done.2, f32[1,8,64,2048]{3,2,1,0:T(8,128)S(1)} %copy-done.2, f32[1,8,64,2048]{3,2,1,0:T(8,128)S(1)} %copy-done.2, ...), custom_call_target="tpu_custom_call" | custom-call | tf_op jit(solution)/shard_map/pallas_call | solution.py:113
  134.8 0.0 copy-start.5
  134.9 28.5 %shard_map.97 = (f32[4,64,2048]{2,1,0:T(8,128)}, f32[64,512]{1,0:T(8,128)S(1)}, f32[64,2048]{1,0:T(8,128)S(1)}, f32[64,2048]{1,0:T(8,128)S(1)}, f32[64,64]{1,0:T(8,128)S(1)}, /*index=5*/f32[64,64]{1,0:T(8,128)S(1)}) custom-call(s32[1,8]{1,0:T(1,128)S(1)} %copy-done.6, f32[8,64,64]{2,1,0:T(8,128)S(1)} %add.47.sketched, f32[8,64,64]{2,1,0:T(8,128)S(1)} %shard_map.96.inner, ...), custom_call_target="tpu_custom_call" | custom-call | tf_op jit(solution)/shard_map/pallas_call | solution.py:174
  163.4 1.2 collective-permute-start.14
  164.5 1.0 collective-permute-start.13
  165.6 0.2 fusion
  165.8 0.1 collective-permute-start.16
  165.9 1.2 collective-permute-done.16
  167.1 0.3 collective-permute-start.17
  167.5 8.7 %collective-permute-done.14.far = f32[64,2048]{1,0:T(8,128)S(1)} collective-permute-done((f32[64,2048]{1,0:T(8,128)S(1)}, f32[64,2048]{1,0:T(8,128)S(1)}, u32[]{:S(2)}, u32[]{:S(2)}) %collective-permute-start.14) | collective-permute-done | bytes 524320 | tf_op jit(solution)/shard_map/ppermute | solution.py:238
  176.2 2.0 collective-permute-start.15
  178.1 0.0 collective-permute-done.13.core.partner
  178.1 0.7 shard_map.99
  178.9 0.0 all-gather.3.cloned.1.call-done
  178.9 5.0 %fusion.7 = f32[64,2048]{1,0:T(8,128)S(1)} fusion(f32[64,512]{1,0:T(8,128)S(1)} %get-tuple-element.15, f32[512,2048]{1,0:T(8,128)} %bitcast.32), kind=kOutput, calls=%fused_computation.15 | convolution fusion | flops 805306368 | bytes 4849664 | tf_op jit(solution)/shard_map/dot_general | solution.py:18
  184.0 0.6 fusion.8
  184.6 0.1 collective-permute-start.18
  184.7 1.2 collective-permute-start.19
  185.8 1.0 collective-permute-start.20
  186.8 10.2 %all-gather = f32[1,64,2048]{2,1,0:T(8,128)S(1)} all-gather(f32[1,64,512]{2,1,0:T(8,128)} %param.13), channel_id=2, replica_groups=mesh['rows'=8,'panels'=4] {'panels'}, dimensions={2}, use_global_device_ids=true | all-gather | bytes 655360 | tf_op jit(solution)/shard_map/all_gather | solution.py:300
  197.0 0.0 collective-permute-done.17
  197.0 0.8 add.53.sketched
  197.7 0.0 collective-permute-done.15.far_core
  197.7 11.5 %shard_map.98 = (f32[64,512]{1,0:T(8,128)}, f32[64,192]{1,0:T(8,128)S(1)}) custom-call(s32[1]{0:T(128)} %bitcast.chunk, f32[64,2048]{1,0:T(8,128)S(1)} %get-tuple-element.9.own, f32[64,2048]{1,0:T(8,128)S(1)} %collective-permute-done.13.core.partner, f32[64,2048]{1,0:T(8,128)S(1)} %collective-permute-done.14.far, ...), custom_call_target="tpu_custom_call" | custom-call | tf_op jit(solution)/shard_map/pallas_call | solution.py:227
  209.2 0.0 collective-permute-done.18.core
  209.3 0.0 collective-permute-done.19.far
  209.3 1.0 shard_map.100
  (16 shorter events, 0.2 us)
Async XLA Ops:
  7.2 6.8 %copy-start = (f32[64,2048]{1,0:T(8,128)S(1)}, f32[64,2048]{1,0:T(8,128)}, u32[]{:S(2)}) copy-start(f32[64,2048]{1,0:T(8,128)} %param.15) | copy-start | bytes 1572868
  7.2 99.5 %copy-start.4 = (f32[8,64,256]{2,1,0:T(8,128)S(1)}, f32[8,64,256]{2,1,0:T(8,128)}, u32[]{:S(2)}) copy-start(f32[8,64,256]{2,1,0:T(8,128)} %refs_6_.1) | copy-start | bytes 1572868
  7.2 171.7 %all-gather.3.cloned.1.call-start = ((), (), s32[]{:S(2)}) async-start(), calls=%async_computation | async-start | bytes 4718592 | tf_op jit(solution)/shard_map/all_gather | solution.py:316
  7.9 16.1 %collective-permute-start.4 = (f32[8,64,256]{2,1,0:T(8,128)}, f32[8,64,256]{2,1,0:T(8,128)S(1)}, u32[]{:S(2)}, u32[]{:S(2)}) collective-permute-start(f32[8,64,256]{2,1,0:T(8,128)} %refs_6_.1), channel_id=1, source_target_pairs={{8,0},{12,4},{16,8},{20,12},{24,16},{28,20},{9,1},{13,5},{17,9},{2... | collective-permute-start | bytes 1572872 | tf_op jit(solution)/shard_map/ppermute | solution.py:249
  9.2 18.8 %collective-permute-start.3 = (f32[8,64,256]{2,1,0:T(8,128)}, f32[8,64,256]{2,1,0:T(8,128)S(1)}, u32[]{:S(2)}, u32[]{:S(2)}) collective-permute-start(f32[8,64,256]{2,1,0:T(8,128)} %refs_6_.1), channel_id=1, source_target_pairs={{0,8},{4,12},{8,16},{12,20},{16,24},{20,28},{1,9},{5,13},{9,17},{1... | collective-permute-start | bytes 1572872 | tf_op jit(solution)/shard_map/ppermute | solution.py:249
  15.9 13.6 %collective-permute-start = (f32[8,64,64]{2,1,0:T(8,128)S(1)}, f32[8,64,64]{2,1,0:T(8,128)S(1)}, u32[]{:S(2)}, u32[]{:S(2)}) collective-permute-start(f32[8,64,64]{2,1,0:T(8,128)S(1)} %convolution_bitcast_fusion), channel_id=1, source_target_pairs={{0,4},{4,0},{8,12},{12,8},{16,20},{20,16},{24,28},{28,24},{1,5},{5... | collective-permute-start | bytes 393224 | tf_op jit(solution)/shard_map/ppermute | solution.py:238
  17.3 50.0 %collective-permute-start.8 = (f32[8,64,256]{2,1,0:T(8,128)}, f32[8,64,256]{2,1,0:T(8,128)S(1)}, u32[]{:S(2)}, u32[]{:S(2)}) collective-permute-start(f32[8,64,256]{2,1,0:T(8,128)} %refs_6_.1), channel_id=1, source_target_pairs={{0,4},{4,0},{8,12},{12,8},{16,20},{20,16},{24,28},{28,24},{1,5},{5... | collective-permute-start | bytes 1572872 | tf_op jit(solution)/shard_map/ppermute | solution.py:238
  24.0 43.8 %collective-permute-start.6 = (f32[8,64,256]{2,1,0:T(8,128)S(1)}, f32[8,64,256]{2,1,0:T(8,128)}, u32[]{:S(2)}, u32[]{:S(2)}) collective-permute-start(f32[8,64,256]{2,1,0:T(8,128)S(1)} %collective-permute-done.4.refs_8_), channel_id=1, source_target_pairs={{8,0},{12,4},{16,8},{20,12},{9,1},{13,5},{17,9},{21,13},{10,2},{14... | collective-permute-start | bytes 1572872 | tf_op jit(solution)/shard_map/ppermute | solution.py:249
  28.0 44.4 %collective-permute-start.7 = (f32[8,64,256]{2,1,0:T(8,128)S(1)}, f32[8,64,256]{2,1,0:T(8,128)}, u32[]{:S(2)}, u32[]{:S(2)}) collective-permute-start(f32[8,64,256]{2,1,0:T(8,128)S(1)} %collective-permute-done.3.refs_9_), channel_id=1, source_target_pairs={{8,16},{12,20},{16,24},{20,28},{9,17},{13,21},{17,25},{21,29},{10,... | collective-permute-start | bytes 1572872 | tf_op jit(solution)/shard_map/ppermute | solution.py:249
  29.5 21.9 %collective-permute-start.1 = (f32[8,64,64]{2,1,0:T(8,128)S(1)}, f32[8,64,64]{2,1,0:T(8,128)S(1)}, u32[]{:S(2)}, u32[]{:S(2)}) collective-permute-start(f32[8,64,64]{2,1,0:T(8,128)S(1)} %add.45), channel_id=1, source_target_pairs={{0,8},{4,12},{8,0},{12,4},{16,24},{20,28},{24,16},{28,20},{1,9},{5... | collective-permute-start | bytes 393224 | tf_op jit(solution)/shard_map/ppermute | solution.py:238
  51.4 53.2 %collective-permute-start.2 = (f32[8,64,64]{2,1,0:T(8,128)S(1)}, f32[8,64,64]{2,1,0:T(8,128)}, u32[]{:S(2)}, u32[]{:S(2)}) collective-permute-start(f32[8,64,64]{2,1,0:T(8,128)S(1)} %add.46), channel_id=1, source_target_pairs={{0,16},{4,20},{8,24},{12,28},{16,0},{20,4},{24,8},{28,12},{1,17},{... | collective-permute-start | bytes 393224 | tf_op jit(solution)/shard_map/ppermute | solution.py:238
  65.9 49.7 %collective-permute-start.5 = (f32[8,64,256]{2,1,0:T(8,128)}, f32[8,64,256]{2,1,0:T(8,128)}, u32[]{:S(2)}, u32[]{:S(2)}) collective-permute-start(f32[8,64,256]{2,1,0:T(8,128)} %get-tuple-element.17), channel_id=1, source_target_pairs={{8,12},{12,8},{16,20},{20,16},{9,13},{13,9},{17,21},{21,17},{10,14... | collective-permute-start | bytes 1572872 | tf_op jit(solution)/shard_map/ppermute | solution.py:238
  67.4 39.3 %collective-permute-start.12 = (f32[8,64,256]{2,1,0:T(8,128)}, f32[8,64,256]{2,1,0:T(8,128)}, u32[]{:S(2)}, u32[]{:S(2)}) collective-permute-start(f32[8,64,256]{2,1,0:T(8,128)} %get-tuple-element.16), channel_id=1, source_target_pairs={{0,4},{4,0},{8,12},{12,8},{16,20},{20,16},{24,28},{28,24},{1,5},{5... | collective-permute-start | bytes 1572872 | tf_op jit(solution)/shard_map/ppermute | solution.py:238
  67.8 47.8 %collective-permute-start.9 = (f32[8,64,256]{2,1,0:T(8,128)S(1)}, f32[8,64,256]{2,1,0:T(8,128)}, u32[]{:S(2)}, u32[]{:S(2)}) collective-permute-start(f32[8,64,256]{2,1,0:T(8,128)S(1)} %collective-permute-done.8.refs_7_), channel_id=1, source_target_pairs={{0,24},{4,28},{24,0},{28,4},{1,25},{5,29},{25,1},{29,5},{2,26},{6,... | collective-permute-start | bytes 1572872 | tf_op jit(solution)/shard_map/ppermute | solution.py:238
  73.5 54.3 %collective-permute-start.10 = (f32[8,64,256]{2,1,0:T(8,128)S(1)}, f32[8,64,256]{2,1,0:T(8,128)}, u32[]{:S(2)}, u32[]{:S(2)}) collective-permute-start(f32[8,64,256]{2,1,0:T(8,128)S(1)} %broadcast_select_fusion.1.refs_7_), channel_id=1, source_target_pairs={{8,0},{12,4},{16,24},{20,28},{9,1},{13,5},{17,25},{21,29},{10,2},{... | collective-permute-start | bytes 1572872 | tf_op jit(solution)/shard_map/ppermute | solution.py:249
  104.6 23.2 %collective-permute-start.11 = (f32[8,64,256]{2,1,0:T(8,128)S(1)}, f32[8,64,256]{2,1,0:T(8,128)}, u32[]{:S(2)}, u32[]{:S(2)}) collective-permute-start(f32[8,64,256]{2,1,0:T(8,128)S(1)} %broadcast_select_fusion.1.refs_7_), channel_id=1, source_target_pairs={{0,4},{4,0},{8,12},{12,8},{16,20},{20,16},{24,28},{28,24},{1,5},{5... | collective-permute-start | bytes 1572872 | tf_op jit(solution)/shard_map/ppermute | solution.py:238
  106.7 2.2 %copy-start.1 = (f32[1,8,64,2048]{3,2,1,0:T(8,128)S(1)}, f32[1,8,64,2048]{3,2,1,0:T(8,128)}, u32[]{:S(2)}) copy-start(f32[1,8,64,2048]{3,2,1,0:T(8,128)} %refs_5_.3) | copy-start | bytes 12582916
  108.9 18.9 %copy-start.2 = (f32[1,8,64,2048]{3,2,1,0:T(8,128)S(1)}, f32[1,8,64,2048]{3,2,1,0:T(8,128)}, u32[]{:S(2)}) copy-start(f32[1,8,64,2048]{3,2,1,0:T(8,128)} %refs_5_.3) | copy-start | bytes 12582916
  115.6 19.2 %copy-start.3 = (f32[1,8,64,2048]{3,2,1,0:T(8,128)S(1)}, f32[1,8,64,2048]{3,2,1,0:T(8,128)}, u32[]{:S(2)}) copy-start(f32[1,8,64,2048]{3,2,1,0:T(8,128)} %param.8) | copy-start | bytes 12582916
  115.6 19.2 %copy-start.6 = (s32[1,8]{1,0:T(1,128)S(1)}, s32[1,8]{1,0:T(1,128)}, u32[]{:S(2)}) copy-start(s32[1,8]{1,0:T(1,128)} %weights.1) | copy-start | bytes 100
  134.8 30.7 %copy-start.5 = (f32[1,64,512]{2,1,0:T(8,128)S(1)}, f32[1,64,512]{2,1,0:T(8,128)}, u32[]{:S(2)}) copy-start(f32[1,64,512]{2,1,0:T(8,128)} %param.14) | copy-start | bytes 393220
  163.4 12.8 %collective-permute-start.14 = (f32[64,2048]{1,0:T(8,128)S(1)}, f32[64,2048]{1,0:T(8,128)S(1)}, u32[]{:S(2)}, u32[]{:S(2)}) collective-permute-start(f32[64,2048]{1,0:T(8,128)S(1)} %get-tuple-element.9.own), channel_id=1, source_target_pairs={{0,2},{1,3},{2,0},{3,1},{4,6},{5,7},{6,4},{7,5},{8,10},{9,11},{10,... | collective-permute-start | bytes 1572872 | tf_op jit(solution)/shard_map/ppermute | solution.py:238
  164.5 13.6 %collective-permute-start.13 = (f32[64,2048]{1,0:T(8,128)S(1)}, f32[64,2048]{1,0:T(8,128)S(1)}, u32[]{:S(2)}, u32[]{:S(2)}) collective-permute-start(f32[64,2048]{1,0:T(8,128)S(1)} %get-tuple-element.9.own), channel_id=1, source_target_pairs={{0,1},{1,0},{2,3},{3,2},{4,5},{5,4},{6,7},{7,6},{8,9},{9,8},{10,11... | collective-permute-start | bytes 1572872 | tf_op jit(solution)/shard_map/ppermute | solution.py:238
  165.8 1.3 collective-permute-start.16
  167.1 29.8 %collective-permute-start.17 = (f32[64,64]{1,0:T(8,128)S(1)}, f32[64,64]{1,0:T(8,128)}, u32[]{:S(2)}, u32[]{:S(2)}) collective-permute-start(f32[64,64]{1,0:T(8,128)S(1)} %add.52), channel_id=1, source_target_pairs={{0,2},{1,3},{2,0},{3,1},{4,6},{5,7},{6,4},{7,5},{8,10},{9,11},{10,... | collective-permute-start | bytes 49160 | tf_op jit(solution)/shard_map/ppermute | solution.py:238
  176.2 21.6 %collective-permute-start.15 = (f32[64,2048]{1,0:T(8,128)S(1)}, f32[64,2048]{1,0:T(8,128)S(1)}, u32[]{:S(2)}, u32[]{:S(2)}) collective-permute-start(f32[64,2048]{1,0:T(8,128)S(1)} %collective-permute-done.14.far), channel_id=1, source_target_pairs={{0,1},{1,0},{2,3},{3,2},{4,5},{5,4},{6,7},{7,6},{8,9},{9,8},{10,11... | collective-permute-start | bytes 1572872 | tf_op jit(solution)/shard_map/ppermute | solution.py:238
  184.6 24.7 %collective-permute-start.18 = (f32[64,512]{1,0:T(8,128)S(1)}, f32[64,512]{1,0:T(8,128)S(1)}, u32[]{:S(2)}, u32[]{:S(2)}) collective-permute-start(f32[64,512]{1,0:T(8,128)S(1)} %get-tuple-element.20), channel_id=1, source_target_pairs={{0,1},{1,0},{2,3},{3,2},{4,5},{5,4},{6,7},{7,6},{8,9},{9,8},{10,11... | collective-permute-start | bytes 393224 | tf_op jit(solution)/shard_map/ppermute | solution.py:238
  184.7 24.6 %collective-permute-start.19 = (f32[64,512]{1,0:T(8,128)S(1)}, f32[64,512]{1,0:T(8,128)S(1)}, u32[]{:S(2)}, u32[]{:S(2)}) collective-permute-start(f32[64,512]{1,0:T(8,128)S(1)} %get-tuple-element.19), channel_id=1, source_target_pairs={{0,2},{1,3},{2,0},{3,1},{4,6},{5,7},{6,4},{7,5},{8,10},{9,11},{10,... | collective-permute-start | bytes 393224 | tf_op jit(solution)/shard_map/ppermute | solution.py:238
  185.8 23.4 %collective-permute-start.20 = (f32[64,512]{1,0:T(8,128)S(1)}, f32[64,512]{1,0:T(8,128)S(1)}, u32[]{:S(2)}, u32[]{:S(2)}) collective-permute-start(f32[64,512]{1,0:T(8,128)S(1)} %get-tuple-element.18), channel_id=1, source_target_pairs={{0,3},{1,2},{2,1},{3,0},{4,7},{5,6},{6,5},{7,4},{8,11},{9,10},{10,... | collective-permute-start | bytes 393224 | tf_op jit(solution)/shard_map/ppermute | solution.py:238
Sparse Core Ops, SparseCore 0:
  10.1 116.3 all-gather.2
where the time goes:
time: 222 us; the launch traced here: 218 us
  waiting for transfers between devices  76.6 us (35%)
  Pallas kernels  55.5 us (25%)
  starting transfers between devices  46.2 us (21%)
  between operations  14.8 us (7%)
  blocking collectives  10.2 us (5%)
  matrix products  7.8 us (4%)
  other arithmetic  4.07 us (2%)
  local copies, waits for them, and re-layouts  2.44 us (1%)
    ppermute x16, waiting for transfers between devices, swap(): return lax.ppermute(value, axis, [(i, i ^ mask) for i in members])  54.5 us
    ppermute x16, starting transfers between devices, swap(): return lax.ppermute(value, axis, [(i, i ^ mask) for i in members])  36.1 us
    pallas_call x1, Pallas kernels, local_tree(): pl.pallas_call(tree_kernel, in_specs=[SMEM, VMEM, VMEM, VMEM], out_specs=...  28.5 us
    ppermute x5, waiting for transfers between devices, move(): return lax.ppermute(value, 'rows', pairs)  21.4 us
    pallas_call x2, Pallas kernels, inner_products(): pl.pallas_call(functools.partial(inner_kernel, count), grid_spec=pltpu.Pr...  13.8 us
    pallas_call x3, Pallas kernels, call(): pl.pallas_call(kernel, in_specs=[SMEM] * scalars + [VMEM] * (len(operands...  13.3 us
    all_gather x1, blocking collectives, local(): whole_tile = lax.all_gather(tile_left, 'panels', axis=1, tiled=True)  10.2 us
    ppermute x5, starting transfers between devices, move(): return lax.ppermute(value, 'rows', pairs)  10 us
  transfers between devices with their start and end apart: 22, of which 7 were waited for; matrix products, arithmetic and copies ran while one was open for 6% of the time, Pallas kernels for 25%

commit v1 on v0

v1 whole, which is shorter than its diff:
```python
import functools

import jax
import jax.numpy as jnp
from jax import lax
from jax.experimental import pallas as pl
from jax.experimental.pallas import tpu as pltpu
from jax.sharding import PartitionSpec as P

highest = lax.Precision.HIGHEST
f32 = jnp.float32
VMEM = pl.BlockSpec(memory_space=pltpu.VMEM)
SMEM = pl.BlockSpec(memory_space=pltpu.SMEM)
LIMIT = pltpu.CompilerParams(vmem_limit_bytes=20 * 1024 * 1024)
ROOMY = pltpu.CompilerParams(vmem_limit_bytes=32 * 1024 * 1024)
SHORT = pl.CostEstimate(flops=10**8, bytes_accessed=10**6, transcendentals=0)


def dot(a, b, dims):
    return lax.dot_general(a, b, (dims, ((), ())), precision=highest, preferred_element_type=f32)


def nn(a, b):
    return dot(a, b, ((1,), (0,)))


def nt(a, b):
    return dot(a, b, ((1,), (1,)))


def tn(a, b):
    return dot(a, b, ((0,), (0,)))


def identity(n):
    return (lax.broadcasted_iota(jnp.int32, (n, n), 0) == lax.broadcasted_iota(jnp.int32, (n, n), 1)).astype(f32)


def inverse_factors(matrices):
    n = matrices[0].shape[0]
    step = 8 if len(matrices) < 3 else 4
    eye = identity(n)
    states = []
    for matrix in matrices:
        both = jnp.concatenate([matrix, eye], axis=1)
        states.append([both[8 * m : 8 * m + 8] for m in range(n // 8)])
    sub = lax.broadcasted_iota(jnp.int32, (8, 2 * n), 0)
    for k in range(0, n, step):
        m, s = k // 8, k % 8
        for state in states:
            row = [state[m][s + a : s + a + 1] for a in range(step)]
            pivot = [
                [jnp.broadcast_to(row[a][:, k + b : k + b + 1], (1, 2 * n)) if b >= a else None for b in range(step)]
                for a in range(step)
            ]
            rest = [t for t in range(m, n // 8) if not (t == m and s + step == 8)]
            column = [{t: jnp.broadcast_to(state[t][:, k + b : k + b + 1], (8, 2 * n)) for t in rest} for b in range(step)]
            if m in rest:
                for b in range(step):
                    column[b][m] = jnp.where(sub >= s + step, column[b][m], 0.0)
            done = state[m]
            scaled = []
            for a in range(step):
                inverse = 1.0 / pivot[a][a]
                for b in range(a + 1, step):
                    factor = pivot[a][b] * inverse
                    row[b] = row[b] - factor * row[a]
                    for c in range(b, step):
                        pivot[b][c] = pivot[b][c] - factor * pivot[a][c]
                    for t in rest:
                        column[b][t] = column[b][t] - column[a][t] * factor
                scaled.append(row[a] * inverse)
                done = jnp.where(sub == s + a, row[a] * lax.rsqrt(pivot[a][a]), done)
            state[m] = done
            for t in rest:
                total = state[t]
                for a in range(step):
                    total = total - column[a][t] * scaled[a]
                state[t] = total
    return [jnp.concatenate([block[:, n:] for block in state], axis=0) for state in states]


def ridge_inverses(grams):
    n = grams[0].shape[0]
    eye = identity(n)
    ridges = [0.001 * jnp.sum(jnp.sum(g * eye, axis=1, keepdims=True), axis=0, keepdims=True) / n + 1e-06 for g in grams]
    factors = inverse_factors([g + e * eye for g, e in zip(grams, ridges)])
    return ridges, factors


def shrink(grams):
    eye = identity(grams[0].shape[0])
    ridges, factors = ridge_inverses(grams)
    inverses = [tn(c, c) for c in factors]
    return inverses, [eye - e * s for e, s in zip(ridges, inverses)]


def split(value):
    parts = []
    for _ in range(3):
        part = value.astype(jnp.bfloat16)
        parts.append(part)
        value = value - part.astype(f32)
    return parts


def nt_parts(a, b):
    m, n = a.shape[0], b.shape[0]
    stacked = lax.dot_general(
        jnp.concatenate(split(a), axis=0),
        jnp.concatenate(split(b), axis=0),
        (((1,), (1,)), ((), ())),
        preferred_element_type=f32,
    )

    def block(i, k):
        return stacked[i * m : (i + 1) * m, k * n : (k + 1) * n]

    small = block(1, 1) + block(0, 2) + block(2, 0)
    return block(0, 0) + (block(0, 1) + block(1, 0) + small)


def inner_kernel(count, *refs):
    panels, pieces, add, out = refs[1 : 1 + count], refs[1 + count : 1 + 2 * count], refs[1 + 2 * count : -1], refs[-1]
    for j in range(out.shape[0]):
        left = jnp.concatenate([piece[j] for piece in pieces], axis=1)
        right = jnp.concatenate([panel[0, j] for panel in panels], axis=1)
        term = nt_parts(left, right)
        out[j] = term + add[0][j] if add else term


def inner_products(panel_right, pieces, sources, add=None):
    count = len(pieces)
    _, j, rank, _ = panel_right.shape
    width = pieces[0].shape[2]
    group = j // 2
    square = pl.BlockSpec((group, rank, rank), lambda i, s: (i, 0, 0))
    in_specs = [pl.BlockSpec((1, group, rank, width), functools.partial(lambda i, s, k: (0, i, 0, s[k]), k=k)) for k in range(count)]
    in_specs += [pl.BlockSpec((group, rank, width), lambda i, s: (i, 0, 0))] * count
    in_specs += [square] if add is not None else []
    return pl.pallas_call(
        functools.partial(inner_kernel, count),
        grid_spec=pltpu.PrefetchScalarGridSpec(num_scalar_prefetch=1, grid=(j // group,), in_specs=in_specs, out_specs=square),
        out_shape=held(j, rank, rank),
        compiler_params=ROOMY,
        cost_estimate=SHORT,
    )(jnp.stack(sources).astype(jnp.int32), *([panel_right] * count), *pieces, *([] if add is None else [add]))


def tree_kernel(weights, sketched, inner, products, path, whole):
    count, rank, _ = sketched.shape
    nodes = count // 2
    leaves = [
        jnp.concatenate([nn(sketched[j], inner[j]) * weights[0, j].astype(f32) for j in (2 * n, 2 * n + 1)], axis=1)
        for n in range(nodes)
    ]
    pair = [slice(2 * n * rank, 2 * (n + 1) * rank) for n in range(nodes)]
    crossing = [nn(leaf, products[s]) for leaf, s in zip(leaves, pair)]
    crossing_all = jnp.concatenate(crossing, axis=0)
    gram = jnp.concatenate([nt(crossing_all[:, s], leaf) for leaf, s in zip(leaves, pair)], axis=1)
    chains = [None] * nodes
    level = [(n, n + 1, None) for n in range(nodes)]

    def times(coefs, matrix):
        return matrix if coefs is None else nn(coefs, matrix)

    def times_t(matrix, coefs):
        return matrix if coefs is None else nt(matrix, coefs)

    def after(matrix, coefs):
        return matrix if coefs is None else nn(matrix, coefs)

    while len(level) > 1:
        spans = [slice(a * rank, b * rank) for a, b, _ in level]
        crossed = [times(h, gram[s]) for (_, _, h), s in zip(level, spans)]
        inverses, shrunk = shrink([times_t(x[:, s], h) for x, s, (_, _, h) in zip(crossed, spans, level)])
        parents = []
        for m in range(0, len(level), 2):
            (a, _, ha), (_, b, hb) = level[m], level[m + 1]
            coefs = jnp.concatenate([after(shrunk[m], ha), after(shrunk[m + 1], hb)], axis=1)
            rows = nn(coefs, gram[a * rank : b * rank])
            for child in (m, m + 1):
                first, last, h = level[child]
                step = nn(times_t(rows[:, spans[child]], h), inverses[child])
                for n in range(first, last):
                    chains[n] = step if chains[n] is None else nn(step, chains[n])
            parents.append((a, b, coefs))
        level = parents
    coefs = level[0][2]
    for n in range(nodes):
        both = nn(chains[n], crossing[n][:, pair[n]])
        for j in (0, 1):
            k = 2 * n + j
            path[:, k * rank : (k + 1) * rank] = nt(both[:, j * rank : (j + 1) * rank], inner[k]) * weights[0, k].astype(f32)
    for n, leaf in enumerate(leaves):
        whole[:, pair[n]] = nn(coefs[:, n * rank : (n + 1) * rank], leaf)
    whole[:, count * rank :] = nt(nn(coefs, gram), coefs)


def top_kernel(whole, panel, top, sent, squares, held, sem):
    copy = pltpu.make_async_copy(panel, held, sem)
    copy.start()
    rank = whole.shape[0]
    depth = panel.shape[0]
    gram = whole[:, depth:]
    inverses, shrunk = shrink([gram])
    squares[:, :rank] = inverses[0]
    squares[:, rank:] = nn(shrunk[0], gram)
    copy.wait()
    factor = nn(whole[:, :depth], held[...])
    top[...] = factor
    sent[...] = nn(shrunk[0], factor)


def chip_kernel(own, partner, top, squares, tile, step, near_out, gram_out):
    near = own[...] + partner[...]
    near_out[...] = near
    rank = top.shape[0]
    step[...] = nn(squares[:, rank:] + nt(partner[...], top[...]), squares[:, :rank])
    stack = jnp.concatenate([tile[...], near], axis=0)
    gram_out[...] = nt(stack, stack)


def root_kernel(chunk, near, far, far_core, tile, gram_in, sketched, new_left, coefs_out):
    rank, width = tile.shape
    other = far[...] + far_core[...]
    cross = nt(other, jnp.concatenate([tile[...], near[...], other], axis=0))
    above = jnp.concatenate([gram_in[...], cross[:, : 2 * rank].T], axis=1)
    gram = jnp.concatenate([above, cross], axis=0)
    parts = [slice(k * rank, (k + 1) * rank) for k in range(3)]
    inverses, shrunk = shrink([gram[s, s] for s in parts[1:]])
    both = jnp.concatenate(shrunk, axis=1)
    rows = nn(both, gram[rank:])
    inverse, last = shrink([nt(rows[:, rank:], both)])
    coefs = jnp.concatenate([sketched[...], -nn(last[0], both)], axis=1)
    final = nn(coefs, gram)
    down = nn(nt(final[:, rank:], both), inverse[0])
    steps = [-nn(nn(down, rows[:, s]), i) for s, i in zip(parts[1:], inverses)]
    _, factors = ridge_inverses([nt(final, coefs)])
    factor = factors[0]
    scale = float(width) ** 0.5
    columns = new_left.shape[1]
    here = pl.ds(pl.multiple_of(chunk[0] * columns, columns), columns)
    stack = jnp.concatenate([tile[:, here], near[:, here], far[:, here] + far_core[:, here]], axis=0)
    new_left[...] = nn(nn(factor, coefs) * scale, stack)
    coefs_out[...] = nn(factor, jnp.concatenate([final[:, parts[0]]] + steps, axis=1)) / scale


def copy_kernel(value, out):
    out[...] = value[...]


def right_kernel(*refs):
    paths, pieces, outs = refs[:4], refs[4:-4], refs[-4:]
    rank = paths[0].shape[0]
    stack = jnp.concatenate([path[...] for path in paths], axis=0)
    part = nn(stack, jnp.concatenate([piece[...] for piece in pieces], axis=1))
    for k, out in enumerate(outs):
        out[...] = part[k * rank : (k + 1) * rank]


def collect_kernel(spots, step, own, side, near, near_side, *refs):
    outs, held = refs[:4], refs[4]
    half = own.shape[1] // 2
    odd = spots[4] == 1
    k = 0
    for first, second in ((own, side), (near, near_side)):
        part = nn(step[...], jnp.concatenate([first[...], second[...]], axis=1))
        for i in range(2):
            a = part[:, i * half : (i + 1) * half]
            b = part[:, (2 + i) * half : (3 + i) * half]
            held[spots[k]] = jnp.concatenate([jnp.where(odd, b, a), jnp.where(odd, a, b)], axis=1)
            k += 1
    for k, out in enumerate(outs):
        out[...] = held[k]


def finish_kernel(coefs, tile, own, core, far, far_core, new_right):
    stack = jnp.concatenate([tile[...], own[...] + core[...], far[...] + far_core[...]], axis=0)
    new_right[...] = nn(coefs[...], stack)


def held(*shape):
    return pltpu.VMEM(shape, f32)


def call(kernel, out_shape, *operands, scalars=0, scratch=()):
    return pl.pallas_call(
        kernel,
        in_specs=[SMEM] * scalars + [VMEM] * (len(operands) - scalars),
        out_specs=jax.tree.map(lambda _: VMEM, out_shape, is_leaf=lambda v: not isinstance(v, list)),
        out_shape=out_shape,
        scratch_shapes=scratch,
        compiler_params=LIMIT,
        cost_estimate=SHORT,
    )(*operands)


def swap(value, axis, mask, members=None):
    members = range(lax.axis_size(axis)) if members is None else members
    return lax.ppermute(value, axis, [(i, i ^ mask) for i in members])


def chip_step(sent, top, squares, tile):
    rank, width = tile.shape
    core = swap(sent, "panels", 1)
    shapes = [held(rank, rank), held(rank, width), held(2 * rank, 2 * rank)]
    return core, *call(chip_kernel, shapes, sent, core, top, squares, tile)


def gather_panels(value):
    core = swap(value, "panels", 1)
    far = swap(jnp.stack([value, core]), "panels", 2)
    return [value, core, far[0], far[1]]


def gather_line(block, index, partial, tile, beside):
    ends, middle = (0, 1, 6, 7), (2, 3, 4, 5)
    is_end = (index < 2) | (index > 5)
    outward = [(2, 0), (3, 1), (4, 6), (5, 7)]

    near = swap(block, "rows", 2)
    center = swap(block, "rows", 6, middle)
    side = swap(block, "rows", 1)
    for mask in (1, 2):
        partial = partial + swap(partial, "rows", mask)
    near, center, side, partial, beside = lax.optimization_barrier((near, center, side, partial, beside))

    outer = lax.ppermute(center, "rows", outward)
    inner = swap(near, "rows", 6, middle)
    near_side = swap(near, "rows", 1)
    crossed = jnp.where(is_end, side, center)
    far_side = lax.ppermute(crossed, "rows", [(i, i ^ (6 if i in ends else 1)) for i in range(8)])
    outer, inner, near_side, far_side, partial, tile = lax.optimization_barrier(
        (outer, inner, near_side, far_side, partial, tile)
    )

    opposite = jnp.where(is_end, outer, inner)
    opposite, inner, partial = lax.optimization_barrier((opposite, inner, partial))
    far = lax.ppermute(inner, "rows", outward)
    opposite_side = swap(opposite, "rows", 1)
    partial = partial + swap(partial, "rows", 4)
    tiles = gather_panels(tile)
    early = [block, side, near, near_side, opposite, far_side, center]
    late = [opposite_side, far]
    return [(v, index ^ k) for v, k in zip(early, (0, 1, 2, 3, 4, 7, 6))], [
        (v, index ^ k) for v, k in zip(late, (5, 6))
    ], partial, tiles, beside


def local(panel_left, panel_right, pivot_left, pivot_right, pattern, tile_left, tile_right, sketch):
    rows = lax.axis_size("rows")
    row = lax.axis_index("rows")
    place = lax.axis_index("panels")
    count, rank, local_columns = pivot_left.shape
    columns = tile_left.shape[2]
    width = panel_left.shape[3]
    wide = held(rank, width)
    square = held(rank, rank)
    chunk = held(rank, columns)
    tile_left, tile_right = tile_left[0], tile_right[0]

    sketch_here = lax.dynamic_slice_in_dim(sketch, row * local_columns, local_columns, 1)
    sketched = jnp.einsum("rb,jkb->jrk", sketch_here, pivot_left, precision=highest)
    sketch_tile = lax.dynamic_slice_in_dim(sketch, place * columns, columns, 1)
    tile_sketched = nt(sketch_tile, tile_right)
    panel = panel_left.reshape(count * rank, width)
    products = nt(panel, panel)
    routed = rows == 8 and local_columns % 128 == 0
    tile = jnp.concatenate([tile_left, tile_sketched, jnp.zeros_like(tile_sketched)], axis=1)
    if routed:
        early, late, sketched, tiles, products = gather_line(pivot_right, row, sketched, tile, products)
    else:
        sketched = lax.psum(sketched, "rows")
        tiles = gather_panels(tile)
    tile_sketched = sum(tile[:, columns : columns + rank] for tile in tiles)
    whole_tile = jnp.zeros((rank, width), f32)
    for mask, tile in enumerate(tiles):
        whole_tile = lax.dynamic_update_slice_in_dim(whole_tile, tile[:, :columns], (place ^ mask) * columns, 1)

    if routed:
        inner = inner_products(panel_right, [v for v, _ in early], [s for _, s in early])
        inner, sketched, tile_sketched, whole_tile = lax.optimization_barrier((inner, sketched, tile_sketched, whole_tile))
        _, pivot_left = lax.optimization_barrier((late, pivot_left))
        pivot = call(copy_kernel, held(count * rank, local_columns), pivot_left.reshape(count * rank, local_columns))
        inner, pivot = lax.optimization_barrier((inner, pivot))
        opposite = swap(pivot, "rows", 4)
        inner = inner_products(panel_right, [v for v, _ in late], [s for _, s in late], inner)
    else:
        full = lax.all_gather(pivot_right, "rows", axis=2, tiled=True)
        inner = inner_products(panel_right, [full], [jnp.int32(0)])

    path, whole = call(
        tree_kernel,
        [held(rank, count * rank), held(rank, (count + 1) * rank)],
        pattern,
        sketched,
        inner,
        products,
        scalars=1,
    )
    top, sent, squares = pl.pallas_call(
        top_kernel,
        in_specs=[VMEM, pl.BlockSpec(memory_space=pl.ANY)],
        out_specs=[VMEM] * 3,
        out_shape=[wide, wide, held(rank, 2 * rank)],
        scratch_shapes=[pltpu.VMEM(panel.shape, f32), pltpu.SemaphoreType.DMA],
        compiler_params=LIMIT,
        cost_estimate=SHORT,
    )(whole, panel)
    if routed:
        pieces = [pivot, opposite]
        paths = [path] + [swap(path, "rows", mask) for mask in (1, 2, 3)]
        half = held(rank, 2 * local_columns)
        paths, pieces, sent = lax.optimization_barrier((paths, pieces, sent))
        far = swap(sent, "panels", 2)
        core, step, near, gram = chip_step(sent, top, squares, whole_tile)
        mine, *given = call(right_kernel, [half] * 4, *paths, *pieces)
        got = [mine] + [swap(v, "rows", mask) for mask, v in zip((1, 2, 3), given)]
        far, got = lax.optimization_barrier((far, got))
        depth = row // 2
        spots = jnp.stack([depth ^ place, depth ^ 2 ^ place, depth ^ 1 ^ place, depth ^ 3 ^ place, row % 2])
        parts = call(collect_kernel, [chunk] * 4, spots.astype(jnp.int32), step, *got, scalars=1, scratch=[pltpu.VMEM((4, rank, columns), f32)])
        rights = [swap(parts[mask], "panels", mask) if mask else parts[0] for mask in range(4)]
    else:
        core, step, near, gram = chip_step(sent, top, squares, whole_tile)
        far = swap(sent, "panels", 2)
        full_left = lax.all_gather(pivot_left, "rows", axis=2, tiled=True)
        right = nn(step, nn(path, full_left.reshape(count * rank, width)))
        rights = []
        for mask in range(4):
            part = lax.dynamic_slice_in_dim(right, (place ^ mask) * columns, columns, 1)
            rights.append(swap(part, "panels", mask) if mask else part)

    far_core = swap(far, "panels", 1)
    new_left, coefs = call(
        root_kernel,
        [jax.ShapeDtypeStruct((rank, columns), f32), held(rank, 3 * rank)],
        place.reshape(1).astype(jnp.int32),
        near,
        far,
        far_core,
        whole_tile,
        gram,
        tile_sketched,
        scalars=1,
    )
    new_right = call(finish_kernel, jax.ShapeDtypeStruct((rank, columns), f32), coefs, tile_right, *rights)
    return (new_left[None], new_right[None])


def solution(mesh):
    return jax.shard_map(
        local,
        mesh=mesh,
        in_specs=(
            P("rows", "panels", None, None),
            P("rows", "panels", None, None),
            P("panels", None, "rows"),
            P("panels", None, "rows"),
            P("rows", "panels"),
            P("rows", None, "panels"),
            P("rows", None, "panels"),
            P(),
        ),
        out_specs=(P("rows", None, "panels"), P("rows", None, "panels")),
        check_vma=False,
    )
```

time: 222 us -> 149 us (0.67); the launches traced: 218 us -> 148 us
  waiting for transfers between devices: 76.6 us -> 50.3 us
  starting transfers between devices: 46.2 us -> 29.4 us
  Pallas kernels: 55.5 us -> 41.4 us
  between operations: 14.8 us -> 0.97 us
  blocking collectives: 10.2 us -> 0 us
  local copies, waits for them, and re-layouts: 2.44 us -> 10.4 us
  matrix products: 7.8 us -> 11.5 us
    ppermute x16 -> x24, waiting for transfers between devices: 54.5 us -> 21.9 us  [swap(): return lax.ppermute(value, axis, [(i, i ^ mask) for i in members])]
    pallas_call x1, Pallas kernels: 28.5 us -> 5.58 us  [local(): pl.pallas_call(top_kernel, in_specs=[VMEM, pl.BlockSpec(memory_space=pl.A...]
    pallas_call x3 -> x7, Pallas kernels: 13.3 us -> 29.6 us  [call(): pl.pallas_call(kernel, in_specs=[SMEM] * scalars + [VMEM] * (len(operands...]
    ppermute x16 -> x24, starting transfers between devices: 36.1 us -> 23.6 us  [swap(): return lax.ppermute(value, axis, [(i, i ^ mask) for i in members])]
    all_gather x1 -> x0, blocking collectives: 10.2 us -> none  [local(): whole_tile = lax.all_gather(tile_left, 'panels', axis=1, tiled=True)]
    unnamed x14 -> x34, local copies, waits for them, and re-layouts: 2.22 us -> 10 us
    pallas_call x2, Pallas kernels: 13.8 us -> 6.2 us  [inner_products(): pl.pallas_call(functools.partial(inner_kernel, count), grid_spec=pltpu.Pr...]
    ppermute x5 -> x3, waiting for transfers between devices: 21.4 us -> 28.3 us  [the longest x1 19.7 us: gather_line(): outer = lax.ppermute(center, 'rows', outward)]
  transfers between devices with their start and end apart: 22 -> 27, of which waited for: 7 -> 11; matrix products, arithmetic and copies ran while one was open for 6% -> 10% of each run, Pallas kernels for 25% -> 27%
where the time goes in v1:
time: 149 us; the launch traced here: 148 us
  waiting for transfers between devices  50.3 us (34%)
  Pallas kernels  41.4 us (28%)
  starting transfers between devices  29.4 us (20%)
  matrix products  11.5 us (8%)
  local copies, waits for them, and re-layouts  10.4 us (7%)
  other arithmetic  4.15 us (3%)
    pallas_call x7, Pallas kernels, call(): pl.pallas_call(kernel, in_specs=[SMEM] * scalars + [VMEM] * (len(operands...  29.6 us
    ppermute x24, starting transfers between devices, swap(): return lax.ppermute(value, axis, [(i, i ^ mask) for i in members])  23.6 us
    ppermute x24, waiting for transfers between devices, swap(): return lax.ppermute(value, axis, [(i, i ^ mask) for i in members])  21.9 us
    ppermute x1, waiting for transfers between devices, gather_line(): outer = lax.ppermute(center, 'rows', outward)  19.7 us
    unnamed x34, local copies, waits for them, and re-layouts  10 us
    dot_general x2, matrix products, dot(): lax.dot_general(a, b, (dims, ((), ())), precision=highest, preferred_elem...  9.6 us
    ppermute x1, waiting for transfers between devices, gather_line(): far = lax.ppermute(inner, 'rows', outward)  8.66 us
    pallas_call x2, Pallas kernels, inner_products(): pl.pallas_call(functools.partial(inner_kernel, count), grid_spec=pltpu.Pr...  6.2 us
  transfers between devices with their start and end apart: 27, of which 11 were waited for; matrix products, arithmetic and copies ran while one was open for 10% of the time, Pallas kernels for 27%

profile of v1, /device:TPU:1, one launch (start us, length us, event | category | flops | bytes accessed | tf_op | source)
XLA Modules:
  0.0 148.1 jit_solution(8250231087321793858)
XLA Ops:
  0.7 1.0 copy-done
  1.7 1.9 %convolution_bitcast_fusion = f32[8,64,64]{2,1,0:T(8,128)S(1)} fusion(f32[8,64,256]{2,1,0:T(8,128)} %param.10, f32[64,2048]{1,0:T(8,128)S(1)} %copy-done, s32[]{:T(128)S(6)} %select_n.39), kind=kOutput, calls=%fused_computation | convolution fusion | flops 100663296 | bytes 720900 | tf_op jit(solution)/shard_map/rb,jkb->jrk/dot_general | solution.py:364
  3.6 2.1 %collective-permute-start.3 = (f32[8,64,64]{2,1,0:T(8,128)S(1)}, f32[8,64,64]{2,1,0:T(8,128)S(1)}, u32[]{:S(2)}, u32[]{:S(2)}) collective-permute-start(f32[8,64,64]{2,1,0:T(8,128)S(1)} %convolution_bitcast_fusion), channel_id=1, source_target_pairs={{0,4},{4,0},{8,12},{12,8},{16,20},{20,16},{24,28},{28,24},{1,5},{5... | collective-permute-start | bytes 393224 | tf_op jit(solution)/shard_map/ppermute | solution.py:301
  5.7 1.3 collective-permute-start
  7.0 0.7 collective-permute-start.1
  7.7 0.3 collective-permute-start.2
  8.0 3.8 %collective-permute-done.3 = f32[8,64,64]{2,1,0:T(8,128)S(1)} collective-permute-done((f32[8,64,64]{2,1,0:T(8,128)S(1)}, f32[8,64,64]{2,1,0:T(8,128)S(1)}, u32[]{:S(2)}, u32[]{:S(2)}) %collective-permute-start.3) | collective-permute-done | bytes 131104 | tf_op jit(solution)/shard_map/ppermute | solution.py:301
  11.8 1.3 collective-permute-start.4
  13.1 9.3 %fusion.7.products = f32[512,512]{1,0:T(8,128)S(1)} fusion(f32[512,2048]{1,0:T(8,128)} %bitcast.36), kind=kOutput, calls=%fused_computation.22 | convolution fusion | flops 6442450944 | bytes 5242880 | tf_op jit(solution)/shard_map/dot_general | solution.py:20
  22.4 1.7 %collective-permute-done.4 = f32[8,64,64]{2,1,0:T(8,128)} collective-permute-done((f32[8,64,64]{2,1,0:T(8,128)S(1)}, f32[8,64,64]{2,1,0:T(8,128)}, u32[]{:S(2)}, u32[]{:S(2)}) %collective-permute-start.4) | collective-permute-done | bytes 131104 | tf_op jit(solution)/shard_map/ppermute | solution.py:301
  24.1 1.1 add.41
  25.2 1.5 collective-permute-start.6
  26.7 0.4 collective-permute-start.7
  27.1 1.3 collective-permute-start.5
  28.4 0.9 broadcast_select_fusion.1
  29.3 3.1 %collective-permute-start.8 = (f32[8,64,256]{2,1,0:T(8,128)}, f32[8,64,256]{2,1,0:T(8,128)}, u32[]{:S(2)}, u32[]{:S(2)}) collective-permute-start(f32[8,64,256]{2,1,0:T(8,128)} %broadcast_select_fusion.1), channel_id=1, source_target_pairs={{0,24},{4,28},{8,12},{12,8},{16,20},{20,16},{24,0},{28,4},{1,25},{... | collective-permute-start | bytes 1572872 | tf_op jit(solution)/shard_map/ppermute | solution.py:333
  32.4 0.1 pad.6.clone
  32.5 0.1 stack.65.refs_0_
  32.6 0.3 fusion
  32.9 0.9 maximum_maximum_fusion
  33.8 19.7 %collective-permute-done.5 = f32[8,64,256]{2,1,0:T(8,128)} collective-permute-done((f32[8,64,256]{2,1,0:T(8,128)S(1)}, f32[8,64,256]{2,1,0:T(8,128)}, u32[]{:S(2)}, u32[]{:S(2)}) %collective-permute-start.5) | collective-permute-done | bytes 524320 | tf_op jit(solution)/shard_map/ppermute | solution.py:329
  53.5 2.1 %collective-permute-start.10 = (f32[64,640]{1,0:T(8,128)S(1)}, f32[64,640]{1,0:T(8,128)S(1)}, u32[]{:S(2)}, u32[]{:S(2)}) collective-permute-start(f32[64,640]{1,0:T(8,128)S(1)} %maximum_maximum_fusion), channel_id=1, source_target_pairs={{0,1},{1,0},{2,3},{3,2},{4,5},{5,4},{6,7},{7,6},{8,9},{9,8},{10,11... | collective-permute-start | bytes 491528 | tf_op jit(solution)/shard_map/ppermute | solution.py:301
  55.6 1.1 broadcast_select_fusion.refs_12_
  56.7 0.3 collective-permute-start.9
  57.1 1.3 collective-permute-start.11
  58.4 1.3 collective-permute-start.12
  59.7 1.5 collective-permute-start.13
  61.2 2.2 %copy-done.1 = f32[1,8,64,2048]{3,2,1,0:T(8,128)S(1)} copy-done((f32[1,8,64,2048]{3,2,1,0:T(8,128)S(1)}, f32[1,8,64,2048]{3,2,1,0:T(8,128)}, u32[]{:S(2)}) %copy-start.1) | copy-done | bytes 4194328
  63.4 1.0 copy-done.5
  64.4 1.0 copy-done.7
  65.5 4.4 %shard_map.95.refs_5_ = f32[8,64,64]{2,1,0:T(8,128)S(1)} custom-call(s32[7]{0:T(128)S(1)} %stack.65.refs_0_, f32[1,8,64,2048]{3,2,1,0:T(8,128)S(1)} %copy-done.1, f32[1,8,64,2048]{3,2,1,0:T(8,128)S(1)} %copy-done.1, f32[1,8,64,2048]{3,2,1,0:T(8,128)S(1)} %copy-done.1, f32[1,8,64,2048]{3,2,1,0:T(8,128)S(1)} %copy-done.1, f32[1,8,64,2048]{3,2,1,0:T(8,128)S(1)} %copy-done.1, ...), custom_call_target="tpu_custom_call" | custom-call | flops 100000000 | bytes 1000000 | tf_op jit(solution)/shard_map/pallas_call | solution.py:141
  69.9 1.7 %collective-permute-done.9 = f32[8,64,64]{2,1,0:T(8,128)S(1)} collective-permute-done((f32[8,64,64]{2,1,0:T(8,128)S(1)}, f32[8,64,64]{2,1,0:T(8,128)S(1)}, u32[]{:S(2)}, u32[]{:S(2)}) %collective-permute-start.9) | collective-permute-done | bytes 131104 | tf_op jit(solution)/shard_map/ppermute | solution.py:301
  71.8 8.7 %collective-permute-done.13.refs_4_ = f32[8,64,256]{2,1,0:T(8,128)S(1)} collective-permute-done((f32[8,64,256]{2,1,0:T(8,128)}, f32[8,64,256]{2,1,0:T(8,128)S(1)}, u32[]{:S(2)}, u32[]{:S(2)}) %collective-permute-start.13) | collective-permute-done | bytes 524320 | tf_op jit(solution)/shard_map/ppermute | solution.py:340
  80.5 0.4 collective-permute-start.17
  80.9 1.8 %shard_map.97.inner = f32[8,64,64]{2,1,0:T(8,128)S(1)} custom-call(s32[2]{0:T(128)S(1)} %pad_add_fusion.refs_0_, f32[1,8,64,2048]{3,2,1,0:T(8,128)S(1)} %copy-done.2, f32[1,8,64,2048]{3,2,1,0:T(8,128)S(1)} %copy-done.2, f32[8,64,256]{2,1,0:T(8,128)S(1)} %collective-permute-done.12.refs_3_, f32[8,64,256]{2,1,0:T(8,128)S(1)} %collective-permute-done.13.refs_4_, ...), custom_call_target="tpu_custom_call" | custom-call | flops 100000000 | bytes 1000000 | tf_op jit(solution)/shard_map/pallas_call | solution.py:141
  82.7 11.2 %shard_map.98 = (f32[64,512]{1,0:T(8,128)S(1)}, f32[64,576]{1,0:T(8,128)S(1)}) custom-call(s32[1,8]{1,0:T(1,128)S(1)} %copy-done.15, f32[8,64,64]{2,1,0:T(8,128)S(1)} %add.43.sketched, f32[8,64,64]{2,1,0:T(8,128)S(1)} %shard_map.97.inner, f32[512,512]{1,0:T(8,128)S(1)} %fusion.7.products), custom_call_target="tpu_custom_call" | custom-call | flops 100000000 | bytes 1000000 | tf_op jit(solution)/shard_map/pallas_call | solution.py:288
  94.0 2.2 %collective-permute-start.15 = (f32[64,512]{1,0:T(8,128)S(1)}, f32[64,512]{1,0:T(8,128)S(1)}, u32[]{:S(2)}, u32[]{:S(2)}) collective-permute-start(f32[64,512]{1,0:T(8,128)S(1)} %get-tuple-element.80.refs_0_), channel_id=1, source_target_pairs={{0,8},{4,12},{8,0},{12,4},{16,24},{20,28},{24,16},{28,20},{1,9},{5... | collective-permute-start | bytes 393224 | tf_op jit(solution)/shard_map/ppermute | solution.py:301
  96.1 1.1 collective-permute-start.16
  97.2 5.6 %shard_map.99 = (f32[64,2048]{1,0:T(8,128)S(1)}, f32[64,2048]{1,0:T(8,128)S(1)}, f32[64,128]{1,0:T(8,128)S(1)}) custom-call(f32[64,576]{1,0:T(8,128)S(1)} %get-tuple-element.73.whole, f32[512,2048]{1,0:T(8,128)S(1)} %bitcast.37), custom_call_target="tpu_custom_call" | custom-call | flops 100000000 | bytes 1000000 | tf_op jit(solution)/shard_map/pallas_call | solution.py:402
  102.8 6.2 %collective-permute-done.15.refs_2_ = f32[64,512]{1,0:T(8,128)S(1)} collective-permute-done((f32[64,512]{1,0:T(8,128)S(1)}, f32[64,512]{1,0:T(8,128)S(1)}, u32[]{:S(2)}, u32[]{:S(2)}) %collective-permute-start.15) | collective-permute-done | bytes 131104 | tf_op jit(solution)/shard_map/ppermute | solution.py:301
  109.1 2.3 %collective-permute-done.16.refs_3_ = f32[64,512]{1,0:T(8,128)S(1)} collective-permute-done((f32[64,512]{1,0:T(8,128)S(1)}, f32[64,512]{1,0:T(8,128)S(1)}, u32[]{:S(2)}, u32[]{:S(2)}) %collective-permute-start.16) | collective-permute-done | bytes 131104 | tf_op jit(solution)/shard_map/ppermute | solution.py:301
  111.4 0.3 collective-permute-start.19
  111.7 0.8 collective-permute-start.18
  112.4 1.0 shard_map.101
  113.5 1.3 collective-permute-start.20
  114.8 1.4 collective-permute-start.22
  116.2 2.5 %collective-permute-done.20.side = f32[64,512]{1,0:T(8,128)S(1)} collective-permute-done((f32[64,512]{1,0:T(8,128)S(1)}, f32[64,512]{1,0:T(8,128)S(1)}, u32[]{:S(2)}, u32[]{:S(2)}) %collective-permute-start.20) | collective-permute-done | bytes 131104 | tf_op jit(solution)/shard_map/ppermute | solution.py:301
  118.7 0.7 copy-done.9
  119.3 0.2 collective-permute-done.21.near
  119.6 0.7 copy-done.11
  120.2 2.1 %collective-permute-done.22.near_side = f32[64,512]{1,0:T(8,128)S(1)} collective-permute-done((f32[64,512]{1,0:T(8,128)S(1)}, f32[64,512]{1,0:T(8,128)S(1)}, u32[]{:S(2)}, u32[]{:S(2)}) %collective-permute-start.22) | collective-permute-done | bytes 131104 | tf_op jit(solution)/shard_map/ppermute | solution.py:301
  122.4 0.7 copy-done.13
  123.0 1.4 collective-permute-done.19.far
  124.4 1.3 collective-permute-start.23
  125.7 0.1 stack.76.spots
  125.8 3.5 %shard_map.100 = (f32[64,64]{1,0:T(8,128)S(1)}, f32[64,2048]{1,0:T(8,128)S(1)}, f32[128,128]{1,0:T(8,128)S(1)}) custom-call(f32[64,2048]{1,0:T(8,128)S(1)} %get-tuple-element.75.own, f32[64,2048]{1,0:T(8,128)} %collective-permute-done.18.partner, f32[64,2048]{1,0:T(8,128)S(1)} %get-tuple-element.76.top, f32[64,128]{1,0:T(8,128)S(1)} %get-tuple-element.77.squares, ...), custom_call_target="tpu_custom_call" | custom-call | flops 100000000 | bytes 1000000 | tf_op jit(solution)/shard_map/pallas_call | solution.py:288
  129.3 0.9 copy-done.10
  130.2 0.9 copy-done.12
  131.1 0.9 copy-done.14
  132.1 1.2 shard_map.103
  133.3 0.3 collective-permute-start.25
  133.6 1.8 %collective-permute-start.26 = (f32[64,512]{1,0:T(8,128)S(1)}, f32[64,512]{1,0:T(8,128)S(1)}, u32[]{:S(2)}, u32[]{:S(2)}) collective-permute-start(f32[64,512]{1,0:T(8,128)S(1)} %get-tuple-element.103), channel_id=1, source_target_pairs={{0,3},{1,2},{2,1},{3,0},{4,7},{5,6},{6,5},{7,4},{8,11},{9,10},{10,... | collective-permute-start | bytes 393224 | tf_op jit(solution)/shard_map/ppermute | solution.py:301
  135.4 11.6 %shard_map.102 = (f32[64,512]{1,0:T(8,128)}, f32[64,192]{1,0:T(8,128)S(1)}) custom-call(s32[1]{0:T(128)} %bitcast.chunk, f32[64,2048]{1,0:T(8,128)S(1)} %get-tuple-element.79.near, f32[64,2048]{1,0:T(8,128)S(1)} %collective-permute-done.19.far, f32[64,2048]{1,0:T(8,128)S(1)} %collective-permute-done.23.far_core, ...), custom_call_target="tpu_custom_call" | custom-call | flops 100000000 | bytes 1000000 | tf_op jit(solution)/shard_map/pallas_call | solution.py:288
  147.1 1.0 shard_map.104
  (56 shorter events, 0.6 us)
Async XLA Ops:
  0.6 1.0 copy-start
  3.6 8.2 %collective-permute-start.3 = (f32[8,64,64]{2,1,0:T(8,128)S(1)}, f32[8,64,64]{2,1,0:T(8,128)S(1)}, u32[]{:S(2)}, u32[]{:S(2)}) collective-permute-start(f32[8,64,64]{2,1,0:T(8,128)S(1)} %convolution_bitcast_fusion), channel_id=1, source_target_pairs={{0,4},{4,0},{8,12},{12,8},{16,20},{20,16},{24,28},{28,24},{1,5},{5... | collective-permute-start | bytes 393224 | tf_op jit(solution)/shard_map/ppermute | solution.py:301
  5.7 19.5 %collective-permute-start = (f32[8,64,256]{2,1,0:T(8,128)}, f32[8,64,256]{2,1,0:T(8,128)S(1)}, u32[]{:S(2)}, u32[]{:S(2)}) collective-permute-start(f32[8,64,256]{2,1,0:T(8,128)} %refs_8_.1), channel_id=1, source_target_pairs={{0,8},{4,12},{8,0},{12,4},{16,24},{20,28},{24,16},{28,20},{1,9},{5... | collective-permute-start | bytes 1572872 | tf_op jit(solution)/shard_map/ppermute | solution.py:301
  7.0 18.2 %collective-permute-start.1 = (f32[8,64,256]{2,1,0:T(8,128)}, f32[8,64,256]{2,1,0:T(8,128)S(1)}, u32[]{:S(2)}, u32[]{:S(2)}) collective-permute-start(f32[8,64,256]{2,1,0:T(8,128)} %refs_8_.1), channel_id=1, source_target_pairs={{8,16},{12,20},{16,8},{20,12},{9,17},{13,21},{17,9},{21,13},{10,18... | collective-permute-start | bytes 1572872 | tf_op jit(solution)/shard_map/ppermute | solution.py:301
  7.7 17.5 %collective-permute-start.2 = (f32[8,64,256]{2,1,0:T(8,128)}, f32[8,64,256]{2,1,0:T(8,128)S(1)}, u32[]{:S(2)}, u32[]{:S(2)}) collective-permute-start(f32[8,64,256]{2,1,0:T(8,128)} %refs_8_.1), channel_id=1, source_target_pairs={{0,4},{4,0},{8,12},{12,8},{16,20},{20,16},{24,28},{28,24},{1,5},{5... | collective-permute-start | bytes 1572872 | tf_op jit(solution)/shard_map/ppermute | solution.py:301
  11.8 10.6 %copy-start.16 = (f32[8,64,64]{2,1,0:T(8,128)}, f32[8,64,64]{2,1,0:T(8,128)S(1)}, u32[]{:S(2)}) copy-start(f32[8,64,64]{2,1,0:T(8,128)S(1)} %add.40) | copy-start | bytes 393220
  11.8 12.3 %collective-permute-start.4 = (f32[8,64,64]{2,1,0:T(8,128)S(1)}, f32[8,64,64]{2,1,0:T(8,128)}, u32[]{:S(2)}, u32[]{:S(2)}) collective-permute-start(f32[8,64,64]{2,1,0:T(8,128)S(1)} %add.40), channel_id=1, source_target_pairs={{0,8},{4,12},{8,0},{12,4},{16,24},{20,28},{24,16},{28,20},{1,9},{5... | collective-permute-start | bytes 393224 | tf_op jit(solution)/shard_map/ppermute | solution.py:301
  13.1 19.5 %copy-start.8 = (f32[1,64,512]{2,1,0:T(8,128)S(1)}, f32[1,64,512]{2,1,0:T(8,128)}, u32[]{:S(2)}) copy-start(f32[1,64,512]{2,1,0:T(8,128)} %param.14) | copy-start | bytes 393220
  25.2 31.9 %copy-start.6 = (f32[8,64,256]{2,1,0:T(8,128)}, f32[8,64,256]{2,1,0:T(8,128)S(1)}, u32[]{:S(2)}) copy-start(f32[8,64,256]{2,1,0:T(8,128)S(1)} %collective-permute-done.refs_10_) | copy-start | bytes 1572868
  25.2 28.2 %collective-permute-start.6 = (f32[8,64,256]{2,1,0:T(8,128)S(1)}, f32[8,64,256]{2,1,0:T(8,128)}, u32[]{:S(2)}, u32[]{:S(2)}) collective-permute-start(f32[8,64,256]{2,1,0:T(8,128)S(1)} %collective-permute-done.refs_10_), channel_id=1, source_target_pairs={{8,16},{12,20},{16,8},{20,12},{9,17},{13,21},{17,9},{21,13},{10,18... | collective-permute-start | bytes 1572872 | tf_op jit(solution)/shard_map/ppermute | solution.py:301
  26.7 26.7 %collective-permute-start.7 = (f32[8,64,256]{2,1,0:T(8,128)S(1)}, f32[8,64,256]{2,1,0:T(8,128)}, u32[]{:S(2)}, u32[]{:S(2)}) collective-permute-start(f32[8,64,256]{2,1,0:T(8,128)S(1)} %collective-permute-done.refs_10_), channel_id=1, source_target_pairs={{0,4},{4,0},{8,12},{12,8},{16,20},{20,16},{24,28},{28,24},{1,5},{5... | collective-permute-start | bytes 1572872 | tf_op jit(solution)/shard_map/ppermute | solution.py:301
  27.1 26.3 %collective-permute-start.5 = (f32[8,64,256]{2,1,0:T(8,128)S(1)}, f32[8,64,256]{2,1,0:T(8,128)}, u32[]{:S(2)}, u32[]{:S(2)}) collective-permute-start(f32[8,64,256]{2,1,0:T(8,128)S(1)} %collective-permute-done.1.refs_14_), channel_id=1, source_target_pairs={{8,0},{12,4},{16,24},{20,28},{9,1},{13,5},{17,25},{21,29},{10,2},{... | collective-permute-start | bytes 1572872 | tf_op jit(solution)/shard_map/ppermute | solution.py:329
  29.3 24.2 %collective-permute-start.8 = (f32[8,64,256]{2,1,0:T(8,128)}, f32[8,64,256]{2,1,0:T(8,128)}, u32[]{:S(2)}, u32[]{:S(2)}) collective-permute-start(f32[8,64,256]{2,1,0:T(8,128)} %broadcast_select_fusion.1), channel_id=1, source_target_pairs={{0,24},{4,28},{8,12},{12,8},{16,20},{20,16},{24,0},{28,4},{1,25},{... | collective-permute-start | bytes 1572872 | tf_op jit(solution)/shard_map/ppermute | solution.py:333
  53.5 3.6 %collective-permute-start.10 = (f32[64,640]{1,0:T(8,128)S(1)}, f32[64,640]{1,0:T(8,128)S(1)}, u32[]{:S(2)}, u32[]{:S(2)}) collective-permute-start(f32[64,640]{1,0:T(8,128)S(1)} %maximum_maximum_fusion), channel_id=1, source_target_pairs={{0,1},{1,0},{2,3},{3,2},{4,5},{5,4},{6,7},{7,6},{8,9},{9,8},{10,11... | collective-permute-start | bytes 491528 | tf_op jit(solution)/shard_map/ppermute | solution.py:301
  56.7 14.9 %collective-permute-start.9 = (f32[8,64,64]{2,1,0:T(8,128)S(1)}, f32[8,64,64]{2,1,0:T(8,128)S(1)}, u32[]{:S(2)}, u32[]{:S(2)}) collective-permute-start(f32[8,64,64]{2,1,0:T(8,128)S(1)} %add.41), channel_id=1, source_target_pairs={{0,16},{4,20},{8,24},{12,28},{16,0},{20,4},{24,8},{28,12},{1,17},{... | collective-permute-start | bytes 393224 | tf_op jit(solution)/shard_map/ppermute | solution.py:301
  57.1 14.5 %collective-permute-start.11 = (f32[2,64,640]{2,1,0:T(8,128)S(1)}, f32[2,64,640]{2,1,0:T(8,128)S(1)}, u32[]{:S(2)}, u32[]{:S(2)}) collective-permute-start(f32[2,64,640]{2,1,0:T(8,128)S(1)} %pad_maximum_fusion), channel_id=1, source_target_pairs={{0,2},{1,3},{2,0},{3,1},{4,6},{5,7},{6,4},{7,5},{8,10},{9,11},{10,... | collective-permute-start | bytes 983048 | tf_op jit(solution)/shard_map/ppermute | solution.py:301
  58.4 13.3 %collective-permute-start.12 = (f32[8,64,256]{2,1,0:T(8,128)S(1)}, f32[8,64,256]{2,1,0:T(8,128)S(1)}, u32[]{:S(2)}, u32[]{:S(2)}) collective-permute-start(f32[8,64,256]{2,1,0:T(8,128)S(1)} %broadcast_select_fusion.refs_12_), channel_id=1, source_target_pairs={{0,4},{4,0},{8,12},{12,8},{16,20},{20,16},{24,28},{28,24},{1,5},{5... | collective-permute-start | bytes 1572872 | tf_op jit(solution)/shard_map/ppermute | solution.py:301
  59.7 20.7 %collective-permute-start.13 = (f32[8,64,256]{2,1,0:T(8,128)}, f32[8,64,256]{2,1,0:T(8,128)S(1)}, u32[]{:S(2)}, u32[]{:S(2)}) collective-permute-start(f32[8,64,256]{2,1,0:T(8,128)} %collective-permute-done.6), channel_id=1, source_target_pairs={{8,0},{12,4},{16,24},{20,28},{9,1},{13,5},{17,25},{21,29},{10,2},{... | collective-permute-start | bytes 1572872 | tf_op jit(solution)/shard_map/ppermute | solution.py:340
  61.2 2.2 %copy-start.1 = (f32[1,8,64,2048]{3,2,1,0:T(8,128)S(1)}, f32[1,8,64,2048]{3,2,1,0:T(8,128)}, u32[]{:S(2)}) copy-start(f32[1,8,64,2048]{3,2,1,0:T(8,128)} %refs_2_.3) | copy-start | bytes 12582916
  63.4 1.0 copy-start.5
  64.4 1.0 copy-start.7
  65.5 14.9 %copy-start.4 = (f32[8,64,256]{2,1,0:T(8,128)S(1)}, f32[8,64,256]{2,1,0:T(8,128)}, u32[]{:S(2)}) copy-start(f32[8,64,256]{2,1,0:T(8,128)} %param.10) | copy-start | bytes 1572868
  65.5 15.4 %copy-start.2 = (f32[1,8,64,2048]{3,2,1,0:T(8,128)S(1)}, f32[1,8,64,2048]{3,2,1,0:T(8,128)}, u32[]{:S(2)}) copy-start(f32[1,8,64,2048]{3,2,1,0:T(8,128)} %refs_2_.3) | copy-start | bytes 12582916
  80.5 30.9 %collective-permute-start.17 = (f32[512,256]{1,0:T(8,128)S(1)}, f32[512,256]{1,0:T(8,128)S(1)}, u32[]{:S(2)}, u32[]{:S(2)}) collective-permute-start(f32[512,256]{1,0:T(8,128)S(1)} %shard_map.96.refs_4_), channel_id=1, source_target_pairs={{0,16},{4,20},{8,24},{12,28},{16,0},{20,4},{24,8},{28,12},{1,17},{... | collective-permute-start | bytes 1572872 | tf_op jit(solution)/shard_map/ppermute | solution.py:301
  80.9 1.8 %copy-start.15 = (s32[1,8]{1,0:T(1,128)S(1)}, s32[1,8]{1,0:T(1,128)}, u32[]{:S(2)}) copy-start(s32[1,8]{1,0:T(1,128)} %weights.1) | copy-start | bytes 100
  80.9 16.3 %copy-start.3 = (f32[1,8,64,2048]{3,2,1,0:T(8,128)S(1)}, f32[1,8,64,2048]{3,2,1,0:T(8,128)}, u32[]{:S(2)}) copy-start(f32[1,8,64,2048]{3,2,1,0:T(8,128)} %param.8) | copy-start | bytes 12582916
  93.9 8.9 %collective-permute-start.14 = (f32[64,512]{1,0:T(8,128)S(1)}, f32[64,512]{1,0:T(8,128)S(1)}, u32[]{:S(2)}, u32[]{:S(2)}) collective-permute-start(f32[64,512]{1,0:T(8,128)S(1)} %get-tuple-element.80.refs_0_), channel_id=1, source_target_pairs={{0,4},{4,0},{8,12},{12,8},{16,20},{20,16},{24,28},{28,24},{1,5},{5... | collective-permute-start | bytes 393224 | tf_op jit(solution)/shard_map/ppermute | solution.py:301
  94.0 15.1 %collective-permute-start.15 = (f32[64,512]{1,0:T(8,128)S(1)}, f32[64,512]{1,0:T(8,128)S(1)}, u32[]{:S(2)}, u32[]{:S(2)}) collective-permute-start(f32[64,512]{1,0:T(8,128)S(1)} %get-tuple-element.80.refs_0_), channel_id=1, source_target_pairs={{0,8},{4,12},{8,0},{12,4},{16,24},{20,28},{24,16},{28,20},{1,9},{5... | collective-permute-start | bytes 393224 | tf_op jit(solution)/shard_map/ppermute | solution.py:301
  96.1 15.3 %collective-permute-start.16 = (f32[64,512]{1,0:T(8,128)S(1)}, f32[64,512]{1,0:T(8,128)S(1)}, u32[]{:S(2)}, u32[]{:S(2)}) collective-permute-start(f32[64,512]{1,0:T(8,128)S(1)} %get-tuple-element.80.refs_0_), channel_id=1, source_target_pairs={{0,12},{4,8},{8,4},{12,0},{16,28},{20,24},{24,20},{28,16},{1,13},{... | collective-permute-start | bytes 393224 | tf_op jit(solution)/shard_map/ppermute | solution.py:301
  111.4 13.0 %collective-permute-start.19 = (f32[64,2048]{1,0:T(8,128)S(1)}, f32[64,2048]{1,0:T(8,128)S(1)}, u32[]{:S(2)}, u32[]{:S(2)}) collective-permute-start(f32[64,2048]{1,0:T(8,128)S(1)} %get-tuple-element.75.own), channel_id=1, source_target_pairs={{0,2},{1,3},{2,0},{3,1},{4,6},{5,7},{6,4},{7,5},{8,10},{9,11},{10,... | collective-permute-start | bytes 1572872 | tf_op jit(solution)/shard_map/ppermute | solution.py:301
  111.7 14.2 %collective-permute-start.18 = (f32[64,2048]{1,0:T(8,128)S(1)}, f32[64,2048]{1,0:T(8,128)}, u32[]{:S(2)}, u32[]{:S(2)}) collective-permute-start(f32[64,2048]{1,0:T(8,128)S(1)} %get-tuple-element.75.own), channel_id=1, source_target_pairs={{0,1},{1,0},{2,3},{3,2},{4,5},{5,4},{6,7},{7,6},{8,9},{9,8},{10,11... | collective-permute-start | bytes 1572872 | tf_op jit(solution)/shard_map/ppermute | solution.py:301
  113.5 5.2 %collective-permute-start.20 = (f32[64,512]{1,0:T(8,128)S(1)}, f32[64,512]{1,0:T(8,128)S(1)}, u32[]{:S(2)}, u32[]{:S(2)}) collective-permute-start(f32[64,512]{1,0:T(8,128)S(1)} %get-tuple-element.87), channel_id=1, source_target_pairs={{0,4},{4,0},{8,12},{12,8},{16,20},{20,16},{24,28},{28,24},{1,5},{5... | collective-permute-start | bytes 393224 | tf_op jit(solution)/shard_map/ppermute | solution.py:301
  114.8 4.8 %collective-permute-start.21 = (f32[64,512]{1,0:T(8,128)S(1)}, f32[64,512]{1,0:T(8,128)S(1)}, u32[]{:S(2)}, u32[]{:S(2)}) collective-permute-start(f32[64,512]{1,0:T(8,128)S(1)} %get-tuple-element.88), channel_id=1, source_target_pairs={{0,8},{4,12},{8,0},{12,4},{16,24},{20,28},{24,16},{28,20},{1,9},{5... | collective-permute-start | bytes 393224 | tf_op jit(solution)/shard_map/ppermute | solution.py:301
  114.8 7.6 %collective-permute-start.22 = (f32[64,512]{1,0:T(8,128)S(1)}, f32[64,512]{1,0:T(8,128)S(1)}, u32[]{:S(2)}, u32[]{:S(2)}) collective-permute-start(f32[64,512]{1,0:T(8,128)S(1)} %get-tuple-element.89), channel_id=1, source_target_pairs={{0,12},{4,8},{8,4},{12,0},{16,28},{20,24},{24,20},{28,16},{1,13},{... | collective-permute-start | bytes 393224 | tf_op jit(solution)/shard_map/ppermute | solution.py:301
  118.7 0.7 copy-start.9
  119.6 0.7 copy-start.11
  122.4 0.7 copy-start.13
  124.4 11.0 %collective-permute-start.23 = (f32[64,2048]{1,0:T(8,128)S(1)}, f32[64,2048]{1,0:T(8,128)S(1)}, u32[]{:S(2)}, u32[]{:S(2)}) collective-permute-start(f32[64,2048]{1,0:T(8,128)S(1)} %collective-permute-done.19.far), channel_id=1, source_target_pairs={{0,1},{1,0},{2,3},{3,2},{4,5},{5,4},{6,7},{7,6},{8,9},{9,8},{10,11... | collective-permute-start | bytes 1572872 | tf_op jit(solution)/shard_map/ppermute | solution.py:301
  129.3 0.9 copy-start.10
  130.2 0.9 copy-start.12
  131.1 0.9 copy-start.14
  133.2 13.9 %collective-permute-start.24 = (f32[64,512]{1,0:T(8,128)S(1)}, f32[64,512]{1,0:T(8,128)S(1)}, u32[]{:S(2)}, u32[]{:S(2)}) collective-permute-start(f32[64,512]{1,0:T(8,128)S(1)} %get-tuple-element.101), channel_id=1, source_target_pairs={{0,1},{1,0},{2,3},{3,2},{4,5},{5,4},{6,7},{7,6},{8,9},{9,8},{10,11... | collective-permute-start | bytes 393224 | tf_op jit(solution)/shard_map/ppermute | solution.py:301
  133.3 13.8 %collective-permute-start.25 = (f32[64,512]{1,0:T(8,128)S(1)}, f32[64,512]{1,0:T(8,128)S(1)}, u32[]{:S(2)}, u32[]{:S(2)}) collective-permute-start(f32[64,512]{1,0:T(8,128)S(1)} %get-tuple-element.102), channel_id=1, source_target_pairs={{0,2},{1,3},{2,0},{3,1},{4,6},{5,7},{6,4},{7,5},{8,10},{9,11},{10,... | collective-permute-start | bytes 393224 | tf_op jit(solution)/shard_map/ppermute | solution.py:301
  133.6 13.5 %collective-permute-start.26 = (f32[64,512]{1,0:T(8,128)S(1)}, f32[64,512]{1,0:T(8,128)S(1)}, u32[]{:S(2)}, u32[]{:S(2)}) collective-permute-start(f32[64,512]{1,0:T(8,128)S(1)} %get-tuple-element.103), channel_id=1, source_target_pairs={{0,3},{1,2},{2,1},{3,0},{4,7},{5,6},{6,5},{7,4},{8,11},{9,10},{10,... | collective-permute-start | bytes 393224 | tf_op jit(solution)/shard_map/ppermute | solution.py:301

commit v2 on v1

--- a/solution.py
+++ b/solution.py
@@ -11,7 +11,7 @@
 f32 = jnp.float32
 VMEM = pl.BlockSpec(memory_space=pltpu.VMEM)
 SMEM = pl.BlockSpec(memory_space=pltpu.SMEM)
-LIMIT = pltpu.CompilerParams(vmem_limit_bytes=20 * 1024 * 1024)
+LIMIT = pltpu.CompilerParams(vmem_limit_bytes=12 * 1024 * 1024)
 ROOMY = pltpu.CompilerParams(vmem_limit_bytes=32 * 1024 * 1024)
 SHORT = pl.CostEstimate(flops=10**8, bytes_accessed=10**6, transcendentals=0)
 
@@ -34,6 +34,13 @@
 
 def identity(n):
     return (lax.broadcasted_iota(jnp.int32, (n, n), 0) == lax.broadcasted_iota(jnp.int32, (n, n), 1)).astype(f32)
+
+
+def reciprocal(value):
+    guess = pl.reciprocal(value, approx=True)
+    for _ in range(2):
+        guess = guess * (2.0 - value * guess)
+    return guess
 
 
 def inverse_factors(matrices):
@@ -61,7 +68,7 @@
             done = state[m]
             scaled = []
             for a in range(step):
-                inverse = 1.0 / pivot[a][a]
+                inverse = reciprocal(pivot[a][a])
                 for b in range(a + 1, step):
                     factor = pivot[a][b] * inverse
                     row[b] = row[b] - factor * row[a]
@@ -212,19 +219,24 @@
     sent[...] = nn(shrunk[0], factor)
 
 
-def chip_kernel(own, partner, top, squares, tile, step, near_out, gram_out):
+def chip_kernel(place, own, partner, top, squares, tiles, tiles_core, step, near_out, tile_out, sketched, gram_out):
+    rank, width = top.shape
+    columns = width // 4
+    step[...] = nn(squares[:, rank:] + nt_parts(partner[...], top[...]), squares[:, :rank])
     near = own[...] + partner[...]
     near_out[...] = near
-    rank = top.shape[0]
-    step[...] = nn(squares[:, rank:] + nt(partner[...], top[...]), squares[:, :rank])
-    stack = jnp.concatenate([tile[...], near], axis=0)
-    gram_out[...] = nt(stack, stack)
+    parts = [tiles[0], tiles_core[0], tiles[1], tiles_core[1]]
+    sketched[...] = sum(part[:, columns : columns + rank] for part in parts)
+    for k, part in enumerate(parts):
+        tile_out[:, pl.ds(pl.multiple_of((place[0] ^ k) * columns, columns), columns)] = part[:, :columns]
+    stack = jnp.concatenate([tile_out[...], near], axis=0)
+    gram_out[...] = nt_parts(stack, stack)
 
 
 def root_kernel(chunk, near, far, far_core, tile, gram_in, sketched, new_left, coefs_out):
     rank, width = tile.shape
     other = far[...] + far_core[...]
-    cross = nt(other, jnp.concatenate([tile[...], near[...], other], axis=0))
+    cross = nt_parts(other, jnp.concatenate([tile[...], near[...], other], axis=0))
     above = jnp.concatenate([gram_in[...], cross[:, : 2 * rank].T], axis=1)
     gram = jnp.concatenate([above, cross], axis=0)
     parts = [slice(k * rank, (k + 1) * rank) for k in range(3)]
@@ -301,17 +313,12 @@
     return lax.ppermute(value, axis, [(i, i ^ mask) for i in members])
 
 
-def chip_step(sent, top, squares, tile):
-    rank, width = tile.shape
+def chip_step(place, sent, top, squares, tiles, tiles_core):
+    rank, width = top.shape
     core = swap(sent, "panels", 1)
-    shapes = [held(rank, rank), held(rank, width), held(2 * rank, 2 * rank)]
-    return core, *call(chip_kernel, shapes, sent, core, top, squares, tile)
-
-
-def gather_panels(value):
-    core = swap(value, "panels", 1)
-    far = swap(jnp.stack([value, core]), "panels", 2)
-    return [value, core, far[0], far[1]]
+    square, wide = held(rank, rank), held(rank, width)
+    shapes = [square, wide, wide, square, held(2 * rank, 2 * rank)]
+    return call(chip_kernel, shapes, place, sent, core, top, squares, tiles, tiles_core, scalars=1)
 
 
 def gather_line(block, index, partial, tile, beside):
@@ -324,9 +331,9 @@
     side = swap(block, "rows", 1)
     for mask in (1, 2):
         partial = partial + swap(partial, "rows", mask)
+    outer = lax.ppermute(center, "rows", outward)
     near, center, side, partial, beside = lax.optimization_barrier((near, center, side, partial, beside))
 
-    outer = lax.ppermute(center, "rows", outward)
     inner = swap(near, "rows", 6, middle)
     near_side = swap(near, "rows", 1)
     crossed = jnp.where(is_end, side, center)
@@ -340,7 +347,7 @@
     far = lax.ppermute(inner, "rows", outward)
     opposite_side = swap(opposite, "rows", 1)
     partial = partial + swap(partial, "rows", 4)
-    tiles = gather_panels(tile)
+    tiles = jnp.stack([tile, swap(tile, "panels", 2)])
     early = [block, side, near, near_side, opposite, far_side, center]
     late = [opposite_side, far]
     return [(v, index ^ k) for v, k in zip(early, (0, 1, 2, 3, 4, 7, 6))], [
@@ -359,6 +366,7 @@
     square = held(rank, rank)
     chunk = held(rank, columns)
     tile_left, tile_right = tile_left[0], tile_right[0]
+    spot = place.reshape(1).astype(jnp.int32)
 
     sketch_here = lax.dynamic_slice_in_dim(sketch, row * local_columns, local_columns, 1)
     sketched = jnp.einsum("rb,jkb->jrk", sketch_here, pivot_left, precision=highest)
@@ -372,16 +380,12 @@
         early, late, sketched, tiles, products = gather_line(pivot_right, row, sketched, tile, products)
     else:
         sketched = lax.psum(sketched, "rows")
-        tiles = gather_panels(tile)
-    tile_sketched = sum(tile[:, columns : columns + rank] for tile in tiles)
-    whole_tile = jnp.zeros((rank, width), f32)
-    for mask, tile in enumerate(tiles):
-        whole_tile = lax.dynamic_update_slice_in_dim(whole_tile, tile[:, :columns], (place ^ mask) * columns, 1)
+        tiles = jnp.stack([tile, swap(tile, "panels", 2)])
 
     if routed:
         inner = inner_products(panel_right, [v for v, _ in early], [s for _, s in early])
-        inner, sketched, tile_sketched, whole_tile = lax.optimization_barrier((inner, sketched, tile_sketched, whole_tile))
-        _, pivot_left = lax.optimization_barrier((late, pivot_left))
+        inner, sketched, tiles = lax.optimization_barrier((inner, sketched, tiles))
+        _, pivot_left, tiles = lax.optimization_barrier((late, pivot_left, tiles))
         pivot = call(copy_kernel, held(count * rank, local_columns), pivot_left.reshape(count * rank, local_columns))
         inner, pivot = lax.optimization_barrier((inner, pivot))
         opposite = swap(pivot, "rows", 4)
@@ -389,6 +393,7 @@
     else:
         full = lax.all_gather(pivot_right, "rows", axis=2, tiled=True)
         inner = inner_products(panel_right, [full], [jnp.int32(0)])
+    tiles_core = swap(tiles, "panels", 1)
 
     path, whole = call(
         tree_kernel,
@@ -405,7 +410,7 @@
         out_specs=[VMEM] * 3,
         out_shape=[wide, wide, held(rank, 2 * rank)],
         scratch_shapes=[pltpu.VMEM(panel.shape, f32), pltpu.SemaphoreType.DMA],
-        compiler_params=LIMIT,
+        compiler_params=ROOMY,
         cost_estimate=SHORT,
     )(whole, panel)
     if routed:
@@ -414,16 +419,16 @@
         half = held(rank, 2 * local_columns)
         paths, pieces, sent = lax.optimization_barrier((paths, pieces, sent))
         far = swap(sent, "panels", 2)
-        core, step, near, gram = chip_step(sent, top, squares, whole_tile)
+        step, near, whole_tile, tile_sketched, gram = chip_step(spot, sent, top, squares, tiles, tiles_core)
         mine, *given = call(right_kernel, [half] * 4, *paths, *pieces)
         got = [mine] + [swap(v, "rows", mask) for mask, v in zip((1, 2, 3), given)]
-        far, got = lax.optimization_barrier((far, got))
         depth = row // 2
         spots = jnp.stack([depth ^ place, depth ^ 2 ^ place, depth ^ 1 ^ place, depth ^ 3 ^ place, row % 2])
         parts = call(collect_kernel, [chunk] * 4, spots.astype(jnp.int32), step, *got, scalars=1, scratch=[pltpu.VMEM((4, rank, columns), f32)])
-        rights = [swap(parts[mask], "panels", mask) if mask else parts[0] for mask in range(4)]
+        far, own_part = lax.optimization_barrier((far, parts[0]))
+        rights = [own_part] + [swap(parts[mask], "panels", mask) for mask in (1, 2, 3)]
     else:
-        core, step, near, gram = chip_step(sent, top, squares, whole_tile)
+        step, near, whole_tile, tile_sketched, gram = chip_step(spot, sent, top, squares, tiles, tiles_core)
         far = swap(sent, "panels", 2)
         full_left = lax.all_gather(pivot_left, "rows", axis=2, tiled=True)
         right = nn(step, nn(path, full_left.reshape(count * rank, width)))
@@ -436,7 +441,7 @@
     new_left, coefs = call(
         root_kernel,
         [jax.ShapeDtypeStruct((rank, columns), f32), held(rank, 3 * rank)],
-        place.reshape(1).astype(jnp.int32),
+        spot,
         near,
         far,
         far_core,

time: 149 us -> 139 us (0.933)
  waiting for transfers between devices: 50.3 us -> 35.7 us
  other arithmetic: 4.15 us -> 6.78 us
  Pallas kernels: 41.4 us -> 44 us
  local copies, waits for them, and re-layouts: 10.4 us -> 8.02 us
  starting transfers between devices: 29.4 us -> 31 us
    ppermute x1, waiting for transfers between devices: 8.66 us -> 1.35 us  [gather_line(): far = lax.ppermute(inner, 'rows', outward)]
    ppermute x24, waiting for transfers between devices: 21.9 us -> 15.3 us  [swap(): return lax.ppermute(value, axis, [(i, i ^ mask) for i in members])]
    unnamed x34 -> x30, local copies, waits for them, and re-layouts: 10 us -> 7.77 us
    ppermute x24, starting transfers between devices: 23.6 us -> 25.1 us  [swap(): return lax.ppermute(value, axis, [(i, i ^ mask) for i in members])]
  transfers between devices with their start and end apart: 27 -> 27, of which waited for: 11 -> 8; matrix products, arithmetic and copies ran while one was open for 10% -> 11% of each run, Pallas kernels for 27% -> 31%
where the time goes in v2:
time: 139 us; the launch traced here: 138 us
  Pallas kernels  44 us (32%)
  waiting for transfers between devices  35.7 us (26%)
  starting transfers between devices  31 us (22%)
  matrix products  11.6 us (8%)
  local copies, waits for them, and re-layouts  8.02 us (6%)
  other arithmetic  6.78 us (5%)
    pallas_call x7, Pallas kernels, call(): pl.pallas_call(kernel, in_specs=[SMEM] * scalars + [VMEM] * (len(operands...  30.4 us
    ppermute x24, starting transfers between devices, swap(): return lax.ppermute(value, axis, [(i, i ^ mask) for i in members])  25.1 us
    ppermute x1, waiting for transfers between devices, gather_line(): outer = lax.ppermute(center, 'rows', outward)  19.1 us
    ppermute x24, waiting for transfers between devices, swap(): return lax.ppermute(value, axis, [(i, i ^ mask) for i in members])  15.3 us
    dot_general x2, matrix products, dot(): lax.dot_general(a, b, (dims, ((), ())), precision=highest, preferred_elem...  9.64 us
    unnamed x30, local copies, waits for them, and re-layouts  7.77 us
    pallas_call x2, Pallas kernels, inner_products(): pl.pallas_call(functools.partial(inner_kernel, count), grid_spec=pltpu.Pr...  7.49 us
    pallas_call x1, Pallas kernels, local(): pl.pallas_call(top_kernel, in_specs=[VMEM, pl.BlockSpec(memory_space=pl.A...  6.13 us
  transfers between devices with their start and end apart: 27, of which 8 were waited for; matrix products, arithmetic and copies ran while one was open for 11% of the time, Pallas kernels for 31%

profile of v2, /device:TPU:1, one launch (start us, length us, event | category | flops | bytes accessed | tf_op | source)
XLA Modules:
  0.0 138.0 jit_solution(11361691653720360787)
XLA Ops:
  0.6 0.0 copy-start
  0.7 1.0 copy-done
  1.7 1.9 %convolution_bitcast_fusion = f32[8,64,64]{2,1,0:T(8,128)S(1)} fusion(f32[8,64,256]{2,1,0:T(8,128)} %param.10, f32[64,2048]{1,0:T(8,128)S(1)} %copy-done, s32[]{:T(128)S(6)} %select_n.29), kind=kOutput, calls=%fused_computation | convolution fusion | flops 100663296 | bytes 720900 | tf_op jit(solution)/shard_map/rb,jkb->jrk/dot_general | solution.py:372
  3.6 2.1 %collective-permute-start.3 = (f32[8,64,64]{2,1,0:T(8,128)S(1)}, f32[8,64,64]{2,1,0:T(8,128)S(1)}, u32[]{:S(2)}, u32[]{:S(2)}) collective-permute-start(f32[8,64,64]{2,1,0:T(8,128)S(1)} %convolution_bitcast_fusion), channel_id=1, source_target_pairs={{0,4},{4,0},{8,12},{12,8},{16,20},{20,16},{24,28},{28,24},{1,5},{5... | collective-permute-start | bytes 393224 | tf_op jit(solution)/shard_map/ppermute | solution.py:313
  5.7 1.3 collective-permute-start
  7.0 0.7 collective-permute-start.1
  7.7 0.3 collective-permute-start.2
  8.0 3.8 %collective-permute-done.3 = f32[8,64,64]{2,1,0:T(8,128)S(1)} collective-permute-done((f32[8,64,64]{2,1,0:T(8,128)S(1)}, f32[8,64,64]{2,1,0:T(8,128)S(1)}, u32[]{:S(2)}, u32[]{:S(2)}) %collective-permute-start.3) | collective-permute-done | bytes 131104 | tf_op jit(solution)/shard_map/ppermute | solution.py:313
  11.8 1.3 collective-permute-start.4
  13.1 9.4 %fusion.7.products = f32[512,512]{1,0:T(8,128)S(1)} fusion(f32[512,2048]{1,0:T(8,128)} %bitcast.32), kind=kOutput, calls=%fused_computation.13 | convolution fusion | flops 6442450944 | bytes 5242880 | tf_op jit(solution)/shard_map/dot_general | solution.py:20
  22.5 1.7 %collective-permute-done.4 = f32[8,64,64]{2,1,0:T(8,128)} collective-permute-done((f32[8,64,64]{2,1,0:T(8,128)S(1)}, f32[8,64,64]{2,1,0:T(8,128)}, u32[]{:S(2)}, u32[]{:S(2)}) %collective-permute-start.4) | collective-permute-done | bytes 131104 | tf_op jit(solution)/shard_map/ppermute | solution.py:313
  24.1 1.1 add.22
  25.2 1.5 %collective-permute-start.6 = (f32[8,64,256]{2,1,0:T(8,128)S(1)}, f32[8,64,256]{2,1,0:T(8,128)}, u32[]{:S(2)}, u32[]{:S(2)}) collective-permute-start(f32[8,64,256]{2,1,0:T(8,128)S(1)} %collective-permute-done.refs_10_), channel_id=1, source_target_pairs={{8,16},{12,20},{16,8},{20,12},{9,17},{13,21},{17,9},{21,13},{10,18... | collective-permute-start | bytes 1572872 | tf_op jit(solution)/shard_map/ppermute | solution.py:313
  26.7 0.4 collective-permute-start.7
  27.1 1.3 collective-permute-start.5
  28.4 0.9 broadcast_select_fusion.1
  29.3 3.1 %collective-permute-start.8 = (f32[8,64,256]{2,1,0:T(8,128)}, f32[8,64,256]{2,1,0:T(8,128)}, u32[]{:S(2)}, u32[]{:S(2)}) collective-permute-start(f32[8,64,256]{2,1,0:T(8,128)} %broadcast_select_fusion.1), channel_id=1, source_target_pairs={{0,24},{4,28},{8,12},{12,8},{16,20},{20,16},{24,0},{28,4},{1,25},{... | collective-permute-start | bytes 1572872 | tf_op jit(solution)/shard_map/ppermute | solution.py:340
  32.5 0.1 pad.6.clone
  32.5 0.3 fusion
  32.8 1.6 %maximum_maximum_fusion = f32[64,640]{1,0:T(8,128)} fusion(f32[64,64]{1,0:T(8,128)S(1)} %fusion, f32[64,512]{1,0:T(8,128)} %bitcast.36, f32[640]{0:T(1024)S(1)} %pad.6.clone), kind=kLoop, calls=%fused_computation.4 | loop fusion | flops 81920 | bytes 313856 | tf_op jit(solution)/shard_map/concatenate | solution.py:378
  34.4 19.1 %collective-permute-done.5 = f32[8,64,256]{2,1,0:T(8,128)} collective-permute-done((f32[8,64,256]{2,1,0:T(8,128)S(1)}, f32[8,64,256]{2,1,0:T(8,128)}, u32[]{:S(2)}, u32[]{:S(2)}) %collective-permute-start.5) | collective-permute-done | bytes 524320 | tf_op jit(solution)/shard_map/ppermute | solution.py:334
  53.5 1.1 broadcast_select_fusion.refs_12_
  54.6 1.4 %collective-permute-start.11 = (f32[8,64,256]{2,1,0:T(8,128)S(1)}, f32[8,64,256]{2,1,0:T(8,128)}, u32[]{:S(2)}, u32[]{:S(2)}) collective-permute-start(f32[8,64,256]{2,1,0:T(8,128)S(1)} %broadcast_select_fusion.refs_12_), channel_id=1, source_target_pairs={{0,4},{4,0},{8,12},{12,8},{16,20},{20,16},{24,28},{28,24},{1,5},{5... | collective-permute-start | bytes 1572872 | tf_op jit(solution)/shard_map/ppermute | solution.py:313
  56.0 1.5 %collective-permute-start.12 = (f32[8,64,256]{2,1,0:T(8,128)}, f32[8,64,256]{2,1,0:T(8,128)}, u32[]{:S(2)}, u32[]{:S(2)}) collective-permute-start(f32[8,64,256]{2,1,0:T(8,128)} %collective-permute-done.6), channel_id=1, source_target_pairs={{8,0},{12,4},{16,24},{20,28},{9,1},{13,5},{17,25},{21,29},{10,2},{... | collective-permute-start | bytes 1572872 | tf_op jit(solution)/shard_map/ppermute | solution.py:347
  57.5 1.3 collective-permute-start.10
  58.8 2.8 %collective-permute-start.9 = (f32[8,64,64]{2,1,0:T(8,128)S(1)}, f32[8,64,64]{2,1,0:T(8,128)}, u32[]{:S(2)}, u32[]{:S(2)}) collective-permute-start(f32[8,64,64]{2,1,0:T(8,128)S(1)} %add.22), channel_id=1, source_target_pairs={{0,16},{4,20},{8,24},{12,28},{16,0},{20,4},{24,8},{28,12},{1,17},{... | collective-permute-start | bytes 393224 | tf_op jit(solution)/shard_map/ppermute | solution.py:313
  61.6 0.1 stack.65.refs_0_
  61.7 2.2 %copy-done.1 = f32[1,8,64,2048]{3,2,1,0:T(8,128)S(1)} copy-done((f32[1,8,64,2048]{3,2,1,0:T(8,128)S(1)}, f32[1,8,64,2048]{3,2,1,0:T(8,128)}, u32[]{:S(2)}) %copy-start.1) | copy-done | bytes 4194328
  63.9 1.0 copy-done.5
  64.9 1.0 copy-done.7
  66.0 4.4 %shard_map.95.refs_5_ = f32[8,64,64]{2,1,0:T(8,128)S(1)} custom-call(s32[7]{0:T(128)S(1)} %stack.65.refs_0_, f32[1,8,64,2048]{3,2,1,0:T(8,128)S(1)} %copy-done.1, f32[1,8,64,2048]{3,2,1,0:T(8,128)S(1)} %copy-done.1, f32[1,8,64,2048]{3,2,1,0:T(8,128)S(1)} %copy-done.1, f32[1,8,64,2048]{3,2,1,0:T(8,128)S(1)} %copy-done.1, f32[1,8,64,2048]{3,2,1,0:T(8,128)S(1)} %copy-done.1, ...), custom_call_target="tpu_custom_call" | custom-call | flops 100000000 | bytes 1000000 | tf_op jit(solution)/shard_map/pallas_call | solution.py:148
  70.4 1.9 %collective-permute-done.9 = f32[8,64,64]{2,1,0:T(8,128)} collective-permute-done((f32[8,64,64]{2,1,0:T(8,128)S(1)}, f32[8,64,64]{2,1,0:T(8,128)}, u32[]{:S(2)}, u32[]{:S(2)}) %collective-permute-start.9) | collective-permute-done | bytes 131104 | tf_op jit(solution)/shard_map/ppermute | solution.py:313
  72.2 1.0 add.24.sketched
  73.2 1.0 pad_maximum_fusion.tiles
  74.3 1.4 collective-permute-done.12.refs_4_
  75.7 0.1 collective-permute-start.16
  75.7 0.1 pad_add_fusion.refs_0_
  75.8 3.1 %shard_map.97.inner = f32[8,64,64]{2,1,0:T(8,128)S(1)} custom-call(s32[2]{0:T(128)S(1)} %pad_add_fusion.refs_0_, f32[1,8,64,2048]{3,2,1,0:T(8,128)S(1)} %copy-done.2, f32[1,8,64,2048]{3,2,1,0:T(8,128)S(1)} %copy-done.2, f32[8,64,256]{2,1,0:T(8,128)} %collective-permute-done.11.refs_3_, f32[8,64,256]{2,1,0:T(8,128)} %collective-permute-done.12.refs_4_, ...), custom_call_target="tpu_custom_call" | custom-call | flops 100000000 | bytes 1000000 | tf_op jit(solution)/shard_map/pallas_call | solution.py:148
  78.9 11.9 %shard_map.98 = (f32[64,512]{1,0:T(8,128)S(1)}, f32[64,576]{1,0:T(8,128)S(1)}) custom-call(s32[1,8]{1,0:T(1,128)S(1)} %copy-done.13, f32[8,64,64]{2,1,0:T(8,128)S(1)} %add.24.sketched, f32[8,64,64]{2,1,0:T(8,128)S(1)} %shard_map.97.inner, f32[512,512]{1,0:T(8,128)S(1)} %fusion.7.products), custom_call_target="tpu_custom_call" | custom-call | flops 100000000 | bytes 1000000 | tf_op jit(solution)/shard_map/pallas_call | solution.py:300
  90.9 0.1 collective-permute-start.13
  90.9 1.7 %collective-permute-start.14 = (f32[64,512]{1,0:T(8,128)S(1)}, f32[64,512]{1,0:T(8,128)S(1)}, u32[]{:S(2)}, u32[]{:S(2)}) collective-permute-start(f32[64,512]{1,0:T(8,128)S(1)} %get-tuple-element.81.refs_0_), channel_id=1, source_target_pairs={{0,8},{4,12},{8,0},{12,4},{16,24},{20,28},{24,16},{28,20},{1,9},{5... | collective-permute-start | bytes 393224 | tf_op jit(solution)/shard_map/ppermute | solution.py:313
  92.6 1.0 collective-permute-start.15
  93.6 6.1 %shard_map.99 = (f32[64,2048]{1,0:T(8,128)S(1)}, f32[64,2048]{1,0:T(8,128)S(1)}, f32[64,128]{1,0:T(8,128)S(1)}) custom-call(f32[64,576]{1,0:T(8,128)S(1)} %get-tuple-element.73.whole, f32[512,2048]{1,0:T(8,128)S(1)} %bitcast.33), custom_call_target="tpu_custom_call" | custom-call | flops 100000000 | bytes 1000000 | tf_op jit(solution)/shard_map/pallas_call | solution.py:407
  99.7 3.8 %collective-permute-done.14.refs_2_ = f32[64,512]{1,0:T(8,128)S(1)} collective-permute-done((f32[64,512]{1,0:T(8,128)S(1)}, f32[64,512]{1,0:T(8,128)S(1)}, u32[]{:S(2)}, u32[]{:S(2)}) %collective-permute-start.14) | collective-permute-done | bytes 131104 | tf_op jit(solution)/shard_map/ppermute | solution.py:313
  103.5 2.6 %collective-permute-done.15.refs_3_ = f32[64,512]{1,0:T(8,128)S(1)} collective-permute-done((f32[64,512]{1,0:T(8,128)S(1)}, f32[64,512]{1,0:T(8,128)S(1)}, u32[]{:S(2)}, u32[]{:S(2)}) %collective-permute-start.15) | collective-permute-done | bytes 131104 | tf_op jit(solution)/shard_map/ppermute | solution.py:313
  106.1 0.5 collective-permute-start.17
  106.6 2.3 %collective-permute-start.19 = (f32[64,2048]{1,0:T(8,128)S(1)}, f32[64,2048]{1,0:T(8,128)S(1)}, u32[]{:S(2)}, u32[]{:S(2)}) collective-permute-start(f32[64,2048]{1,0:T(8,128)S(1)} %get-tuple-element.75.own), channel_id=1, source_target_pairs={{0,2},{1,3},{2,0},{3,1},{4,6},{5,7},{6,4},{7,5},{8,10},{9,11},{10,... | collective-permute-start | bytes 1572872 | tf_op jit(solution)/shard_map/ppermute | solution.py:313
  108.9 0.3 collective-permute-start.18
  109.2 1.7 %shard_map.101 = (f32[64,512]{1,0:T(8,128)S(1)}, f32[64,512]{1,0:T(8,128)}, f32[64,512]{1,0:T(8,128)}, f32[64,512]{1,0:T(8,128)}) custom-call(f32[64,512]{1,0:T(8,128)S(1)} %get-tuple-element.81.refs_0_, f32[64,512]{1,0:T(8,128)S(1)} %collective-permute-done.13.refs_1_, f32[64,512]{1,0:T(8,128)S(1)} %collective-permute-done.14.refs_2_, ...), custom_call_target="tpu_custom_call" | custom-call | flops 100000000 | bytes 1000000 | tf_op jit(solution)/shard_map/pallas_call | solution.py:300
  111.0 1.2 collective-permute-start.20
  112.2 0.7 copy-done.9
  112.9 1.4 %collective-permute-start.22 = (f32[64,512]{1,0:T(8,128)}, f32[64,512]{1,0:T(8,128)}, u32[]{:S(2)}, u32[]{:S(2)}) collective-permute-start(f32[64,512]{1,0:T(8,128)} %get-tuple-element.90), channel_id=1, source_target_pairs={{0,12},{4,8},{8,4},{12,0},{16,28},{20,24},{24,20},{28,16},{1,13},{... | collective-permute-start | bytes 393224 | tf_op jit(solution)/shard_map/ppermute | solution.py:313
  114.3 0.1 stack.76.spots
  114.4 1.0 copy-done.10
  115.4 0.8 copy-done.12
  116.2 2.1 %shard_map.100 = (f32[64,64]{1,0:T(8,128)S(1)}, f32[64,2048]{1,0:T(8,128)S(1)}, f32[64,2048]{1,0:T(8,128)S(1)}, f32[64,64]{1,0:T(8,128)S(1)}, f32[128,128]{1,0:T(8,128)S(1)}) custom-call(s32[1]{0:T(128)} %bitcast.place.chunk, f32[64,2048]{1,0:T(8,128)S(1)} %get-tuple-element.75.own, f32[64,2048]{1,0:T(8,128)S(1)} %collective-permute-done.17.partner, ...), custom_call_target="tpu_custom_call" | custom-call | flops 100000000 | bytes 1000000 | tf_op jit(solution)/shard_map/pallas_call | solution.py:300
  118.2 1.6 %collective-permute-done.22.near_side = f32[64,512]{1,0:T(8,128)} collective-permute-done((f32[64,512]{1,0:T(8,128)}, f32[64,512]{1,0:T(8,128)}, u32[]{:S(2)}, u32[]{:S(2)}) %collective-permute-start.22) | collective-permute-done | bytes 131104 | tf_op jit(solution)/shard_map/ppermute | solution.py:313
  119.8 1.5 %shard_map.102 = (f32[64,512]{1,0:T(8,128)S(1)}, f32[64,512]{1,0:T(8,128)S(1)}, f32[64,512]{1,0:T(8,128)S(1)}, f32[64,512]{1,0:T(8,128)S(1)}) custom-call(s32[5]{0:T(128)S(1)} %stack.76.spots, f32[64,64]{1,0:T(8,128)S(1)} %get-tuple-element.80.step, f32[64,512]{1,0:T(8,128)S(1)} %get-tuple-element.87.own, f32[64,512]{1,0:T(8,128)S(1)} %collective-permute-done.20.side, ...), custom_call_target="tpu_custom_call" | custom-call | flops 100000000 | bytes 1000000 | tf_op jit(solution)/shard_map/pallas_call | solution.py:300
  121.4 1.4 %collective-permute-start.23 = (f32[64,2048]{1,0:T(8,128)S(1)}, f32[64,2048]{1,0:T(8,128)S(1)}, u32[]{:S(2)}, u32[]{:S(2)}) collective-permute-start(f32[64,2048]{1,0:T(8,128)S(1)} %collective-permute-done.19.far), channel_id=1, source_target_pairs={{0,1},{1,0},{2,3},{3,2},{4,5},{5,4},{6,7},{7,6},{8,9},{9,8},{10,11... | collective-permute-start | bytes 1572872 | tf_op jit(solution)/shard_map/ppermute | solution.py:313
  122.8 0.1 collective-permute-start.24
  122.9 0.4 collective-permute-start.25
  123.3 1.7 %collective-permute-start.26 = (f32[64,512]{1,0:T(8,128)S(1)}, f32[64,512]{1,0:T(8,128)S(1)}, u32[]{:S(2)}, u32[]{:S(2)}) collective-permute-start(f32[64,512]{1,0:T(8,128)S(1)} %get-tuple-element.101), channel_id=1, source_target_pairs={{0,3},{1,2},{2,1},{3,0},{4,7},{5,6},{6,5},{7,4},{8,11},{9,10},{10,... | collective-permute-start | bytes 393224 | tf_op jit(solution)/shard_map/ppermute | solution.py:313
  124.9 12.0 %shard_map.103 = (f32[64,512]{1,0:T(8,128)}, f32[64,192]{1,0:T(8,128)S(1)}) custom-call(s32[1]{0:T(128)} %bitcast.place.chunk, f32[64,2048]{1,0:T(8,128)S(1)} %get-tuple-element.79.near, f32[64,2048]{1,0:T(8,128)S(1)} %collective-permute-done.19.far, f32[64,2048]{1,0:T(8,128)S(1)} %collective-permute-done.23.far_core, ...), custom_call_target="tpu_custom_call" | custom-call | flops 100000000 | bytes 1000000 | tf_op jit(solution)/shard_map/pallas_call | solution.py:300
  137.0 1.0 shard_map.104
  (45 shorter events, 0.2 us)
Async XLA Ops:
  0.6 1.0 copy-start
  3.6 8.2 %collective-permute-start.3 = (f32[8,64,64]{2,1,0:T(8,128)S(1)}, f32[8,64,64]{2,1,0:T(8,128)S(1)}, u32[]{:S(2)}, u32[]{:S(2)}) collective-permute-start(f32[8,64,64]{2,1,0:T(8,128)S(1)} %convolution_bitcast_fusion), channel_id=1, source_target_pairs={{0,4},{4,0},{8,12},{12,8},{16,20},{20,16},{24,28},{28,24},{1,5},{5... | collective-permute-start | bytes 393224 | tf_op jit(solution)/shard_map/ppermute | solution.py:313
  5.7 19.5 %collective-permute-start = (f32[8,64,256]{2,1,0:T(8,128)}, f32[8,64,256]{2,1,0:T(8,128)S(1)}, u32[]{:S(2)}, u32[]{:S(2)}) collective-permute-start(f32[8,64,256]{2,1,0:T(8,128)} %refs_8_.1), channel_id=1, source_target_pairs={{0,8},{4,12},{8,0},{12,4},{16,24},{20,28},{24,16},{28,20},{1,9},{5... | collective-permute-start | bytes 1572872 | tf_op jit(solution)/shard_map/ppermute | solution.py:313
  7.0 18.2 %collective-permute-start.1 = (f32[8,64,256]{2,1,0:T(8,128)}, f32[8,64,256]{2,1,0:T(8,128)S(1)}, u32[]{:S(2)}, u32[]{:S(2)}) collective-permute-start(f32[8,64,256]{2,1,0:T(8,128)} %refs_8_.1), channel_id=1, source_target_pairs={{8,16},{12,20},{16,8},{20,12},{9,17},{13,21},{17,9},{21,13},{10,18... | collective-permute-start | bytes 1572872 | tf_op jit(solution)/shard_map/ppermute | solution.py:313
  7.7 17.5 %collective-permute-start.2 = (f32[8,64,256]{2,1,0:T(8,128)}, f32[8,64,256]{2,1,0:T(8,128)S(1)}, u32[]{:S(2)}, u32[]{:S(2)}) collective-permute-start(f32[8,64,256]{2,1,0:T(8,128)} %refs_8_.1), channel_id=1, source_target_pairs={{0,4},{4,0},{8,12},{12,8},{16,20},{20,16},{24,28},{28,24},{1,5},{5... | collective-permute-start | bytes 1572872 | tf_op jit(solution)/shard_map/ppermute | solution.py:313
  11.8 10.7 %copy-start.14 = (f32[8,64,64]{2,1,0:T(8,128)}, f32[8,64,64]{2,1,0:T(8,128)S(1)}, u32[]{:S(2)}) copy-start(f32[8,64,64]{2,1,0:T(8,128)S(1)} %add.21) | copy-start | bytes 393220
  11.8 12.3 %collective-permute-start.4 = (f32[8,64,64]{2,1,0:T(8,128)S(1)}, f32[8,64,64]{2,1,0:T(8,128)}, u32[]{:S(2)}, u32[]{:S(2)}) collective-permute-start(f32[8,64,64]{2,1,0:T(8,128)S(1)} %add.21), channel_id=1, source_target_pairs={{0,8},{4,12},{8,0},{12,4},{16,24},{20,28},{24,16},{28,20},{1,9},{5... | collective-permute-start | bytes 393224 | tf_op jit(solution)/shard_map/ppermute | solution.py:313
  13.1 19.5 %copy-start.8 = (f32[1,64,512]{2,1,0:T(8,128)S(1)}, f32[1,64,512]{2,1,0:T(8,128)}, u32[]{:S(2)}) copy-start(f32[1,64,512]{2,1,0:T(8,128)} %param.14) | copy-start | bytes 393220
  25.2 28.2 %copy-start.6 = (f32[8,64,256]{2,1,0:T(8,128)}, f32[8,64,256]{2,1,0:T(8,128)S(1)}, u32[]{:S(2)}) copy-start(f32[8,64,256]{2,1,0:T(8,128)S(1)} %collective-permute-done.refs_10_) | copy-start | bytes 1572868
  25.2 28.2 %collective-permute-start.6 = (f32[8,64,256]{2,1,0:T(8,128)S(1)}, f32[8,64,256]{2,1,0:T(8,128)}, u32[]{:S(2)}, u32[]{:S(2)}) collective-permute-start(f32[8,64,256]{2,1,0:T(8,128)S(1)} %collective-permute-done.refs_10_), channel_id=1, source_target_pairs={{8,16},{12,20},{16,8},{20,12},{9,17},{13,21},{17,9},{21,13},{10,18... | collective-permute-start | bytes 1572872 | tf_op jit(solution)/shard_map/ppermute | solution.py:313
  26.7 26.7 %collective-permute-start.7 = (f32[8,64,256]{2,1,0:T(8,128)S(1)}, f32[8,64,256]{2,1,0:T(8,128)}, u32[]{:S(2)}, u32[]{:S(2)}) collective-permute-start(f32[8,64,256]{2,1,0:T(8,128)S(1)} %collective-permute-done.refs_10_), channel_id=1, source_target_pairs={{0,4},{4,0},{8,12},{12,8},{16,20},{20,16},{24,28},{28,24},{1,5},{5... | collective-permute-start | bytes 1572872 | tf_op jit(solution)/shard_map/ppermute | solution.py:313
  27.1 26.3 %collective-permute-start.5 = (f32[8,64,256]{2,1,0:T(8,128)S(1)}, f32[8,64,256]{2,1,0:T(8,128)}, u32[]{:S(2)}, u32[]{:S(2)}) collective-permute-start(f32[8,64,256]{2,1,0:T(8,128)S(1)} %collective-permute-done.1.refs_14_), channel_id=1, source_target_pairs={{8,0},{12,4},{16,24},{20,28},{9,1},{13,5},{17,25},{21,29},{10,2},{... | collective-permute-start | bytes 1572872 | tf_op jit(solution)/shard_map/ppermute | solution.py:334
  29.3 24.2 %collective-permute-start.8 = (f32[8,64,256]{2,1,0:T(8,128)}, f32[8,64,256]{2,1,0:T(8,128)}, u32[]{:S(2)}, u32[]{:S(2)}) collective-permute-start(f32[8,64,256]{2,1,0:T(8,128)} %broadcast_select_fusion.1), channel_id=1, source_target_pairs={{0,24},{4,28},{8,12},{12,8},{16,20},{20,16},{24,0},{28,4},{1,25},{... | collective-permute-start | bytes 1572872 | tf_op jit(solution)/shard_map/ppermute | solution.py:340
  54.6 19.7 %collective-permute-start.11 = (f32[8,64,256]{2,1,0:T(8,128)S(1)}, f32[8,64,256]{2,1,0:T(8,128)}, u32[]{:S(2)}, u32[]{:S(2)}) collective-permute-start(f32[8,64,256]{2,1,0:T(8,128)S(1)} %broadcast_select_fusion.refs_12_), channel_id=1, source_target_pairs={{0,4},{4,0},{8,12},{12,8},{16,20},{20,16},{24,28},{28,24},{1,5},{5... | collective-permute-start | bytes 1572872 | tf_op jit(solution)/shard_map/ppermute | solution.py:313
  56.0 19.6 %collective-permute-start.12 = (f32[8,64,256]{2,1,0:T(8,128)}, f32[8,64,256]{2,1,0:T(8,128)}, u32[]{:S(2)}, u32[]{:S(2)}) collective-permute-start(f32[8,64,256]{2,1,0:T(8,128)} %collective-permute-done.6), channel_id=1, source_target_pairs={{8,0},{12,4},{16,24},{20,28},{9,1},{13,5},{17,25},{21,29},{10,2},{... | collective-permute-start | bytes 1572872 | tf_op jit(solution)/shard_map/ppermute | solution.py:347
  57.5 15.7 %collective-permute-start.10 = (f32[64,640]{1,0:T(8,128)}, f32[64,640]{1,0:T(8,128)}, u32[]{:S(2)}, u32[]{:S(2)}) collective-permute-start(f32[64,640]{1,0:T(8,128)} %maximum_maximum_fusion), channel_id=1, source_target_pairs={{0,2},{1,3},{2,0},{3,1},{4,6},{5,7},{6,4},{7,5},{8,10},{9,11},{10,... | collective-permute-start | bytes 491528 | tf_op jit(solution)/shard_map/ppermute | solution.py:313
  58.8 13.5 %collective-permute-start.9 = (f32[8,64,64]{2,1,0:T(8,128)S(1)}, f32[8,64,64]{2,1,0:T(8,128)}, u32[]{:S(2)}, u32[]{:S(2)}) collective-permute-start(f32[8,64,64]{2,1,0:T(8,128)S(1)} %add.22), channel_id=1, source_target_pairs={{0,16},{4,20},{8,24},{12,28},{16,0},{20,4},{24,8},{28,12},{1,17},{... | collective-permute-start | bytes 393224 | tf_op jit(solution)/shard_map/ppermute | solution.py:313
  61.7 2.2 %copy-start.1 = (f32[1,8,64,2048]{3,2,1,0:T(8,128)S(1)}, f32[1,8,64,2048]{3,2,1,0:T(8,128)}, u32[]{:S(2)}) copy-start(f32[1,8,64,2048]{3,2,1,0:T(8,128)} %refs_2_.3) | copy-start | bytes 12582916
  63.9 1.0 copy-start.5
  64.9 1.0 copy-start.7
  66.0 9.7 %copy-start.4 = (f32[8,64,256]{2,1,0:T(8,128)S(1)}, f32[8,64,256]{2,1,0:T(8,128)}, u32[]{:S(2)}) copy-start(f32[8,64,256]{2,1,0:T(8,128)} %param.10) | copy-start | bytes 1572868
  66.0 9.9 %copy-start.2 = (f32[1,8,64,2048]{3,2,1,0:T(8,128)S(1)}, f32[1,8,64,2048]{3,2,1,0:T(8,128)}, u32[]{:S(2)}) copy-start(f32[1,8,64,2048]{3,2,1,0:T(8,128)} %refs_2_.3) | copy-start | bytes 12582916
  75.7 30.4 %collective-permute-start.16 = (f32[512,256]{1,0:T(8,128)S(1)}, f32[512,256]{1,0:T(8,128)S(1)}, u32[]{:S(2)}, u32[]{:S(2)}) collective-permute-start(f32[512,256]{1,0:T(8,128)S(1)} %shard_map.96.refs_4_), channel_id=1, source_target_pairs={{0,16},{4,20},{8,24},{12,28},{16,0},{20,4},{24,8},{28,12},{1,17},{... | collective-permute-start | bytes 1572872 | tf_op jit(solution)/shard_map/ppermute | solution.py:313
  75.8 3.1 %copy-start.13 = (s32[1,8]{1,0:T(1,128)S(1)}, s32[1,8]{1,0:T(1,128)}, u32[]{:S(2)}) copy-start(s32[1,8]{1,0:T(1,128)} %weights.1) | copy-start | bytes 100
  75.8 17.7 %copy-start.3 = (f32[1,8,64,2048]{3,2,1,0:T(8,128)S(1)}, f32[1,8,64,2048]{3,2,1,0:T(8,128)}, u32[]{:S(2)}) copy-start(f32[1,8,64,2048]{3,2,1,0:T(8,128)} %param.8) | copy-start | bytes 12582916
  90.9 8.9 %collective-permute-start.13 = (f32[64,512]{1,0:T(8,128)S(1)}, f32[64,512]{1,0:T(8,128)S(1)}, u32[]{:S(2)}, u32[]{:S(2)}) collective-permute-start(f32[64,512]{1,0:T(8,128)S(1)} %get-tuple-element.81.refs_0_), channel_id=1, source_target_pairs={{0,4},{4,0},{8,12},{12,8},{16,20},{20,16},{24,28},{28,24},{1,5},{5... | collective-permute-start | bytes 393224 | tf_op jit(solution)/shard_map/ppermute | solution.py:313
  90.9 12.6 %collective-permute-start.14 = (f32[64,512]{1,0:T(8,128)S(1)}, f32[64,512]{1,0:T(8,128)S(1)}, u32[]{:S(2)}, u32[]{:S(2)}) collective-permute-start(f32[64,512]{1,0:T(8,128)S(1)} %get-tuple-element.81.refs_0_), channel_id=1, source_target_pairs={{0,8},{4,12},{8,0},{12,4},{16,24},{20,28},{24,16},{28,20},{1,9},{5... | collective-permute-start | bytes 393224 | tf_op jit(solution)/shard_map/ppermute | solution.py:313
  92.6 13.5 %collective-permute-start.15 = (f32[64,512]{1,0:T(8,128)S(1)}, f32[64,512]{1,0:T(8,128)S(1)}, u32[]{:S(2)}, u32[]{:S(2)}) collective-permute-start(f32[64,512]{1,0:T(8,128)S(1)} %get-tuple-element.81.refs_0_), channel_id=1, source_target_pairs={{0,12},{4,8},{8,4},{12,0},{16,28},{20,24},{24,20},{28,16},{1,13},{... | collective-permute-start | bytes 393224 | tf_op jit(solution)/shard_map/ppermute | solution.py:313
  99.7 12.5 %copy-start.11 = (f32[64,128]{1,0:T(8,128)}, f32[64,128]{1,0:T(8,128)S(1)}, u32[]{:S(2)}) copy-start(f32[64,128]{1,0:T(8,128)S(1)} %get-tuple-element.77.squares) | copy-start | bytes 98308
  106.1 8.3 %collective-permute-start.17 = (f32[64,2048]{1,0:T(8,128)S(1)}, f32[64,2048]{1,0:T(8,128)S(1)}, u32[]{:S(2)}, u32[]{:S(2)}) collective-permute-start(f32[64,2048]{1,0:T(8,128)S(1)} %get-tuple-element.75.own), channel_id=1, source_target_pairs={{0,1},{1,0},{2,3},{3,2},{4,5},{5,4},{6,7},{7,6},{8,9},{9,8},{10,11... | collective-permute-start | bytes 1572872 | tf_op jit(solution)/shard_map/ppermute | solution.py:313
  106.6 14.8 %collective-permute-start.19 = (f32[64,2048]{1,0:T(8,128)S(1)}, f32[64,2048]{1,0:T(8,128)S(1)}, u32[]{:S(2)}, u32[]{:S(2)}) collective-permute-start(f32[64,2048]{1,0:T(8,128)S(1)} %get-tuple-element.75.own), channel_id=1, source_target_pairs={{0,2},{1,3},{2,0},{3,1},{4,6},{5,7},{6,4},{7,5},{8,10},{9,11},{10,... | collective-permute-start | bytes 1572872 | tf_op jit(solution)/shard_map/ppermute | solution.py:313
  108.9 3.3 %collective-permute-start.18 = (f32[2,64,640]{2,1,0:T(8,128)S(1)}, f32[2,64,640]{2,1,0:T(8,128)S(1)}, u32[]{:S(2)}, u32[]{:S(2)}) collective-permute-start(f32[2,64,640]{2,1,0:T(8,128)S(1)} %pad_maximum_fusion.tiles), channel_id=1, source_target_pairs={{0,1},{1,0},{2,3},{3,2},{4,5},{5,4},{6,7},{7,6},{8,9},{9,8},{10,11... | collective-permute-start | bytes 983048 | tf_op jit(solution)/shard_map/ppermute | solution.py:313
  111.0 7.3 %collective-permute-start.20 = (f32[64,512]{1,0:T(8,128)}, f32[64,512]{1,0:T(8,128)S(1)}, u32[]{:S(2)}, u32[]{:S(2)}) collective-permute-start(f32[64,512]{1,0:T(8,128)} %get-tuple-element.88), channel_id=1, source_target_pairs={{0,4},{4,0},{8,12},{12,8},{16,20},{20,16},{24,28},{28,24},{1,5},{5... | collective-permute-start | bytes 393224 | tf_op jit(solution)/shard_map/ppermute | solution.py:313
  112.2 6.0 %collective-permute-start.21 = (f32[64,512]{1,0:T(8,128)}, f32[64,512]{1,0:T(8,128)S(1)}, u32[]{:S(2)}, u32[]{:S(2)}) collective-permute-start(f32[64,512]{1,0:T(8,128)} %get-tuple-element.89), channel_id=1, source_target_pairs={{0,8},{4,12},{8,0},{12,4},{16,24},{20,28},{24,16},{28,20},{1,9},{5... | collective-permute-start | bytes 393224 | tf_op jit(solution)/shard_map/ppermute | solution.py:313
  112.2 0.7 copy-start.9
  112.9 6.9 %collective-permute-start.22 = (f32[64,512]{1,0:T(8,128)}, f32[64,512]{1,0:T(8,128)}, u32[]{:S(2)}, u32[]{:S(2)}) collective-permute-start(f32[64,512]{1,0:T(8,128)} %get-tuple-element.90), channel_id=1, source_target_pairs={{0,12},{4,8},{8,4},{12,0},{16,28},{20,24},{24,20},{28,16},{1,13},{... | collective-permute-start | bytes 393224 | tf_op jit(solution)/shard_map/ppermute | solution.py:313
  114.4 1.0 copy-start.10
  115.4 0.8 copy-start.12
  121.4 3.6 %collective-permute-start.23 = (f32[64,2048]{1,0:T(8,128)S(1)}, f32[64,2048]{1,0:T(8,128)S(1)}, u32[]{:S(2)}, u32[]{:S(2)}) collective-permute-start(f32[64,2048]{1,0:T(8,128)S(1)} %collective-permute-done.19.far), channel_id=1, source_target_pairs={{0,1},{1,0},{2,3},{3,2},{4,5},{5,4},{6,7},{7,6},{8,9},{9,8},{10,11... | collective-permute-start | bytes 1572872 | tf_op jit(solution)/shard_map/ppermute | solution.py:313
  122.8 14.2 %collective-permute-start.24 = (f32[64,512]{1,0:T(8,128)S(1)}, f32[64,512]{1,0:T(8,128)S(1)}, u32[]{:S(2)}, u32[]{:S(2)}) collective-permute-start(f32[64,512]{1,0:T(8,128)S(1)} %get-tuple-element.99), channel_id=1, source_target_pairs={{0,1},{1,0},{2,3},{3,2},{4,5},{5,4},{6,7},{7,6},{8,9},{9,8},{10,11... | collective-permute-start | bytes 393224 | tf_op jit(solution)/shard_map/ppermute | solution.py:313
  122.9 14.1 %collective-permute-start.25 = (f32[64,512]{1,0:T(8,128)S(1)}, f32[64,512]{1,0:T(8,128)S(1)}, u32[]{:S(2)}, u32[]{:S(2)}) collective-permute-start(f32[64,512]{1,0:T(8,128)S(1)} %get-tuple-element.100), channel_id=1, source_target_pairs={{0,2},{1,3},{2,0},{3,1},{4,6},{5,7},{6,4},{7,5},{8,10},{9,11},{10,... | collective-permute-start | bytes 393224 | tf_op jit(solution)/shard_map/ppermute | solution.py:313
  123.3 13.7 %collective-permute-start.26 = (f32[64,512]{1,0:T(8,128)S(1)}, f32[64,512]{1,0:T(8,128)S(1)}, u32[]{:S(2)}, u32[]{:S(2)}) collective-permute-start(f32[64,512]{1,0:T(8,128)S(1)} %get-tuple-element.101), channel_id=1, source_target_pairs={{0,3},{1,2},{2,1},{3,0},{4,7},{5,6},{6,5},{7,4},{8,11},{9,10},{10,... | collective-permute-start | bytes 393224 | tf_op jit(solution)/shard_map/ppermute | solution.py:313

commit v3 on v2

--- a/solution.py
+++ b/solution.py
@@ -12,7 +12,7 @@
 VMEM = pl.BlockSpec(memory_space=pltpu.VMEM)
 SMEM = pl.BlockSpec(memory_space=pltpu.SMEM)
 LIMIT = pltpu.CompilerParams(vmem_limit_bytes=12 * 1024 * 1024)
-ROOMY = pltpu.CompilerParams(vmem_limit_bytes=32 * 1024 * 1024)
+ROOMY = pltpu.CompilerParams(vmem_limit_bytes=20 * 1024 * 1024)
 SHORT = pl.CostEstimate(flops=10**8, bytes_accessed=10**6, transcendentals=0)
 
 
@@ -34,13 +34,6 @@
 
 def identity(n):
     return (lax.broadcasted_iota(jnp.int32, (n, n), 0) == lax.broadcasted_iota(jnp.int32, (n, n), 1)).astype(f32)
-
-
-def reciprocal(value):
-    guess = pl.reciprocal(value, approx=True)
-    for _ in range(2):
-        guess = guess * (2.0 - value * guess)
-    return guess
 
 
 def inverse_factors(matrices):
@@ -68,7 +61,7 @@
             done = state[m]
             scaled = []
             for a in range(step):
-                inverse = reciprocal(pivot[a][a])
+                inverse = 1.0 / pivot[a][a]
                 for b in range(a + 1, step):
                     factor = pivot[a][b] * inverse
                     row[b] = row[b] - factor * row[a]
@@ -343,7 +336,6 @@
     )
 
     opposite = jnp.where(is_end, outer, inner)
-    opposite, inner, partial = lax.optimization_barrier((opposite, inner, partial))
     far = lax.ppermute(inner, "rows", outward)
     opposite_side = swap(opposite, "rows", 1)
     partial = partial + swap(partial, "rows", 4)

time: 139 us -> 137 us (0.986)
  Pallas kernels: 44 us -> 40.9 us
  waiting for transfers between devices: 35.7 us -> 37.1 us
    pallas_call x7, Pallas kernels: 30.4 us -> 27.9 us  [call(): pl.pallas_call(kernel, in_specs=[SMEM] * scalars + [VMEM] * (len(operands...]
  transfers between devices with their start and end apart: 27 -> 27, of which waited for: 8 -> 8; matrix products, arithmetic and copies ran while one was open for 11% -> 11% of each run, Pallas kernels for 31% -> 29%
where the time goes in v3:
time: 137 us; the launch traced here: 136 us
  Pallas kernels  40.9 us (30%)
  waiting for transfers between devices  37.1 us (27%)
  starting transfers between devices  31 us (23%)
  matrix products  11.5 us (8%)
  local copies, waits for them, and re-layouts  8.02 us (6%)
  other arithmetic  6.78 us (5%)
    pallas_call x7, Pallas kernels, call(): pl.pallas_call(kernel, in_specs=[SMEM] * scalars + [VMEM] * (len(operands...  27.9 us
    ppermute x24, starting transfers between devices, swap(): return lax.ppermute(value, axis, [(i, i ^ mask) for i in members])  25.1 us
    ppermute x1, waiting for transfers between devices, gather_line(): outer = lax.ppermute(center, 'rows', outward)  19.1 us
    ppermute x24, waiting for transfers between devices, swap(): return lax.ppermute(value, axis, [(i, i ^ mask) for i in members])  16.6 us
    dot_general x2, matrix products, dot(): lax.dot_general(a, b, (dims, ((), ())), precision=highest, preferred_elem...  9.6 us
    unnamed x30, local copies, waits for them, and re-layouts  7.77 us
    pallas_call x2, Pallas kernels, inner_products(): pl.pallas_call(functools.partial(inner_kernel, count), grid_spec=pltpu.Pr...  7.49 us
    pallas_call x1, Pallas kernels, local(): pl.pallas_call(top_kernel, in_specs=[VMEM, pl.BlockSpec(memory_space=pl.A...  5.58 us
  transfers between devices with their start and end apart: 27, of which 8 were waited for; matrix products, arithmetic and copies ran while one was open for 11% of the time, Pallas kernels for 29%

profile of v3, /device:TPU:1, one launch (start us, length us, event | category | flops | bytes accessed | tf_op | source)
XLA Modules:
  0.0 136.2 jit_solution(6973743988748392127)
XLA Ops:
  0.6 0.0 copy-start
  0.7 1.0 copy-done
  1.7 1.9 %convolution_bitcast_fusion = f32[8,64,64]{2,1,0:T(8,128)S(1)} fusion(f32[8,64,256]{2,1,0:T(8,128)} %param.10, f32[64,2048]{1,0:T(8,128)S(1)} %copy-done, s32[]{:T(128)S(6)} %select_n.29), kind=kOutput, calls=%fused_computation | convolution fusion | flops 100663296 | bytes 720900 | tf_op jit(solution)/shard_map/rb,jkb->jrk/dot_general | solution.py:364
  3.6 2.1 %collective-permute-start.3 = (f32[8,64,64]{2,1,0:T(8,128)S(1)}, f32[8,64,64]{2,1,0:T(8,128)S(1)}, u32[]{:S(2)}, u32[]{:S(2)}) collective-permute-start(f32[8,64,64]{2,1,0:T(8,128)S(1)} %convolution_bitcast_fusion), channel_id=1, source_target_pairs={{0,4},{4,0},{8,12},{12,8},{16,20},{20,16},{24,28},{28,24},{1,5},{5... | collective-permute-start | bytes 393224 | tf_op jit(solution)/shard_map/ppermute | solution.py:306
  5.7 1.3 collective-permute-start
  7.0 0.7 collective-permute-start.1
  7.7 0.3 collective-permute-start.2
  8.0 3.8 %collective-permute-done.3 = f32[8,64,64]{2,1,0:T(8,128)S(1)} collective-permute-done((f32[8,64,64]{2,1,0:T(8,128)S(1)}, f32[8,64,64]{2,1,0:T(8,128)S(1)}, u32[]{:S(2)}, u32[]{:S(2)}) %collective-permute-start.3) | collective-permute-done | bytes 131104 | tf_op jit(solution)/shard_map/ppermute | solution.py:306
  11.8 1.3 collective-permute-start.4
  13.1 9.3 %fusion.7.products = f32[512,512]{1,0:T(8,128)S(1)} fusion(f32[512,2048]{1,0:T(8,128)} %bitcast.32), kind=kOutput, calls=%fused_computation.13 | convolution fusion | flops 6442450944 | bytes 5242880 | tf_op jit(solution)/shard_map/dot_general | solution.py:20
  22.4 1.7 %collective-permute-done.4 = f32[8,64,64]{2,1,0:T(8,128)} collective-permute-done((f32[8,64,64]{2,1,0:T(8,128)S(1)}, f32[8,64,64]{2,1,0:T(8,128)}, u32[]{:S(2)}, u32[]{:S(2)}) %collective-permute-start.4) | collective-permute-done | bytes 131104 | tf_op jit(solution)/shard_map/ppermute | solution.py:306
  24.1 1.1 add.22
  25.2 1.5 %collective-permute-start.6 = (f32[8,64,256]{2,1,0:T(8,128)S(1)}, f32[8,64,256]{2,1,0:T(8,128)}, u32[]{:S(2)}, u32[]{:S(2)}) collective-permute-start(f32[8,64,256]{2,1,0:T(8,128)S(1)} %collective-permute-done.refs_10_), channel_id=1, source_target_pairs={{8,16},{12,20},{16,8},{20,12},{9,17},{13,21},{17,9},{21,13},{10,18... | collective-permute-start | bytes 1572872 | tf_op jit(solution)/shard_map/ppermute | solution.py:306
  26.7 0.4 collective-permute-start.7
  27.1 1.3 collective-permute-start.5
  28.4 0.9 broadcast_select_fusion.1
  29.3 3.1 %collective-permute-start.8 = (f32[8,64,256]{2,1,0:T(8,128)}, f32[8,64,256]{2,1,0:T(8,128)}, u32[]{:S(2)}, u32[]{:S(2)}) collective-permute-start(f32[8,64,256]{2,1,0:T(8,128)} %broadcast_select_fusion.1), channel_id=1, source_target_pairs={{0,24},{4,28},{8,12},{12,8},{16,20},{20,16},{24,0},{28,4},{1,25},{... | collective-permute-start | bytes 1572872 | tf_op jit(solution)/shard_map/ppermute | solution.py:333
  32.5 0.1 pad.6.clone
  32.5 0.3 fusion
  32.8 1.6 %maximum_maximum_fusion = f32[64,640]{1,0:T(8,128)} fusion(f32[64,64]{1,0:T(8,128)S(1)} %fusion, f32[64,512]{1,0:T(8,128)} %bitcast.36, f32[640]{0:T(1024)S(1)} %pad.6.clone), kind=kLoop, calls=%fused_computation.4 | loop fusion | flops 81920 | bytes 313856 | tf_op jit(solution)/shard_map/concatenate | solution.py:370
  34.4 19.1 %collective-permute-done.5 = f32[8,64,256]{2,1,0:T(8,128)} collective-permute-done((f32[8,64,256]{2,1,0:T(8,128)S(1)}, f32[8,64,256]{2,1,0:T(8,128)}, u32[]{:S(2)}, u32[]{:S(2)}) %collective-permute-start.5) | collective-permute-done | bytes 524320 | tf_op jit(solution)/shard_map/ppermute | solution.py:327
  53.5 1.1 broadcast_select_fusion.refs_12_
  54.6 1.4 %collective-permute-start.11 = (f32[8,64,256]{2,1,0:T(8,128)S(1)}, f32[8,64,256]{2,1,0:T(8,128)}, u32[]{:S(2)}, u32[]{:S(2)}) collective-permute-start(f32[8,64,256]{2,1,0:T(8,128)S(1)} %broadcast_select_fusion.refs_12_), channel_id=1, source_target_pairs={{0,4},{4,0},{8,12},{12,8},{16,20},{20,16},{24,28},{28,24},{1,5},{5... | collective-permute-start | bytes 1572872 | tf_op jit(solution)/shard_map/ppermute | solution.py:306
  56.0 1.5 %collective-permute-start.12 = (f32[8,64,256]{2,1,0:T(8,128)}, f32[8,64,256]{2,1,0:T(8,128)}, u32[]{:S(2)}, u32[]{:S(2)}) collective-permute-start(f32[8,64,256]{2,1,0:T(8,128)} %collective-permute-done.6), channel_id=1, source_target_pairs={{8,0},{12,4},{16,24},{20,28},{9,1},{13,5},{17,25},{21,29},{10,2},{... | collective-permute-start | bytes 1572872 | tf_op jit(solution)/shard_map/ppermute | solution.py:339
  57.5 1.3 collective-permute-start.10
  58.8 2.8 %collective-permute-start.9 = (f32[8,64,64]{2,1,0:T(8,128)S(1)}, f32[8,64,64]{2,1,0:T(8,128)}, u32[]{:S(2)}, u32[]{:S(2)}) collective-permute-start(f32[8,64,64]{2,1,0:T(8,128)S(1)} %add.22), channel_id=1, source_target_pairs={{0,16},{4,20},{8,24},{12,28},{16,0},{20,4},{24,8},{28,12},{1,17},{... | collective-permute-start | bytes 393224 | tf_op jit(solution)/shard_map/ppermute | solution.py:306
  61.6 0.1 stack.65.refs_0_
  61.7 2.2 %copy-done.1 = f32[1,8,64,2048]{3,2,1,0:T(8,128)S(1)} copy-done((f32[1,8,64,2048]{3,2,1,0:T(8,128)S(1)}, f32[1,8,64,2048]{3,2,1,0:T(8,128)}, u32[]{:S(2)}) %copy-start.1) | copy-done | bytes 4194328
  63.9 1.0 copy-done.5
  64.9 1.0 copy-done.7
  66.0 4.4 %shard_map.95.refs_5_ = f32[8,64,64]{2,1,0:T(8,128)S(1)} custom-call(s32[7]{0:T(128)S(1)} %stack.65.refs_0_, f32[1,8,64,2048]{3,2,1,0:T(8,128)S(1)} %copy-done.1, f32[1,8,64,2048]{3,2,1,0:T(8,128)S(1)} %copy-done.1, f32[1,8,64,2048]{3,2,1,0:T(8,128)S(1)} %copy-done.1, f32[1,8,64,2048]{3,2,1,0:T(8,128)S(1)} %copy-done.1, f32[1,8,64,2048]{3,2,1,0:T(8,128)S(1)} %copy-done.1, ...), custom_call_target="tpu_custom_call" | custom-call | flops 100000000 | bytes 1000000 | tf_op jit(solution)/shard_map/pallas_call | solution.py:141
  70.4 1.9 %collective-permute-done.9 = f32[8,64,64]{2,1,0:T(8,128)} collective-permute-done((f32[8,64,64]{2,1,0:T(8,128)S(1)}, f32[8,64,64]{2,1,0:T(8,128)}, u32[]{:S(2)}, u32[]{:S(2)}) %collective-permute-start.9) | collective-permute-done | bytes 131104 | tf_op jit(solution)/shard_map/ppermute | solution.py:306
  72.2 1.0 add.24.sketched
  73.2 1.0 pad_maximum_fusion.tiles
  74.3 1.4 collective-permute-done.12.refs_4_
  75.7 0.1 collective-permute-start.16
  75.7 0.1 pad_add_fusion.refs_0_
  75.8 3.1 %shard_map.97.inner = f32[8,64,64]{2,1,0:T(8,128)S(1)} custom-call(s32[2]{0:T(128)S(1)} %pad_add_fusion.refs_0_, f32[1,8,64,2048]{3,2,1,0:T(8,128)S(1)} %copy-done.2, f32[1,8,64,2048]{3,2,1,0:T(8,128)S(1)} %copy-done.2, f32[8,64,256]{2,1,0:T(8,128)} %collective-permute-done.11.refs_3_, f32[8,64,256]{2,1,0:T(8,128)} %collective-permute-done.12.refs_4_, ...), custom_call_target="tpu_custom_call" | custom-call | flops 100000000 | bytes 1000000 | tf_op jit(solution)/shard_map/pallas_call | solution.py:141
  78.9 11.2 %shard_map.98 = (f32[64,512]{1,0:T(8,128)S(1)}, f32[64,576]{1,0:T(8,128)S(1)}) custom-call(s32[1,8]{1,0:T(1,128)S(1)} %copy-done.13, f32[8,64,64]{2,1,0:T(8,128)S(1)} %add.24.sketched, f32[8,64,64]{2,1,0:T(8,128)S(1)} %shard_map.97.inner, f32[512,512]{1,0:T(8,128)S(1)} %fusion.7.products), custom_call_target="tpu_custom_call" | custom-call | flops 100000000 | bytes 1000000 | tf_op jit(solution)/shard_map/pallas_call | solution.py:293
  90.1 0.1 collective-permute-start.13
  90.2 1.7 %collective-permute-start.14 = (f32[64,512]{1,0:T(8,128)S(1)}, f32[64,512]{1,0:T(8,128)S(1)}, u32[]{:S(2)}, u32[]{:S(2)}) collective-permute-start(f32[64,512]{1,0:T(8,128)S(1)} %get-tuple-element.75.refs_0_), channel_id=1, source_target_pairs={{0,8},{4,12},{8,0},{12,4},{16,24},{20,28},{24,16},{28,20},{1,9},{5... | collective-permute-start | bytes 393224 | tf_op jit(solution)/shard_map/ppermute | solution.py:306
  91.9 1.0 collective-permute-start.15
  92.8 5.6 %shard_map.99 = (f32[64,2048]{1,0:T(8,128)S(1)}, f32[64,2048]{1,0:T(8,128)S(1)}, f32[64,128]{1,0:T(8,128)S(1)}) custom-call(f32[64,576]{1,0:T(8,128)S(1)} %get-tuple-element.67.whole, f32[512,2048]{1,0:T(8,128)S(1)} %bitcast.33), custom_call_target="tpu_custom_call" | custom-call | flops 100000000 | bytes 1000000 | tf_op jit(solution)/shard_map/pallas_call | solution.py:399
  98.4 5.1 %collective-permute-done.14.refs_2_ = f32[64,512]{1,0:T(8,128)S(1)} collective-permute-done((f32[64,512]{1,0:T(8,128)S(1)}, f32[64,512]{1,0:T(8,128)S(1)}, u32[]{:S(2)}, u32[]{:S(2)}) %collective-permute-start.14) | collective-permute-done | bytes 131104 | tf_op jit(solution)/shard_map/ppermute | solution.py:306
  103.5 2.6 %collective-permute-done.15.refs_3_ = f32[64,512]{1,0:T(8,128)S(1)} collective-permute-done((f32[64,512]{1,0:T(8,128)S(1)}, f32[64,512]{1,0:T(8,128)S(1)}, u32[]{:S(2)}, u32[]{:S(2)}) %collective-permute-start.15) | collective-permute-done | bytes 131104 | tf_op jit(solution)/shard_map/ppermute | solution.py:306
  106.1 0.5 collective-permute-start.17
  106.6 2.3 %collective-permute-start.19 = (f32[64,2048]{1,0:T(8,128)S(1)}, f32[64,2048]{1,0:T(8,128)S(1)}, u32[]{:S(2)}, u32[]{:S(2)}) collective-permute-start(f32[64,2048]{1,0:T(8,128)S(1)} %get-tuple-element.69.own), channel_id=1, source_target_pairs={{0,2},{1,3},{2,0},{3,1},{4,6},{5,7},{6,4},{7,5},{8,10},{9,11},{10,... | collective-permute-start | bytes 1572872 | tf_op jit(solution)/shard_map/ppermute | solution.py:306
  108.9 0.3 collective-permute-start.18
  109.2 1.7 %shard_map.101 = (f32[64,512]{1,0:T(8,128)S(1)}, f32[64,512]{1,0:T(8,128)}, f32[64,512]{1,0:T(8,128)}, f32[64,512]{1,0:T(8,128)}) custom-call(f32[64,512]{1,0:T(8,128)S(1)} %get-tuple-element.75.refs_0_, f32[64,512]{1,0:T(8,128)S(1)} %collective-permute-done.13.refs_1_, f32[64,512]{1,0:T(8,128)S(1)} %collective-permute-done.14.refs_2_, ...), custom_call_target="tpu_custom_call" | custom-call | flops 100000000 | bytes 1000000 | tf_op jit(solution)/shard_map/pallas_call | solution.py:293
  111.0 1.2 collective-permute-start.20
  112.2 0.7 copy-done.9
  112.9 1.4 %collective-permute-start.22 = (f32[64,512]{1,0:T(8,128)}, f32[64,512]{1,0:T(8,128)}, u32[]{:S(2)}, u32[]{:S(2)}) collective-permute-start(f32[64,512]{1,0:T(8,128)} %get-tuple-element.84), channel_id=1, source_target_pairs={{0,12},{4,8},{8,4},{12,0},{16,28},{20,24},{24,20},{28,16},{1,13},{... | collective-permute-start | bytes 393224 | tf_op jit(solution)/shard_map/ppermute | solution.py:306
  114.3 0.1 stack.76.spots
  114.4 1.0 copy-done.10
  115.4 0.8 copy-done.12
  116.2 2.1 %shard_map.100 = (f32[64,64]{1,0:T(8,128)S(1)}, f32[64,2048]{1,0:T(8,128)S(1)}, f32[64,2048]{1,0:T(8,128)S(1)}, f32[64,64]{1,0:T(8,128)S(1)}, f32[128,128]{1,0:T(8,128)S(1)}) custom-call(s32[1]{0:T(128)} %bitcast.place.chunk, f32[64,2048]{1,0:T(8,128)S(1)} %get-tuple-element.69.own, f32[64,2048]{1,0:T(8,128)S(1)} %collective-permute-done.17.partner, ...), custom_call_target="tpu_custom_call" | custom-call | flops 100000000 | bytes 1000000 | tf_op jit(solution)/shard_map/pallas_call | solution.py:293
  118.2 1.6 %collective-permute-done.22.near_side = f32[64,512]{1,0:T(8,128)} collective-permute-done((f32[64,512]{1,0:T(8,128)}, f32[64,512]{1,0:T(8,128)}, u32[]{:S(2)}, u32[]{:S(2)}) %collective-permute-start.22) | collective-permute-done | bytes 131104 | tf_op jit(solution)/shard_map/ppermute | solution.py:306
  119.8 1.5 %shard_map.102 = (f32[64,512]{1,0:T(8,128)S(1)}, f32[64,512]{1,0:T(8,128)S(1)}, f32[64,512]{1,0:T(8,128)S(1)}, f32[64,512]{1,0:T(8,128)S(1)}) custom-call(s32[5]{0:T(128)S(1)} %stack.76.spots, f32[64,64]{1,0:T(8,128)S(1)} %get-tuple-element.74.step, f32[64,512]{1,0:T(8,128)S(1)} %get-tuple-element.81.own, f32[64,512]{1,0:T(8,128)S(1)} %collective-permute-done.20.side, ...), custom_call_target="tpu_custom_call" | custom-call | flops 100000000 | bytes 1000000 | tf_op jit(solution)/shard_map/pallas_call | solution.py:293
  121.4 1.4 %collective-permute-start.23 = (f32[64,2048]{1,0:T(8,128)S(1)}, f32[64,2048]{1,0:T(8,128)S(1)}, u32[]{:S(2)}, u32[]{:S(2)}) collective-permute-start(f32[64,2048]{1,0:T(8,128)S(1)} %collective-permute-done.19.far), channel_id=1, source_target_pairs={{0,1},{1,0},{2,3},{3,2},{4,5},{5,4},{6,7},{7,6},{8,9},{9,8},{10,11... | collective-permute-start | bytes 1572872 | tf_op jit(solution)/shard_map/ppermute | solution.py:306
  122.8 0.1 collective-permute-start.24
  122.9 0.4 collective-permute-start.25
  123.3 1.7 %collective-permute-start.26 = (f32[64,512]{1,0:T(8,128)S(1)}, f32[64,512]{1,0:T(8,128)S(1)}, u32[]{:S(2)}, u32[]{:S(2)}) collective-permute-start(f32[64,512]{1,0:T(8,128)S(1)} %get-tuple-element.95), channel_id=1, source_target_pairs={{0,3},{1,2},{2,1},{3,0},{4,7},{5,6},{6,5},{7,4},{8,11},{9,10},{10,... | collective-permute-start | bytes 393224 | tf_op jit(solution)/shard_map/ppermute | solution.py:306
  124.9 10.3 %shard_map.103 = (f32[64,512]{1,0:T(8,128)}, f32[64,192]{1,0:T(8,128)S(1)}) custom-call(s32[1]{0:T(128)} %bitcast.place.chunk, f32[64,2048]{1,0:T(8,128)S(1)} %get-tuple-element.73.near, f32[64,2048]{1,0:T(8,128)S(1)} %collective-permute-done.19.far, f32[64,2048]{1,0:T(8,128)S(1)} %collective-permute-done.23.far_core, ...), custom_call_target="tpu_custom_call" | custom-call | flops 100000000 | bytes 1000000 | tf_op jit(solution)/shard_map/pallas_call | solution.py:293
  135.2 1.0 shard_map.104
  (45 shorter events, 0.2 us)
Async XLA Ops:
  0.6 1.0 copy-start
  3.6 8.2 %collective-permute-start.3 = (f32[8,64,64]{2,1,0:T(8,128)S(1)}, f32[8,64,64]{2,1,0:T(8,128)S(1)}, u32[]{:S(2)}, u32[]{:S(2)}) collective-permute-start(f32[8,64,64]{2,1,0:T(8,128)S(1)} %convolution_bitcast_fusion), channel_id=1, source_target_pairs={{0,4},{4,0},{8,12},{12,8},{16,20},{20,16},{24,28},{28,24},{1,5},{5... | collective-permute-start | bytes 393224 | tf_op jit(solution)/shard_map/ppermute | solution.py:306
  5.7 19.5 %collective-permute-start = (f32[8,64,256]{2,1,0:T(8,128)}, f32[8,64,256]{2,1,0:T(8,128)S(1)}, u32[]{:S(2)}, u32[]{:S(2)}) collective-permute-start(f32[8,64,256]{2,1,0:T(8,128)} %refs_8_.1), channel_id=1, source_target_pairs={{0,8},{4,12},{8,0},{12,4},{16,24},{20,28},{24,16},{28,20},{1,9},{5... | collective-permute-start | bytes 1572872 | tf_op jit(solution)/shard_map/ppermute | solution.py:306
  7.0 18.2 %collective-permute-start.1 = (f32[8,64,256]{2,1,0:T(8,128)}, f32[8,64,256]{2,1,0:T(8,128)S(1)}, u32[]{:S(2)}, u32[]{:S(2)}) collective-permute-start(f32[8,64,256]{2,1,0:T(8,128)} %refs_8_.1), channel_id=1, source_target_pairs={{8,16},{12,20},{16,8},{20,12},{9,17},{13,21},{17,9},{21,13},{10,18... | collective-permute-start | bytes 1572872 | tf_op jit(solution)/shard_map/ppermute | solution.py:306
  7.7 17.5 %collective-permute-start.2 = (f32[8,64,256]{2,1,0:T(8,128)}, f32[8,64,256]{2,1,0:T(8,128)S(1)}, u32[]{:S(2)}, u32[]{:S(2)}) collective-permute-start(f32[8,64,256]{2,1,0:T(8,128)} %refs_8_.1), channel_id=1, source_target_pairs={{0,4},{4,0},{8,12},{12,8},{16,20},{20,16},{24,28},{28,24},{1,5},{5... | collective-permute-start | bytes 1572872 | tf_op jit(solution)/shard_map/ppermute | solution.py:306
  11.8 10.6 %copy-start.14 = (f32[8,64,64]{2,1,0:T(8,128)}, f32[8,64,64]{2,1,0:T(8,128)S(1)}, u32[]{:S(2)}) copy-start(f32[8,64,64]{2,1,0:T(8,128)S(1)} %add.21) | copy-start | bytes 393220
  11.8 12.3 %collective-permute-start.4 = (f32[8,64,64]{2,1,0:T(8,128)S(1)}, f32[8,64,64]{2,1,0:T(8,128)}, u32[]{:S(2)}, u32[]{:S(2)}) collective-permute-start(f32[8,64,64]{2,1,0:T(8,128)S(1)} %add.21), channel_id=1, source_target_pairs={{0,8},{4,12},{8,0},{12,4},{16,24},{20,28},{24,16},{28,20},{1,9},{5... | collective-permute-start | bytes 393224 | tf_op jit(solution)/shard_map/ppermute | solution.py:306
  13.1 19.5 %copy-start.8 = (f32[1,64,512]{2,1,0:T(8,128)S(1)}, f32[1,64,512]{2,1,0:T(8,128)}, u32[]{:S(2)}) copy-start(f32[1,64,512]{2,1,0:T(8,128)} %param.14) | copy-start | bytes 393220
  25.2 28.2 %copy-start.6 = (f32[8,64,256]{2,1,0:T(8,128)}, f32[8,64,256]{2,1,0:T(8,128)S(1)}, u32[]{:S(2)}) copy-start(f32[8,64,256]{2,1,0:T(8,128)S(1)} %collective-permute-done.refs_10_) | copy-start | bytes 1572868
  25.2 28.2 %collective-permute-start.6 = (f32[8,64,256]{2,1,0:T(8,128)S(1)}, f32[8,64,256]{2,1,0:T(8,128)}, u32[]{:S(2)}, u32[]{:S(2)}) collective-permute-start(f32[8,64,256]{2,1,0:T(8,128)S(1)} %collective-permute-done.refs_10_), channel_id=1, source_target_pairs={{8,16},{12,20},{16,8},{20,12},{9,17},{13,21},{17,9},{21,13},{10,18... | collective-permute-start | bytes 1572872 | tf_op jit(solution)/shard_map/ppermute | solution.py:306
  26.7 26.7 %collective-permute-start.7 = (f32[8,64,256]{2,1,0:T(8,128)S(1)}, f32[8,64,256]{2,1,0:T(8,128)}, u32[]{:S(2)}, u32[]{:S(2)}) collective-permute-start(f32[8,64,256]{2,1,0:T(8,128)S(1)} %collective-permute-done.refs_10_), channel_id=1, source_target_pairs={{0,4},{4,0},{8,12},{12,8},{16,20},{20,16},{24,28},{28,24},{1,5},{5... | collective-permute-start | bytes 1572872 | tf_op jit(solution)/shard_map/ppermute | solution.py:306
  27.1 26.3 %collective-permute-start.5 = (f32[8,64,256]{2,1,0:T(8,128)S(1)}, f32[8,64,256]{2,1,0:T(8,128)}, u32[]{:S(2)}, u32[]{:S(2)}) collective-permute-start(f32[8,64,256]{2,1,0:T(8,128)S(1)} %collective-permute-done.1.refs_14_), channel_id=1, source_target_pairs={{8,0},{12,4},{16,24},{20,28},{9,1},{13,5},{17,25},{21,29},{10,2},{... | collective-permute-start | bytes 1572872 | tf_op jit(solution)/shard_map/ppermute | solution.py:327
  29.3 24.2 %collective-permute-start.8 = (f32[8,64,256]{2,1,0:T(8,128)}, f32[8,64,256]{2,1,0:T(8,128)}, u32[]{:S(2)}, u32[]{:S(2)}) collective-permute-start(f32[8,64,256]{2,1,0:T(8,128)} %broadcast_select_fusion.1), channel_id=1, source_target_pairs={{0,24},{4,28},{8,12},{12,8},{16,20},{20,16},{24,0},{28,4},{1,25},{... | collective-permute-start | bytes 1572872 | tf_op jit(solution)/shard_map/ppermute | solution.py:333
  54.6 19.7 %collective-permute-start.11 = (f32[8,64,256]{2,1,0:T(8,128)S(1)}, f32[8,64,256]{2,1,0:T(8,128)}, u32[]{:S(2)}, u32[]{:S(2)}) collective-permute-start(f32[8,64,256]{2,1,0:T(8,128)S(1)} %broadcast_select_fusion.refs_12_), channel_id=1, source_target_pairs={{0,4},{4,0},{8,12},{12,8},{16,20},{20,16},{24,28},{28,24},{1,5},{5... | collective-permute-start | bytes 1572872 | tf_op jit(solution)/shard_map/ppermute | solution.py:306
  56.0 19.6 %collective-permute-start.12 = (f32[8,64,256]{2,1,0:T(8,128)}, f32[8,64,256]{2,1,0:T(8,128)}, u32[]{:S(2)}, u32[]{:S(2)}) collective-permute-start(f32[8,64,256]{2,1,0:T(8,128)} %collective-permute-done.6), channel_id=1, source_target_pairs={{8,0},{12,4},{16,24},{20,28},{9,1},{13,5},{17,25},{21,29},{10,2},{... | collective-permute-start | bytes 1572872 | tf_op jit(solution)/shard_map/ppermute | solution.py:339
  57.5 15.7 %collective-permute-start.10 = (f32[64,640]{1,0:T(8,128)}, f32[64,640]{1,0:T(8,128)}, u32[]{:S(2)}, u32[]{:S(2)}) collective-permute-start(f32[64,640]{1,0:T(8,128)} %maximum_maximum_fusion), channel_id=1, source_target_pairs={{0,2},{1,3},{2,0},{3,1},{4,6},{5,7},{6,4},{7,5},{8,10},{9,11},{10,... | collective-permute-start | bytes 491528 | tf_op jit(solution)/shard_map/ppermute | solution.py:306
  58.8 13.5 %collective-permute-start.9 = (f32[8,64,64]{2,1,0:T(8,128)S(1)}, f32[8,64,64]{2,1,0:T(8,128)}, u32[]{:S(2)}, u32[]{:S(2)}) collective-permute-start(f32[8,64,64]{2,1,0:T(8,128)S(1)} %add.22), channel_id=1, source_target_pairs={{0,16},{4,20},{8,24},{12,28},{16,0},{20,4},{24,8},{28,12},{1,17},{... | collective-permute-start | bytes 393224 | tf_op jit(solution)/shard_map/ppermute | solution.py:306
  61.7 2.2 %copy-start.1 = (f32[1,8,64,2048]{3,2,1,0:T(8,128)S(1)}, f32[1,8,64,2048]{3,2,1,0:T(8,128)}, u32[]{:S(2)}) copy-start(f32[1,8,64,2048]{3,2,1,0:T(8,128)} %refs_2_.3) | copy-start | bytes 12582916
  63.9 1.0 copy-start.5
  64.9 1.0 copy-start.7
  66.0 9.7 %copy-start.4 = (f32[8,64,256]{2,1,0:T(8,128)S(1)}, f32[8,64,256]{2,1,0:T(8,128)}, u32[]{:S(2)}) copy-start(f32[8,64,256]{2,1,0:T(8,128)} %param.10) | copy-start | bytes 1572868
  66.0 9.9 %copy-start.2 = (f32[1,8,64,2048]{3,2,1,0:T(8,128)S(1)}, f32[1,8,64,2048]{3,2,1,0:T(8,128)}, u32[]{:S(2)}) copy-start(f32[1,8,64,2048]{3,2,1,0:T(8,128)} %refs_2_.3) | copy-start | bytes 12582916
  75.7 30.4 %collective-permute-start.16 = (f32[512,256]{1,0:T(8,128)S(1)}, f32[512,256]{1,0:T(8,128)S(1)}, u32[]{:S(2)}, u32[]{:S(2)}) collective-permute-start(f32[512,256]{1,0:T(8,128)S(1)} %shard_map.96.refs_4_), channel_id=1, source_target_pairs={{0,16},{4,20},{8,24},{12,28},{16,0},{20,4},{24,8},{28,12},{1,17},{... | collective-permute-start | bytes 1572872 | tf_op jit(solution)/shard_map/ppermute | solution.py:306
  75.8 3.1 %copy-start.13 = (s32[1,8]{1,0:T(1,128)S(1)}, s32[1,8]{1,0:T(1,128)}, u32[]{:S(2)}) copy-start(s32[1,8]{1,0:T(1,128)} %weights.1) | copy-start | bytes 100
  75.8 17.0 %copy-start.3 = (f32[1,8,64,2048]{3,2,1,0:T(8,128)S(1)}, f32[1,8,64,2048]{3,2,1,0:T(8,128)}, u32[]{:S(2)}) copy-start(f32[1,8,64,2048]{3,2,1,0:T(8,128)} %param.8) | copy-start | bytes 12582916
  90.1 8.3 %collective-permute-start.13 = (f32[64,512]{1,0:T(8,128)S(1)}, f32[64,512]{1,0:T(8,128)S(1)}, u32[]{:S(2)}, u32[]{:S(2)}) collective-permute-start(f32[64,512]{1,0:T(8,128)S(1)} %get-tuple-element.75.refs_0_), channel_id=1, source_target_pairs={{0,4},{4,0},{8,12},{12,8},{16,20},{20,16},{24,28},{28,24},{1,5},{5... | collective-permute-start | bytes 393224 | tf_op jit(solution)/shard_map/ppermute | solution.py:306
  90.2 13.3 %collective-permute-start.14 = (f32[64,512]{1,0:T(8,128)S(1)}, f32[64,512]{1,0:T(8,128)S(1)}, u32[]{:S(2)}, u32[]{:S(2)}) collective-permute-start(f32[64,512]{1,0:T(8,128)S(1)} %get-tuple-element.75.refs_0_), channel_id=1, source_target_pairs={{0,8},{4,12},{8,0},{12,4},{16,24},{20,28},{24,16},{28,20},{1,9},{5... | collective-permute-start | bytes 393224 | tf_op jit(solution)/shard_map/ppermute | solution.py:306
  91.9 14.2 %collective-permute-start.15 = (f32[64,512]{1,0:T(8,128)S(1)}, f32[64,512]{1,0:T(8,128)S(1)}, u32[]{:S(2)}, u32[]{:S(2)}) collective-permute-start(f32[64,512]{1,0:T(8,128)S(1)} %get-tuple-element.75.refs_0_), channel_id=1, source_target_pairs={{0,12},{4,8},{8,4},{12,0},{16,28},{20,24},{24,20},{28,16},{1,13},{... | collective-permute-start | bytes 393224 | tf_op jit(solution)/shard_map/ppermute | solution.py:306
  98.4 13.8 %copy-start.11 = (f32[64,128]{1,0:T(8,128)}, f32[64,128]{1,0:T(8,128)S(1)}, u32[]{:S(2)}) copy-start(f32[64,128]{1,0:T(8,128)S(1)} %get-tuple-element.71.squares) | copy-start | bytes 98308
  106.1 8.3 %collective-permute-start.17 = (f32[64,2048]{1,0:T(8,128)S(1)}, f32[64,2048]{1,0:T(8,128)S(1)}, u32[]{:S(2)}, u32[]{:S(2)}) collective-permute-start(f32[64,2048]{1,0:T(8,128)S(1)} %get-tuple-element.69.own), channel_id=1, source_target_pairs={{0,1},{1,0},{2,3},{3,2},{4,5},{5,4},{6,7},{7,6},{8,9},{9,8},{10,11... | collective-permute-start | bytes 1572872 | tf_op jit(solution)/shard_map/ppermute | solution.py:306
  106.6 14.8 %collective-permute-start.19 = (f32[64,2048]{1,0:T(8,128)S(1)}, f32[64,2048]{1,0:T(8,128)S(1)}, u32[]{:S(2)}, u32[]{:S(2)}) collective-permute-start(f32[64,2048]{1,0:T(8,128)S(1)} %get-tuple-element.69.own), channel_id=1, source_target_pairs={{0,2},{1,3},{2,0},{3,1},{4,6},{5,7},{6,4},{7,5},{8,10},{9,11},{10,... | collective-permute-start | bytes 1572872 | tf_op jit(solution)/shard_map/ppermute | solution.py:306
  108.9 3.3 %collective-permute-start.18 = (f32[2,64,640]{2,1,0:T(8,128)S(1)}, f32[2,64,640]{2,1,0:T(8,128)S(1)}, u32[]{:S(2)}, u32[]{:S(2)}) collective-permute-start(f32[2,64,640]{2,1,0:T(8,128)S(1)} %pad_maximum_fusion.tiles), channel_id=1, source_target_pairs={{0,1},{1,0},{2,3},{3,2},{4,5},{5,4},{6,7},{7,6},{8,9},{9,8},{10,11... | collective-permute-start | bytes 983048 | tf_op jit(solution)/shard_map/ppermute | solution.py:306
  111.0 7.3 %collective-permute-start.20 = (f32[64,512]{1,0:T(8,128)}, f32[64,512]{1,0:T(8,128)S(1)}, u32[]{:S(2)}, u32[]{:S(2)}) collective-permute-start(f32[64,512]{1,0:T(8,128)} %get-tuple-element.82), channel_id=1, source_target_pairs={{0,4},{4,0},{8,12},{12,8},{16,20},{20,16},{24,28},{28,24},{1,5},{5... | collective-permute-start | bytes 393224 | tf_op jit(solution)/shard_map/ppermute | solution.py:306
  112.2 6.0 %collective-permute-start.21 = (f32[64,512]{1,0:T(8,128)}, f32[64,512]{1,0:T(8,128)S(1)}, u32[]{:S(2)}, u32[]{:S(2)}) collective-permute-start(f32[64,512]{1,0:T(8,128)} %get-tuple-element.83), channel_id=1, source_target_pairs={{0,8},{4,12},{8,0},{12,4},{16,24},{20,28},{24,16},{28,20},{1,9},{5... | collective-permute-start | bytes 393224 | tf_op jit(solution)/shard_map/ppermute | solution.py:306
  112.2 0.7 copy-start.9
  112.9 6.9 %collective-permute-start.22 = (f32[64,512]{1,0:T(8,128)}, f32[64,512]{1,0:T(8,128)}, u32[]{:S(2)}, u32[]{:S(2)}) collective-permute-start(f32[64,512]{1,0:T(8,128)} %get-tuple-element.84), channel_id=1, source_target_pairs={{0,12},{4,8},{8,4},{12,0},{16,28},{20,24},{24,20},{28,16},{1,13},{... | collective-permute-start | bytes 393224 | tf_op jit(solution)/shard_map/ppermute | solution.py:306
  114.4 1.0 copy-start.10
  115.4 0.8 copy-start.12
  121.4 3.6 %collective-permute-start.23 = (f32[64,2048]{1,0:T(8,128)S(1)}, f32[64,2048]{1,0:T(8,128)S(1)}, u32[]{:S(2)}, u32[]{:S(2)}) collective-permute-start(f32[64,2048]{1,0:T(8,128)S(1)} %collective-permute-done.19.far), channel_id=1, source_target_pairs={{0,1},{1,0},{2,3},{3,2},{4,5},{5,4},{6,7},{7,6},{8,9},{9,8},{10,11... | collective-permute-start | bytes 1572872 | tf_op jit(solution)/shard_map/ppermute | solution.py:306
  122.8 12.4 %collective-permute-start.24 = (f32[64,512]{1,0:T(8,128)S(1)}, f32[64,512]{1,0:T(8,128)S(1)}, u32[]{:S(2)}, u32[]{:S(2)}) collective-permute-start(f32[64,512]{1,0:T(8,128)S(1)} %get-tuple-element.93), channel_id=1, source_target_pairs={{0,1},{1,0},{2,3},{3,2},{4,5},{5,4},{6,7},{7,6},{8,9},{9,8},{10,11... | collective-permute-start | bytes 393224 | tf_op jit(solution)/shard_map/ppermute | solution.py:306
  122.9 12.3 %collective-permute-start.25 = (f32[64,512]{1,0:T(8,128)S(1)}, f32[64,512]{1,0:T(8,128)S(1)}, u32[]{:S(2)}, u32[]{:S(2)}) collective-permute-start(f32[64,512]{1,0:T(8,128)S(1)} %get-tuple-element.94), channel_id=1, source_target_pairs={{0,2},{1,3},{2,0},{3,1},{4,6},{5,7},{6,4},{7,5},{8,10},{9,11},{10,... | collective-permute-start | bytes 393224 | tf_op jit(solution)/shard_map/ppermute | solution.py:306
  123.3 12.0 %collective-permute-start.26 = (f32[64,512]{1,0:T(8,128)S(1)}, f32[64,512]{1,0:T(8,128)S(1)}, u32[]{:S(2)}, u32[]{:S(2)}) collective-permute-start(f32[64,512]{1,0:T(8,128)S(1)} %get-tuple-element.95), channel_id=1, source_target_pairs={{0,3},{1,2},{2,1},{3,0},{4,7},{5,6},{6,5},{7,4},{8,11},{9,10},{10,... | collective-permute-start | bytes 393224 | tf_op jit(solution)/shard_map/ppermute | solution.py:306

commit v4 on v3

--- a/solution.py
+++ b/solution.py
@@ -120,6 +120,20 @@
     return block(0, 0) + (block(0, 1) + block(1, 0) + small)
 
 
+def nn_parts(a, b):
+    m = a.shape[0]
+    one, two, three = split(a)
+    none = jnp.zeros_like(one)
+    left = [[one, one, one], [two, two, none], [three, none, none]]
+    stacked = lax.dot_general(
+        jnp.concatenate([jnp.concatenate(row, axis=1) for row in left], axis=0),
+        jnp.concatenate(split(b), axis=0),
+        (((1,), (0,)), ((), ())),
+        preferred_element_type=f32,
+    )
+    return stacked[:m] + (stacked[m : 2 * m] + stacked[2 * m :])
+
+
 def inner_kernel(count, *refs):
     panels, pieces, add, out = refs[1 : 1 + count], refs[1 + count : 1 + 2 * count], refs[1 + 2 * count : -1], refs[-1]
     for j in range(out.shape[0]):
@@ -209,7 +223,7 @@
     copy.wait()
     factor = nn(whole[:, :depth], held[...])
     top[...] = factor
-    sent[...] = nn(shrunk[0], factor)
+    sent[...] = nn_parts(shrunk[0], factor)
 
 
 def chip_kernel(place, own, partner, top, squares, tiles, tiles_core, step, near_out, tile_out, sketched, gram_out):
@@ -270,7 +284,7 @@
     odd = spots[4] == 1
     k = 0
     for first, second in ((own, side), (near, near_side)):
-        part = nn(step[...], jnp.concatenate([first[...], second[...]], axis=1))
+        part = nn_parts(step[...], jnp.concatenate([first[...], second[...]], axis=1))
         for i in range(2):
             a = part[:, i * half : (i + 1) * half]
             b = part[:, (2 + i) * half : (3 + i) * half]

time: 137 us -> 137 us (level)
  no operation moved by 1% of the time
where the time goes in v4:
time: 137 us; the launch traced here: 136 us
  Pallas kernels  40.5 us (30%)
  waiting for transfers between devices  37.3 us (27%)
  starting transfers between devices  31 us (23%)
  matrix products  11.5 us (8%)
  local copies, waits for them, and re-layouts  8.02 us (6%)
  other arithmetic  6.78 us (5%)
    pallas_call x7, Pallas kernels, call(): pl.pallas_call(kernel, in_specs=[SMEM] * scalars + [VMEM] * (len(operands...  27.7 us
    ppermute x24, starting transfers between devices, swap(): return lax.ppermute(value, axis, [(i, i ^ mask) for i in members])  25.1 us
    ppermute x1, waiting for transfers between devices, gather_line(): outer = lax.ppermute(center, 'rows', outward)  19.1 us
    ppermute x24, waiting for transfers between devices, swap(): return lax.ppermute(value, axis, [(i, i ^ mask) for i in members])  16.9 us
    dot_general x2, matrix products, dot(): lax.dot_general(a, b, (dims, ((), ())), precision=highest, preferred_elem...  9.6 us
    unnamed x30, local copies, waits for them, and re-layouts  7.77 us
    pallas_call x2, Pallas kernels, inner_products(): pl.pallas_call(functools.partial(inner_kernel, count), grid_spec=pltpu.Pr...  7.49 us
    pallas_call x1, Pallas kernels, local(): pl.pallas_call(top_kernel, in_specs=[VMEM, pl.BlockSpec(memory_space=pl.A...  5.34 us
  transfers between devices with their start and end apart: 27, of which 8 were waited for; matrix products, arithmetic and copies ran while one was open for 11% of the time, Pallas kernels for 29%

profile of v4, /device:TPU:1, one launch (start us, length us, event | category | flops | bytes accessed | tf_op | source)
XLA Modules:
  0.0 136.1 jit_solution(17232660544177888222)
XLA Ops:
  0.6 0.0 copy-start
  0.7 1.0 copy-done
  1.7 1.9 %convolution_bitcast_fusion = f32[8,64,64]{2,1,0:T(8,128)S(1)} fusion(f32[8,64,256]{2,1,0:T(8,128)} %param.10, f32[64,2048]{1,0:T(8,128)S(1)} %copy-done, s32[]{:T(128)S(6)} %select_n.29), kind=kOutput, calls=%fused_computation | convolution fusion | flops 100663296 | bytes 720900 | tf_op jit(solution)/shard_map/rb,jkb->jrk/dot_general | solution.py:378
  3.6 2.1 %collective-permute-start.3 = (f32[8,64,64]{2,1,0:T(8,128)S(1)}, f32[8,64,64]{2,1,0:T(8,128)S(1)}, u32[]{:S(2)}, u32[]{:S(2)}) collective-permute-start(f32[8,64,64]{2,1,0:T(8,128)S(1)} %convolution_bitcast_fusion), channel_id=1, source_target_pairs={{0,4},{4,0},{8,12},{12,8},{16,20},{20,16},{24,28},{28,24},{1,5},{5... | collective-permute-start | bytes 393224 | tf_op jit(solution)/shard_map/ppermute | solution.py:320
  5.7 1.3 collective-permute-start
  7.0 0.7 collective-permute-start.1
  7.7 0.3 collective-permute-start.2
  8.0 3.8 %collective-permute-done.3 = f32[8,64,64]{2,1,0:T(8,128)S(1)} collective-permute-done((f32[8,64,64]{2,1,0:T(8,128)S(1)}, f32[8,64,64]{2,1,0:T(8,128)S(1)}, u32[]{:S(2)}, u32[]{:S(2)}) %collective-permute-start.3) | collective-permute-done | bytes 131104 | tf_op jit(solution)/shard_map/ppermute | solution.py:320
  11.8 1.3 collective-permute-start.4
  13.1 9.3 %fusion.7.products = f32[512,512]{1,0:T(8,128)S(1)} fusion(f32[512,2048]{1,0:T(8,128)} %bitcast.32), kind=kOutput, calls=%fused_computation.13 | convolution fusion | flops 6442450944 | bytes 5242880 | tf_op jit(solution)/shard_map/dot_general | solution.py:20
  22.4 1.7 %collective-permute-done.4 = f32[8,64,64]{2,1,0:T(8,128)} collective-permute-done((f32[8,64,64]{2,1,0:T(8,128)S(1)}, f32[8,64,64]{2,1,0:T(8,128)}, u32[]{:S(2)}, u32[]{:S(2)}) %collective-permute-start.4) | collective-permute-done | bytes 131104 | tf_op jit(solution)/shard_map/ppermute | solution.py:320
  24.1 1.1 add.22
  25.2 1.5 %collective-permute-start.6 = (f32[8,64,256]{2,1,0:T(8,128)S(1)}, f32[8,64,256]{2,1,0:T(8,128)}, u32[]{:S(2)}, u32[]{:S(2)}) collective-permute-start(f32[8,64,256]{2,1,0:T(8,128)S(1)} %collective-permute-done.refs_10_), channel_id=1, source_target_pairs={{8,16},{12,20},{16,8},{20,12},{9,17},{13,21},{17,9},{21,13},{10,18... | collective-permute-start | bytes 1572872 | tf_op jit(solution)/shard_map/ppermute | solution.py:320
  26.7 0.4 collective-permute-start.7
  27.1 1.3 collective-permute-start.5
  28.4 0.9 broadcast_select_fusion.1
  29.3 3.1 %collective-permute-start.8 = (f32[8,64,256]{2,1,0:T(8,128)}, f32[8,64,256]{2,1,0:T(8,128)}, u32[]{:S(2)}, u32[]{:S(2)}) collective-permute-start(f32[8,64,256]{2,1,0:T(8,128)} %broadcast_select_fusion.1), channel_id=1, source_target_pairs={{0,24},{4,28},{8,12},{12,8},{16,20},{20,16},{24,0},{28,4},{1,25},{... | collective-permute-start | bytes 1572872 | tf_op jit(solution)/shard_map/ppermute | solution.py:347
  32.5 0.1 pad.6.clone
  32.5 0.3 fusion
  32.8 1.6 %maximum_maximum_fusion = f32[64,640]{1,0:T(8,128)} fusion(f32[64,64]{1,0:T(8,128)S(1)} %fusion, f32[64,512]{1,0:T(8,128)} %bitcast.36, f32[640]{0:T(1024)S(1)} %pad.6.clone), kind=kLoop, calls=%fused_computation.4 | loop fusion | flops 81920 | bytes 313856 | tf_op jit(solution)/shard_map/concatenate | solution.py:384
  34.4 19.1 %collective-permute-done.5 = f32[8,64,256]{2,1,0:T(8,128)} collective-permute-done((f32[8,64,256]{2,1,0:T(8,128)S(1)}, f32[8,64,256]{2,1,0:T(8,128)}, u32[]{:S(2)}, u32[]{:S(2)}) %collective-permute-start.5) | collective-permute-done | bytes 524320 | tf_op jit(solution)/shard_map/ppermute | solution.py:341
  53.5 1.1 broadcast_select_fusion.refs_12_
  54.6 1.4 %collective-permute-start.11 = (f32[8,64,256]{2,1,0:T(8,128)S(1)}, f32[8,64,256]{2,1,0:T(8,128)}, u32[]{:S(2)}, u32[]{:S(2)}) collective-permute-start(f32[8,64,256]{2,1,0:T(8,128)S(1)} %broadcast_select_fusion.refs_12_), channel_id=1, source_target_pairs={{0,4},{4,0},{8,12},{12,8},{16,20},{20,16},{24,28},{28,24},{1,5},{5... | collective-permute-start | bytes 1572872 | tf_op jit(solution)/shard_map/ppermute | solution.py:320
  56.0 1.5 %collective-permute-start.12 = (f32[8,64,256]{2,1,0:T(8,128)}, f32[8,64,256]{2,1,0:T(8,128)}, u32[]{:S(2)}, u32[]{:S(2)}) collective-permute-start(f32[8,64,256]{2,1,0:T(8,128)} %collective-permute-done.6), channel_id=1, source_target_pairs={{8,0},{12,4},{16,24},{20,28},{9,1},{13,5},{17,25},{21,29},{10,2},{... | collective-permute-start | bytes 1572872 | tf_op jit(solution)/shard_map/ppermute | solution.py:353
  57.5 1.3 collective-permute-start.10
  58.8 2.8 %collective-permute-start.9 = (f32[8,64,64]{2,1,0:T(8,128)S(1)}, f32[8,64,64]{2,1,0:T(8,128)}, u32[]{:S(2)}, u32[]{:S(2)}) collective-permute-start(f32[8,64,64]{2,1,0:T(8,128)S(1)} %add.22), channel_id=1, source_target_pairs={{0,16},{4,20},{8,24},{12,28},{16,0},{20,4},{24,8},{28,12},{1,17},{... | collective-permute-start | bytes 393224 | tf_op jit(solution)/shard_map/ppermute | solution.py:320
  61.6 0.1 stack.65.refs_0_
  61.7 2.2 %copy-done.1 = f32[1,8,64,2048]{3,2,1,0:T(8,128)S(1)} copy-done((f32[1,8,64,2048]{3,2,1,0:T(8,128)S(1)}, f32[1,8,64,2048]{3,2,1,0:T(8,128)}, u32[]{:S(2)}) %copy-start.1) | copy-done | bytes 4194328
  63.9 1.0 copy-done.5
  64.9 1.0 copy-done.7
  66.0 4.4 %shard_map.95.refs_5_ = f32[8,64,64]{2,1,0:T(8,128)S(1)} custom-call(s32[7]{0:T(128)S(1)} %stack.65.refs_0_, f32[1,8,64,2048]{3,2,1,0:T(8,128)S(1)} %copy-done.1, f32[1,8,64,2048]{3,2,1,0:T(8,128)S(1)} %copy-done.1, f32[1,8,64,2048]{3,2,1,0:T(8,128)S(1)} %copy-done.1, f32[1,8,64,2048]{3,2,1,0:T(8,128)S(1)} %copy-done.1, f32[1,8,64,2048]{3,2,1,0:T(8,128)S(1)} %copy-done.1, ...), custom_call_target="tpu_custom_call" | custom-call | flops 100000000 | bytes 1000000 | tf_op jit(solution)/shard_map/pallas_call | solution.py:155
  70.4 1.9 %collective-permute-done.9 = f32[8,64,64]{2,1,0:T(8,128)} collective-permute-done((f32[8,64,64]{2,1,0:T(8,128)S(1)}, f32[8,64,64]{2,1,0:T(8,128)}, u32[]{:S(2)}, u32[]{:S(2)}) %collective-permute-start.9) | collective-permute-done | bytes 131104 | tf_op jit(solution)/shard_map/ppermute | solution.py:320
  72.2 1.0 add.24.sketched
  73.2 1.0 pad_maximum_fusion.tiles
  74.3 1.4 collective-permute-done.12.refs_4_
  75.7 0.1 collective-permute-start.16
  75.7 0.1 pad_add_fusion.refs_0_
  75.8 3.1 %shard_map.97.inner = f32[8,64,64]{2,1,0:T(8,128)S(1)} custom-call(s32[2]{0:T(128)S(1)} %pad_add_fusion.refs_0_, f32[1,8,64,2048]{3,2,1,0:T(8,128)S(1)} %copy-done.2, f32[1,8,64,2048]{3,2,1,0:T(8,128)S(1)} %copy-done.2, f32[8,64,256]{2,1,0:T(8,128)} %collective-permute-done.11.refs_3_, f32[8,64,256]{2,1,0:T(8,128)} %collective-permute-done.12.refs_4_, ...), custom_call_target="tpu_custom_call" | custom-call | flops 100000000 | bytes 1000000 | tf_op jit(solution)/shard_map/pallas_call | solution.py:155
  78.9 11.2 %shard_map.98 = (f32[64,512]{1,0:T(8,128)S(1)}, f32[64,576]{1,0:T(8,128)S(1)}) custom-call(s32[1,8]{1,0:T(1,128)S(1)} %copy-done.13, f32[8,64,64]{2,1,0:T(8,128)S(1)} %add.24.sketched, f32[8,64,64]{2,1,0:T(8,128)S(1)} %shard_map.97.inner, f32[512,512]{1,0:T(8,128)S(1)} %fusion.7.products), custom_call_target="tpu_custom_call" | custom-call | flops 100000000 | bytes 1000000 | tf_op jit(solution)/shard_map/pallas_call | solution.py:307
  90.1 0.1 collective-permute-start.13
  90.2 1.7 %collective-permute-start.14 = (f32[64,512]{1,0:T(8,128)S(1)}, f32[64,512]{1,0:T(8,128)S(1)}, u32[]{:S(2)}, u32[]{:S(2)}) collective-permute-start(f32[64,512]{1,0:T(8,128)S(1)} %get-tuple-element.75.refs_0_), channel_id=1, source_target_pairs={{0,8},{4,12},{8,0},{12,4},{16,24},{20,28},{24,16},{28,20},{1,9},{5... | collective-permute-start | bytes 393224 | tf_op jit(solution)/shard_map/ppermute | solution.py:320
  91.9 1.0 collective-permute-start.15
  92.8 5.3 %shard_map.99 = (f32[64,2048]{1,0:T(8,128)S(1)}, f32[64,2048]{1,0:T(8,128)S(1)}, f32[64,128]{1,0:T(8,128)S(1)}) custom-call(f32[64,576]{1,0:T(8,128)S(1)} %get-tuple-element.67.whole, f32[512,2048]{1,0:T(8,128)S(1)} %bitcast.33), custom_call_target="tpu_custom_call" | custom-call | flops 100000000 | bytes 1000000 | tf_op jit(solution)/shard_map/pallas_call | solution.py:413
  98.2 5.3 %collective-permute-done.14.refs_2_ = f32[64,512]{1,0:T(8,128)S(1)} collective-permute-done((f32[64,512]{1,0:T(8,128)S(1)}, f32[64,512]{1,0:T(8,128)S(1)}, u32[]{:S(2)}, u32[]{:S(2)}) %collective-permute-start.14) | collective-permute-done | bytes 131104 | tf_op jit(solution)/shard_map/ppermute | solution.py:320
  103.5 2.6 %collective-permute-done.15.refs_3_ = f32[64,512]{1,0:T(8,128)S(1)} collective-permute-done((f32[64,512]{1,0:T(8,128)S(1)}, f32[64,512]{1,0:T(8,128)S(1)}, u32[]{:S(2)}, u32[]{:S(2)}) %collective-permute-start.15) | collective-permute-done | bytes 131104 | tf_op jit(solution)/shard_map/ppermute | solution.py:320
  106.1 0.5 collective-permute-start.17
  106.6 2.3 %collective-permute-start.19 = (f32[64,2048]{1,0:T(8,128)S(1)}, f32[64,2048]{1,0:T(8,128)S(1)}, u32[]{:S(2)}, u32[]{:S(2)}) collective-permute-start(f32[64,2048]{1,0:T(8,128)S(1)} %get-tuple-element.69.own), channel_id=1, source_target_pairs={{0,2},{1,3},{2,0},{3,1},{4,6},{5,7},{6,4},{7,5},{8,10},{9,11},{10,... | collective-permute-start | bytes 1572872 | tf_op jit(solution)/shard_map/ppermute | solution.py:320
  108.9 0.3 collective-permute-start.18
  109.2 1.7 %shard_map.101 = (f32[64,512]{1,0:T(8,128)S(1)}, f32[64,512]{1,0:T(8,128)}, f32[64,512]{1,0:T(8,128)}, f32[64,512]{1,0:T(8,128)}) custom-call(f32[64,512]{1,0:T(8,128)S(1)} %get-tuple-element.75.refs_0_, f32[64,512]{1,0:T(8,128)S(1)} %collective-permute-done.13.refs_1_, f32[64,512]{1,0:T(8,128)S(1)} %collective-permute-done.14.refs_2_, ...), custom_call_target="tpu_custom_call" | custom-call | flops 100000000 | bytes 1000000 | tf_op jit(solution)/shard_map/pallas_call | solution.py:307
  111.0 1.2 collective-permute-start.20
  112.2 0.7 copy-done.9
  112.9 1.4 %collective-permute-start.22 = (f32[64,512]{1,0:T(8,128)}, f32[64,512]{1,0:T(8,128)}, u32[]{:S(2)}, u32[]{:S(2)}) collective-permute-start(f32[64,512]{1,0:T(8,128)} %get-tuple-element.84), channel_id=1, source_target_pairs={{0,12},{4,8},{8,4},{12,0},{16,28},{20,24},{24,20},{28,16},{1,13},{... | collective-permute-start | bytes 393224 | tf_op jit(solution)/shard_map/ppermute | solution.py:320
  114.3 0.1 stack.76.spots
  114.4 1.0 copy-done.10
  115.4 0.8 copy-done.12
  116.2 2.1 %shard_map.100 = (f32[64,64]{1,0:T(8,128)S(1)}, f32[64,2048]{1,0:T(8,128)S(1)}, f32[64,2048]{1,0:T(8,128)S(1)}, f32[64,64]{1,0:T(8,128)S(1)}, f32[128,128]{1,0:T(8,128)S(1)}) custom-call(s32[1]{0:T(128)} %bitcast.place.chunk, f32[64,2048]{1,0:T(8,128)S(1)} %get-tuple-element.69.own, f32[64,2048]{1,0:T(8,128)S(1)} %collective-permute-done.17.partner, ...), custom_call_target="tpu_custom_call" | custom-call | flops 100000000 | bytes 1000000 | tf_op jit(solution)/shard_map/pallas_call | solution.py:307
  118.2 1.6 %collective-permute-done.22.near_side = f32[64,512]{1,0:T(8,128)} collective-permute-done((f32[64,512]{1,0:T(8,128)}, f32[64,512]{1,0:T(8,128)}, u32[]{:S(2)}, u32[]{:S(2)}) %collective-permute-start.22) | collective-permute-done | bytes 131104 | tf_op jit(solution)/shard_map/ppermute | solution.py:320
  119.8 1.4 shard_map.102
  121.2 1.4 %collective-permute-start.23 = (f32[64,2048]{1,0:T(8,128)S(1)}, f32[64,2048]{1,0:T(8,128)S(1)}, u32[]{:S(2)}, u32[]{:S(2)}) collective-permute-start(f32[64,2048]{1,0:T(8,128)S(1)} %collective-permute-done.19.far), channel_id=1, source_target_pairs={{0,1},{1,0},{2,3},{3,2},{4,5},{5,4},{6,7},{7,6},{8,9},{9,8},{10,11... | collective-permute-start | bytes 1572872 | tf_op jit(solution)/shard_map/ppermute | solution.py:320
  122.6 0.1 collective-permute-start.24
  122.7 0.6 collective-permute-start.25
  123.3 1.5 %collective-permute-start.26 = (f32[64,512]{1,0:T(8,128)S(1)}, f32[64,512]{1,0:T(8,128)S(1)}, u32[]{:S(2)}, u32[]{:S(2)}) collective-permute-start(f32[64,512]{1,0:T(8,128)S(1)} %get-tuple-element.95), channel_id=1, source_target_pairs={{0,3},{1,2},{2,1},{3,0},{4,7},{5,6},{6,5},{7,4},{8,11},{9,10},{10,... | collective-permute-start | bytes 393224 | tf_op jit(solution)/shard_map/ppermute | solution.py:320
  124.8 10.3 %shard_map.103 = (f32[64,512]{1,0:T(8,128)}, f32[64,192]{1,0:T(8,128)S(1)}) custom-call(s32[1]{0:T(128)} %bitcast.place.chunk, f32[64,2048]{1,0:T(8,128)S(1)} %get-tuple-element.73.near, f32[64,2048]{1,0:T(8,128)S(1)} %collective-permute-done.19.far, f32[64,2048]{1,0:T(8,128)S(1)} %collective-permute-done.23.far_core, ...), custom_call_target="tpu_custom_call" | custom-call | flops 100000000 | bytes 1000000 | tf_op jit(solution)/shard_map/pallas_call | solution.py:307
  135.1 1.0 shard_map.104
  (45 shorter events, 0.2 us)
Async XLA Ops:
  0.6 1.0 copy-start
  3.6 8.2 %collective-permute-start.3 = (f32[8,64,64]{2,1,0:T(8,128)S(1)}, f32[8,64,64]{2,1,0:T(8,128)S(1)}, u32[]{:S(2)}, u32[]{:S(2)}) collective-permute-start(f32[8,64,64]{2,1,0:T(8,128)S(1)} %convolution_bitcast_fusion), channel_id=1, source_target_pairs={{0,4},{4,0},{8,12},{12,8},{16,20},{20,16},{24,28},{28,24},{1,5},{5... | collective-permute-start | bytes 393224 | tf_op jit(solution)/shard_map/ppermute | solution.py:320
  5.7 19.5 %collective-permute-start = (f32[8,64,256]{2,1,0:T(8,128)}, f32[8,64,256]{2,1,0:T(8,128)S(1)}, u32[]{:S(2)}, u32[]{:S(2)}) collective-permute-start(f32[8,64,256]{2,1,0:T(8,128)} %refs_8_.1), channel_id=1, source_target_pairs={{0,8},{4,12},{8,0},{12,4},{16,24},{20,28},{24,16},{28,20},{1,9},{5... | collective-permute-start | bytes 1572872 | tf_op jit(solution)/shard_map/ppermute | solution.py:320
  7.0 18.2 %collective-permute-start.1 = (f32[8,64,256]{2,1,0:T(8,128)}, f32[8,64,256]{2,1,0:T(8,128)S(1)}, u32[]{:S(2)}, u32[]{:S(2)}) collective-permute-start(f32[8,64,256]{2,1,0:T(8,128)} %refs_8_.1), channel_id=1, source_target_pairs={{8,16},{12,20},{16,8},{20,12},{9,17},{13,21},{17,9},{21,13},{10,18... | collective-permute-start | bytes 1572872 | tf_op jit(solution)/shard_map/ppermute | solution.py:320
  7.7 17.5 %collective-permute-start.2 = (f32[8,64,256]{2,1,0:T(8,128)}, f32[8,64,256]{2,1,0:T(8,128)S(1)}, u32[]{:S(2)}, u32[]{:S(2)}) collective-permute-start(f32[8,64,256]{2,1,0:T(8,128)} %refs_8_.1), channel_id=1, source_target_pairs={{0,4},{4,0},{8,12},{12,8},{16,20},{20,16},{24,28},{28,24},{1,5},{5... | collective-permute-start | bytes 1572872 | tf_op jit(solution)/shard_map/ppermute | solution.py:320
  11.8 10.6 %copy-start.14 = (f32[8,64,64]{2,1,0:T(8,128)}, f32[8,64,64]{2,1,0:T(8,128)S(1)}, u32[]{:S(2)}) copy-start(f32[8,64,64]{2,1,0:T(8,128)S(1)} %add.21) | copy-start | bytes 393220
  11.8 12.3 %collective-permute-start.4 = (f32[8,64,64]{2,1,0:T(8,128)S(1)}, f32[8,64,64]{2,1,0:T(8,128)}, u32[]{:S(2)}, u32[]{:S(2)}) collective-permute-start(f32[8,64,64]{2,1,0:T(8,128)S(1)} %add.21), channel_id=1, source_target_pairs={{0,8},{4,12},{8,0},{12,4},{16,24},{20,28},{24,16},{28,20},{1,9},{5... | collective-permute-start | bytes 393224 | tf_op jit(solution)/shard_map/ppermute | solution.py:320
  13.1 19.5 %copy-start.8 = (f32[1,64,512]{2,1,0:T(8,128)S(1)}, f32[1,64,512]{2,1,0:T(8,128)}, u32[]{:S(2)}) copy-start(f32[1,64,512]{2,1,0:T(8,128)} %param.14) | copy-start | bytes 393220
  25.2 28.2 %copy-start.6 = (f32[8,64,256]{2,1,0:T(8,128)}, f32[8,64,256]{2,1,0:T(8,128)S(1)}, u32[]{:S(2)}) copy-start(f32[8,64,256]{2,1,0:T(8,128)S(1)} %collective-permute-done.refs_10_) | copy-start | bytes 1572868
  25.2 28.2 %collective-permute-start.6 = (f32[8,64,256]{2,1,0:T(8,128)S(1)}, f32[8,64,256]{2,1,0:T(8,128)}, u32[]{:S(2)}, u32[]{:S(2)}) collective-permute-start(f32[8,64,256]{2,1,0:T(8,128)S(1)} %collective-permute-done.refs_10_), channel_id=1, source_target_pairs={{8,16},{12,20},{16,8},{20,12},{9,17},{13,21},{17,9},{21,13},{10,18... | collective-permute-start | bytes 1572872 | tf_op jit(solution)/shard_map/ppermute | solution.py:320
  26.7 26.7 %collective-permute-start.7 = (f32[8,64,256]{2,1,0:T(8,128)S(1)}, f32[8,64,256]{2,1,0:T(8,128)}, u32[]{:S(2)}, u32[]{:S(2)}) collective-permute-start(f32[8,64,256]{2,1,0:T(8,128)S(1)} %collective-permute-done.refs_10_), channel_id=1, source_target_pairs={{0,4},{4,0},{8,12},{12,8},{16,20},{20,16},{24,28},{28,24},{1,5},{5... | collective-permute-start | bytes 1572872 | tf_op jit(solution)/shard_map/ppermute | solution.py:320
  27.1 26.3 %collective-permute-start.5 = (f32[8,64,256]{2,1,0:T(8,128)S(1)}, f32[8,64,256]{2,1,0:T(8,128)}, u32[]{:S(2)}, u32[]{:S(2)}) collective-permute-start(f32[8,64,256]{2,1,0:T(8,128)S(1)} %collective-permute-done.1.refs_14_), channel_id=1, source_target_pairs={{8,0},{12,4},{16,24},{20,28},{9,1},{13,5},{17,25},{21,29},{10,2},{... | collective-permute-start | bytes 1572872 | tf_op jit(solution)/shard_map/ppermute | solution.py:341
  29.3 24.2 %collective-permute-start.8 = (f32[8,64,256]{2,1,0:T(8,128)}, f32[8,64,256]{2,1,0:T(8,128)}, u32[]{:S(2)}, u32[]{:S(2)}) collective-permute-start(f32[8,64,256]{2,1,0:T(8,128)} %broadcast_select_fusion.1), channel_id=1, source_target_pairs={{0,24},{4,28},{8,12},{12,8},{16,20},{20,16},{24,0},{28,4},{1,25},{... | collective-permute-start | bytes 1572872 | tf_op jit(solution)/shard_map/ppermute | solution.py:347
  54.6 19.7 %collective-permute-start.11 = (f32[8,64,256]{2,1,0:T(8,128)S(1)}, f32[8,64,256]{2,1,0:T(8,128)}, u32[]{:S(2)}, u32[]{:S(2)}) collective-permute-start(f32[8,64,256]{2,1,0:T(8,128)S(1)} %broadcast_select_fusion.refs_12_), channel_id=1, source_target_pairs={{0,4},{4,0},{8,12},{12,8},{16,20},{20,16},{24,28},{28,24},{1,5},{5... | collective-permute-start | bytes 1572872 | tf_op jit(solution)/shard_map/ppermute | solution.py:320
  56.0 19.6 %collective-permute-start.12 = (f32[8,64,256]{2,1,0:T(8,128)}, f32[8,64,256]{2,1,0:T(8,128)}, u32[]{:S(2)}, u32[]{:S(2)}) collective-permute-start(f32[8,64,256]{2,1,0:T(8,128)} %collective-permute-done.6), channel_id=1, source_target_pairs={{8,0},{12,4},{16,24},{20,28},{9,1},{13,5},{17,25},{21,29},{10,2},{... | collective-permute-start | bytes 1572872 | tf_op jit(solution)/shard_map/ppermute | solution.py:353
  57.5 15.7 %collective-permute-start.10 = (f32[64,640]{1,0:T(8,128)}, f32[64,640]{1,0:T(8,128)}, u32[]{:S(2)}, u32[]{:S(2)}) collective-permute-start(f32[64,640]{1,0:T(8,128)} %maximum_maximum_fusion), channel_id=1, source_target_pairs={{0,2},{1,3},{2,0},{3,1},{4,6},{5,7},{6,4},{7,5},{8,10},{9,11},{10,... | collective-permute-start | bytes 491528 | tf_op jit(solution)/shard_map/ppermute | solution.py:320
  58.8 13.5 %collective-permute-start.9 = (f32[8,64,64]{2,1,0:T(8,128)S(1)}, f32[8,64,64]{2,1,0:T(8,128)}, u32[]{:S(2)}, u32[]{:S(2)}) collective-permute-start(f32[8,64,64]{2,1,0:T(8,128)S(1)} %add.22), channel_id=1, source_target_pairs={{0,16},{4,20},{8,24},{12,28},{16,0},{20,4},{24,8},{28,12},{1,17},{... | collective-permute-start | bytes 393224 | tf_op jit(solution)/shard_map/ppermute | solution.py:320
  61.7 2.2 %copy-start.1 = (f32[1,8,64,2048]{3,2,1,0:T(8,128)S(1)}, f32[1,8,64,2048]{3,2,1,0:T(8,128)}, u32[]{:S(2)}) copy-start(f32[1,8,64,2048]{3,2,1,0:T(8,128)} %refs_2_.3) | copy-start | bytes 12582916
  63.9 1.0 copy-start.5
  64.9 1.0 copy-start.7
  66.0 9.7 %copy-start.4 = (f32[8,64,256]{2,1,0:T(8,128)S(1)}, f32[8,64,256]{2,1,0:T(8,128)}, u32[]{:S(2)}) copy-start(f32[8,64,256]{2,1,0:T(8,128)} %param.10) | copy-start | bytes 1572868
  66.0 9.9 %copy-start.2 = (f32[1,8,64,2048]{3,2,1,0:T(8,128)S(1)}, f32[1,8,64,2048]{3,2,1,0:T(8,128)}, u32[]{:S(2)}) copy-start(f32[1,8,64,2048]{3,2,1,0:T(8,128)} %refs_2_.3) | copy-start | bytes 12582916
  75.7 30.4 %collective-permute-start.16 = (f32[512,256]{1,0:T(8,128)S(1)}, f32[512,256]{1,0:T(8,128)S(1)}, u32[]{:S(2)}, u32[]{:S(2)}) collective-permute-start(f32[512,256]{1,0:T(8,128)S(1)} %shard_map.96.refs_4_), channel_id=1, source_target_pairs={{0,16},{4,20},{8,24},{12,28},{16,0},{20,4},{24,8},{28,12},{1,17},{... | collective-permute-start | bytes 1572872 | tf_op jit(solution)/shard_map/ppermute | solution.py:320
  75.8 3.1 %copy-start.13 = (s32[1,8]{1,0:T(1,128)S(1)}, s32[1,8]{1,0:T(1,128)}, u32[]{:S(2)}) copy-start(s32[1,8]{1,0:T(1,128)} %weights.1) | copy-start | bytes 100
  75.8 17.0 %copy-start.3 = (f32[1,8,64,2048]{3,2,1,0:T(8,128)S(1)}, f32[1,8,64,2048]{3,2,1,0:T(8,128)}, u32[]{:S(2)}) copy-start(f32[1,8,64,2048]{3,2,1,0:T(8,128)} %param.8) | copy-start | bytes 12582916
  90.1 8.1 %collective-permute-start.13 = (f32[64,512]{1,0:T(8,128)S(1)}, f32[64,512]{1,0:T(8,128)S(1)}, u32[]{:S(2)}, u32[]{:S(2)}) collective-permute-start(f32[64,512]{1,0:T(8,128)S(1)} %get-tuple-element.75.refs_0_), channel_id=1, source_target_pairs={{0,4},{4,0},{8,12},{12,8},{16,20},{20,16},{24,28},{28,24},{1,5},{5... | collective-permute-start | bytes 393224 | tf_op jit(solution)/shard_map/ppermute | solution.py:320
  90.2 13.3 %collective-permute-start.14 = (f32[64,512]{1,0:T(8,128)S(1)}, f32[64,512]{1,0:T(8,128)S(1)}, u32[]{:S(2)}, u32[]{:S(2)}) collective-permute-start(f32[64,512]{1,0:T(8,128)S(1)} %get-tuple-element.75.refs_0_), channel_id=1, source_target_pairs={{0,8},{4,12},{8,0},{12,4},{16,24},{20,28},{24,16},{28,20},{1,9},{5... | collective-permute-start | bytes 393224 | tf_op jit(solution)/shard_map/ppermute | solution.py:320
  91.9 14.2 %collective-permute-start.15 = (f32[64,512]{1,0:T(8,128)S(1)}, f32[64,512]{1,0:T(8,128)S(1)}, u32[]{:S(2)}, u32[]{:S(2)}) collective-permute-start(f32[64,512]{1,0:T(8,128)S(1)} %get-tuple-element.75.refs_0_), channel_id=1, source_target_pairs={{0,12},{4,8},{8,4},{12,0},{16,28},{20,24},{24,20},{28,16},{1,13},{... | collective-permute-start | bytes 393224 | tf_op jit(solution)/shard_map/ppermute | solution.py:320
  98.2 14.0 %copy-start.11 = (f32[64,128]{1,0:T(8,128)}, f32[64,128]{1,0:T(8,128)S(1)}, u32[]{:S(2)}) copy-start(f32[64,128]{1,0:T(8,128)S(1)} %get-tuple-element.71.squares) | copy-start | bytes 98308
  106.1 8.3 %collective-permute-start.17 = (f32[64,2048]{1,0:T(8,128)S(1)}, f32[64,2048]{1,0:T(8,128)S(1)}, u32[]{:S(2)}, u32[]{:S(2)}) collective-permute-start(f32[64,2048]{1,0:T(8,128)S(1)} %get-tuple-element.69.own), channel_id=1, source_target_pairs={{0,1},{1,0},{2,3},{3,2},{4,5},{5,4},{6,7},{7,6},{8,9},{9,8},{10,11... | collective-permute-start | bytes 1572872 | tf_op jit(solution)/shard_map/ppermute | solution.py:320
  106.6 14.6 %collective-permute-start.19 = (f32[64,2048]{1,0:T(8,128)S(1)}, f32[64,2048]{1,0:T(8,128)S(1)}, u32[]{:S(2)}, u32[]{:S(2)}) collective-permute-start(f32[64,2048]{1,0:T(8,128)S(1)} %get-tuple-element.69.own), channel_id=1, source_target_pairs={{0,2},{1,3},{2,0},{3,1},{4,6},{5,7},{6,4},{7,5},{8,10},{9,11},{10,... | collective-permute-start | bytes 1572872 | tf_op jit(solution)/shard_map/ppermute | solution.py:320
  108.9 3.3 %collective-permute-start.18 = (f32[2,64,640]{2,1,0:T(8,128)S(1)}, f32[2,64,640]{2,1,0:T(8,128)S(1)}, u32[]{:S(2)}, u32[]{:S(2)}) collective-permute-start(f32[2,64,640]{2,1,0:T(8,128)S(1)} %pad_maximum_fusion.tiles), channel_id=1, source_target_pairs={{0,1},{1,0},{2,3},{3,2},{4,5},{5,4},{6,7},{7,6},{8,9},{9,8},{10,11... | collective-permute-start | bytes 983048 | tf_op jit(solution)/shard_map/ppermute | solution.py:320
  111.0 7.3 %collective-permute-start.20 = (f32[64,512]{1,0:T(8,128)}, f32[64,512]{1,0:T(8,128)S(1)}, u32[]{:S(2)}, u32[]{:S(2)}) collective-permute-start(f32[64,512]{1,0:T(8,128)} %get-tuple-element.82), channel_id=1, source_target_pairs={{0,4},{4,0},{8,12},{12,8},{16,20},{20,16},{24,28},{28,24},{1,5},{5... | collective-permute-start | bytes 393224 | tf_op jit(solution)/shard_map/ppermute | solution.py:320
  112.2 6.0 %collective-permute-start.21 = (f32[64,512]{1,0:T(8,128)}, f32[64,512]{1,0:T(8,128)S(1)}, u32[]{:S(2)}, u32[]{:S(2)}) collective-permute-start(f32[64,512]{1,0:T(8,128)} %get-tuple-element.83), channel_id=1, source_target_pairs={{0,8},{4,12},{8,0},{12,4},{16,24},{20,28},{24,16},{28,20},{1,9},{5... | collective-permute-start | bytes 393224 | tf_op jit(solution)/shard_map/ppermute | solution.py:320
  112.2 0.7 copy-start.9
  112.9 6.9 %collective-permute-start.22 = (f32[64,512]{1,0:T(8,128)}, f32[64,512]{1,0:T(8,128)}, u32[]{:S(2)}, u32[]{:S(2)}) collective-permute-start(f32[64,512]{1,0:T(8,128)} %get-tuple-element.84), channel_id=1, source_target_pairs={{0,12},{4,8},{8,4},{12,0},{16,28},{20,24},{24,20},{28,16},{1,13},{... | collective-permute-start | bytes 393224 | tf_op jit(solution)/shard_map/ppermute | solution.py:320
  114.4 1.0 copy-start.10
  115.4 0.8 copy-start.12
  121.2 3.6 %collective-permute-start.23 = (f32[64,2048]{1,0:T(8,128)S(1)}, f32[64,2048]{1,0:T(8,128)S(1)}, u32[]{:S(2)}, u32[]{:S(2)}) collective-permute-start(f32[64,2048]{1,0:T(8,128)S(1)} %collective-permute-done.19.far), channel_id=1, source_target_pairs={{0,1},{1,0},{2,3},{3,2},{4,5},{5,4},{6,7},{7,6},{8,9},{9,8},{10,11... | collective-permute-start | bytes 1572872 | tf_op jit(solution)/shard_map/ppermute | solution.py:320
  122.6 12.4 %collective-permute-start.24 = (f32[64,512]{1,0:T(8,128)S(1)}, f32[64,512]{1,0:T(8,128)S(1)}, u32[]{:S(2)}, u32[]{:S(2)}) collective-permute-start(f32[64,512]{1,0:T(8,128)S(1)} %get-tuple-element.93), channel_id=1, source_target_pairs={{0,1},{1,0},{2,3},{3,2},{4,5},{5,4},{6,7},{7,6},{8,9},{9,8},{10,11... | collective-permute-start | bytes 393224 | tf_op jit(solution)/shard_map/ppermute | solution.py:320
  122.7 12.3 %collective-permute-start.25 = (f32[64,512]{1,0:T(8,128)S(1)}, f32[64,512]{1,0:T(8,128)S(1)}, u32[]{:S(2)}, u32[]{:S(2)}) collective-permute-start(f32[64,512]{1,0:T(8,128)S(1)} %get-tuple-element.94), channel_id=1, source_target_pairs={{0,2},{1,3},{2,0},{3,1},{4,6},{5,7},{6,4},{7,5},{8,10},{9,11},{10,... | collective-permute-start | bytes 393224 | tf_op jit(solution)/shard_map/ppermute | solution.py:320
  123.3 11.8 %collective-permute-start.26 = (f32[64,512]{1,0:T(8,128)S(1)}, f32[64,512]{1,0:T(8,128)S(1)}, u32[]{:S(2)}, u32[]{:S(2)}) collective-permute-start(f32[64,512]{1,0:T(8,128)S(1)} %get-tuple-element.95), channel_id=1, source_target_pairs={{0,3},{1,2},{2,1},{3,0},{4,7},{5,6},{6,5},{7,4},{8,11},{9,10},{10,... | collective-permute-start | bytes 393224 | tf_op jit(solution)/shard_map/ppermute | solution.py:320
